TPU v7x, 512 devices: a whole 4x8x8 slice. The times are simulated.
512 devices in a mesh: lon: 16 (over y_lo, x), lat: 8 (over z), mem: 4 (over y_hi, core).
Axes of the slice: x: 4, y: 8 (y_hi: 2, y_lo: 4; y = y_hi * 4 + y_lo), z: 8, core: 2. Of those that a mesh axis runs over, the one named last changes fastest.
Arguments:
- anomalies: bfloat16 [80, 128, 2048], P('mem', 'lat', 'lon'), may hold values from -6 to 6
- vector: bfloat16 [128, 2048], P('lat', 'lon'), may hold values from -6 to 6
- cotangent: bfloat16 [128, 2048], P('lat', 'lon'), may hold values from -6 to 6
- taper: bfloat16 [289, 128, 2048], P(None, ('lat', 'mem'), 'lon'), may hold values from 0 to 1
Outputs:
- grad_taper: float32 [289, 128, 2048], P(None, ('lat', 'mem'), 'lon')
- grad_anomalies: float32 [80, 128, 2048], P('mem', 'lat', 'lon')
All inputs are finite; a program needn't handle non-finite values.
Results may differ from a plain program's by a relative error of at most 0.00035.
Values may be sent and summed in bfloat16 or wider, within the bound.
No kernel may reach another device: no remote copies, remote signals or barrier semaphores. Data moves between devices by JAX's collectives and lax.ppermute only.
A program may use at most 64 MiB of HBM per device.

v0:
```python
import jax
import jax.numpy as jnp
from jax import lax
from jax.sharding import PartitionSpec as P

SPAN = 17


def extended_2(cells, sides, width, closed):
    for axis, dim in sides:
        count = lax.axis_size(axis)
        ends = count if closed else count - 1
        head = lax.slice_in_dim(cells, 0, width, axis=dim)
        tail = lax.slice_in_dim(cells, cells.shape[dim] - width, cells.shape[dim], axis=dim)
        cells = jnp.concatenate(
            [
                lax.ppermute(tail, axis, [(i, (i + 1) % count) for i in range(ends)]),
                cells,
                lax.ppermute(head, axis, [((i + 1) % count, i) for i in range(ends)]),
            ],
            axis=dim,
        )
    return cells


def windows(band, width):
    return jnp.stack([band[..., shift : shift + width] for shift in range(SPAN)], 0)


def body(anomalies, vector, cotangent, taper):
    local_members, clat, clon = anomalies.shape
    rim = SPAN // 2
    members = local_members * lax.axis_size("mem")
    taper_full = lax.all_gather(taper, "mem", axis=1, tiled=True)
    stacked = jnp.concatenate([anomalies, vector[None]], 0)
    extended = extended_2(stacked, (("lon", 2), ("lat", 1)), rim, True)
    lat_pos = lax.axis_index("lat")
    row_ids = jnp.arange(clat + 2 * rim)
    keep = ((row_ids >= rim) | (lat_pos > 0)) & (
        (row_ids < clat + rim) | (lat_pos < lax.axis_size("lat") - 1)
    )
    extended = jnp.where(keep[None, :, None], extended, jnp.zeros_like(extended))
    ext_states = extended[:local_members]
    ext_field = extended[local_members]
    grad_in = cotangent.astype(jnp.float32)
    field = vector.astype(jnp.float32)
    center_wide = anomalies.astype(jnp.float32)
    taper_grid = taper_full.reshape(SPAN, SPAN, clat, clon)

    def step(first, row_off):
        band_x = lax.dynamic_slice_in_dim(ext_states, row_off, clat, 1)
        band_v = lax.dynamic_slice_in_dim(ext_field, row_off, clat, 0)
        win_x = windows(band_x, clon)
        win_v = windows(band_v, clon).astype(jnp.float32)
        weight = lax.dynamic_index_in_dim(taper_grid, row_off, 0, keepdims=False).astype(
            jnp.float32
        )
        scaled = grad_in[None] * weight
        first = first + jnp.einsum(
            "kab,kmab->mab", scaled * win_v, win_x, preferred_element_type=jnp.float32
        )
        spread = scaled[:, None] * center_wide[None]
        row_sum = jnp.pad(spread[0], ((0, 0), (0, 0), (0, SPAN - 1)))
        for shift in range(1, SPAN):
            row_sum = row_sum + jnp.pad(spread[shift], ((0, 0), (0, 0), (shift, SPAN - 1 - shift)))
        cov_part = jnp.einsum("mab,kmab->kab", anomalies, win_x, preferred_element_type=jnp.float32)
        return (first, (row_sum, grad_in[None] * cov_part * win_v))

    init = jnp.zeros((local_members, clat, clon), jnp.float32)
    first, (row_sums, parts) = lax.scan(step, init, jnp.arange(SPAN, dtype=jnp.int32))
    pushed = jnp.pad(row_sums[0], ((0, 0), (0, SPAN - 1), (0, 0)))
    for row_off in range(1, SPAN):
        pushed = pushed + jnp.pad(
            row_sums[row_off], ((0, 0), (row_off, SPAN - 1 - row_off), (0, 0))
        )
    partial_sum = parts.reshape(SPAN * SPAN, clat, clon)
    totals = lax.psum_scatter(partial_sum, "mem", scatter_dimension=1, tiled=True)
    grad_taper = totals / (members - 1)
    west_east = jnp.concatenate([pushed[..., :rim], pushed[..., -rim:]], 2)
    lon_recv = extended_2(west_east, (("lon", 2),), rim, True)
    core = pushed[..., rim:-rim]
    core = core.at[..., :rim].add(lon_recv[..., :rim])
    core = core.at[..., -rim:].add(lon_recv[..., -rim:])
    north_south = jnp.concatenate([core[:, :rim], core[:, -rim:]], 1)
    lat_recv = extended_2(north_south, (("lat", 1),), rim, False)
    inner = core[:, rim:-rim]
    inner = inner.at[:, :rim].add(lat_recv[:, :rim])
    inner = inner.at[:, -rim:].add(lat_recv[:, -rim:])
    grad_anomalies = (first + field[None] * inner) / (members - 1)
    return (grad_taper, grad_anomalies)


def solution(mesh):
    placed = (
        P("mem", "lat", "lon"),
        P("lat", "lon"),
        P("lat", "lon"),
        P(None, ("lat", "mem"), "lon"),
    )
    return jax.shard_map(
        body,
        mesh=mesh,
        in_specs=placed,
        out_specs=(P(None, ("lat", "mem"), "lon"), P("mem", "lat", "lon")),
        check_vma=False,
    )
```

profile of v0, /device:TPU:1, one launch (start us, length us, event | category | flops | bytes accessed | tf_op | source)
XLA Modules:
  0.0 382.6 jit_solution(5165551362732232261)
XLA Ops:
  7.2 1.7 copy.8
  9.0 1.1 slice_maximum_fusion
  10.1 3.9 %collective-permute-start = (bf16[21,16,8]{2,1,0:T(8,128)(2,1)S(1)}, bf16[21,16,8]{2,1,0:T(8,128)(2,1)S(1)}, u32[]{:S(2)}, u32[]{:S(2)}) collective-permute-start(bf16[21,16,8]{2,1,0:T(8,128)(2,1)S(1)} %get-tuple-element.303), channel_id=1, source_target_pairs={{0,32},{32,64},{64,96},{96,128},{128,160},{160,192},{192,224},{224... | collective-permute-start | bytes 16136 | tf_op jit(solution)/shard_map/ppermute | solution.py:17
  14.1 6.2 %collective-permute-start.1 = (bf16[21,16,8]{2,1,0:T(8,128)(2,1)S(1)}, bf16[21,16,8]{2,1,0:T(8,128)(2,1)S(1)}, u32[]{:S(2)}, u32[]{:S(2)}) collective-permute-start(bf16[21,16,8]{2,1,0:T(8,128)(2,1)S(1)} %get-tuple-element.304), channel_id=1, source_target_pairs={{32,0},{64,32},{96,64},{128,96},{160,128},{192,160},{224,192},{256... | collective-permute-start | bytes 16136 | tf_op jit(solution)/shard_map/ppermute | solution.py:19
  20.3 1.5 collective-permute-done.1
  21.8 1.0 pad_maximum_fusion
  22.9 4.0 %collective-permute-start.2 = (bf16[21,8,144]{2,1,0:T(8,128)(2,1)S(1)}, bf16[21,8,144]{2,1,0:T(8,128)(2,1)S(1)}, u32[]{:S(2)}, u32[]{:S(2)}) collective-permute-start(bf16[21,8,144]{2,1,0:T(8,128)(2,1)S(1)} %get-tuple-element.301), channel_id=1, source_target_pairs={{0,4},{4,8},{8,12},{12,16},{16,20},{20,24},{24,28},{28,0},{1,5},{5... | collective-permute-start | bytes 145160 | tf_op jit(solution)/shard_map/ppermute | solution.py:17
  26.9 8.6 %collective-permute-start.3 = (bf16[21,8,144]{2,1,0:T(8,128)(2,1)S(1)}, bf16[21,8,144]{2,1,0:T(8,128)(2,1)S(1)}, u32[]{:S(2)}, u32[]{:S(2)}) collective-permute-start(bf16[21,8,144]{2,1,0:T(8,128)(2,1)S(1)} %get-tuple-element.302), channel_id=1, source_target_pairs={{4,0},{8,4},{12,8},{16,12},{20,16},{24,20},{28,24},{0,28},{5,1},{9... | collective-permute-start | bytes 145160 | tf_op jit(solution)/shard_map/ppermute | solution.py:19
  35.6 1.4 collective-permute-done.3
  37.2 15.5 %all-gather.2.cloned.1.call-done = bf16[289,16,128]{2,0,1:T(8,128)(2,1)} async-done(((bf16[289,4,128]{2,0,1:T(8,128)(2,1)}), bf16[289,16,128]{2,0,1:T(8,128)(2,1)}) %all-gather.2.cloned.1.call-update) | async-done | bytes 1183760 | tf_op jit(solution)/shard_map/all_gather | solution.py:34
  52.7 1.4 copy.9
  54.1 203.0 %while.21 = (s32[]{:T(128)}, f32[20,16,128]{2,1,0:T(8,128)S(1)}, f32[17,20,16,144]{3,2,1,0:T(8,128)}, f32[17,17,16,128]{3,2,1,0:T(8,128)}, s32[17]{0:T(128)S(1)}...) while((s32[]{:T(128)}, f32[20,16,128]{2,1,0:T(8,128)S(1)}, ...), condition=%wide.region_1.2_spmd.clone, body=%wide.region_0.1_spmd.clone.sunk | while | flops 5902360 | bytes 19608376 | solution.py:70
  62.6 0.7 fusion.61
  63.9 2.2 bitcast_dynamic-update-slice_fusion.2
  75.8 2.2 bitcast_dynamic-update-slice_fusion.2
  87.7 2.2 bitcast_dynamic-update-slice_fusion.2
  99.7 2.2 bitcast_dynamic-update-slice_fusion.2
  110.4 0.7 fusion.61
  111.6 2.2 bitcast_dynamic-update-slice_fusion.2
  123.6 2.2 bitcast_dynamic-update-slice_fusion.2
  134.3 0.7 fusion.61
  135.5 2.2 bitcast_dynamic-update-slice_fusion.2
  147.4 2.2 bitcast_dynamic-update-slice_fusion.2
  159.4 2.2 bitcast_dynamic-update-slice_fusion.2
  171.3 2.2 bitcast_dynamic-update-slice_fusion.2
  182.0 0.7 fusion.61
  183.2 2.2 bitcast_dynamic-update-slice_fusion.2
  195.2 2.2 bitcast_dynamic-update-slice_fusion.2
  207.1 2.2 bitcast_dynamic-update-slice_fusion.2
  219.1 2.2 bitcast_dynamic-update-slice_fusion.2
  231.0 2.2 bitcast_dynamic-update-slice_fusion.2
  241.8 0.7 fusion.61
  243.0 2.2 bitcast_dynamic-update-slice_fusion.2
  254.9 2.2 bitcast_dynamic-update-slice_fusion.2
  257.2 3.2 slice_bitcast_fusion.33
  260.4 1.0 pad_add_fusion
  261.5 3.1 collective-permute-start.4
  264.8 6.1 %collective-permute-start.5 = (f32[20,32,8]{2,1,0:T(8,128)S(1)}, f32[20,32,8]{2,1,0:T(8,128)S(1)}, u32[]{:S(2)}, u32[]{:S(2)}) collective-permute-start(f32[20,32,8]{2,1,0:T(8,128)S(1)} %get-tuple-element.297), channel_id=1, source_target_pairs={{32,0},{64,32},{96,64},{128,96},{160,128},{192,160},{224,192},{256... | collective-permute-start | bytes 61448 | tf_op jit(solution)/shard_map/ppermute | solution.py:19
  270.9 8.5 %collective-permute-done.4 = f32[20,32,8]{2,1,0:T(8,128)S(1)} collective-permute-done((f32[20,32,8]{2,1,0:T(8,128)S(1)}, f32[20,32,8]{2,1,0:T(8,128)S(1)}, u32[]{:S(2)}, u32[]{:S(2)}) %collective-permute-start.4) | collective-permute-done | bytes 20512 | tf_op jit(solution)/shard_map/ppermute | solution.py:17
  279.6 3.6 scatter-add.14
  283.3 6.2 %scatter-add.15 = f32[20,32,128]{2,1,0:T(8,128)S(1)} dynamic-update-slice(f32[20,32,128]{2,1,0:T(8,128)S(1)} %scatter-add.14, f32[20,32,8]{2,1,0:T(8,128)S(1)} %slice_add_fusion, s32[]{:T(128)} %constant.157.clone.1, s32[]{:T(128)} %constant.157.clone.1, s32[]{:T(128)} %constant.166.clone.1) | dynamic-update-slice | bytes 40964 | tf_op jit(solution)/shard_map/scatter-add | solution.py:83
  289.6 3.5 collective-permute-start.6
  293.1 1.3 dynamic-slice.32
  295.0 1.3 collective-permute-start.7
  296.3 3.9 %collective-permute-done.7 = f32[20,8,128]{2,1,0:T(8,128)S(1)} collective-permute-done((f32[20,8,128]{2,1,0:T(8,128)S(1)}, f32[20,8,128]{2,1,0:T(8,128)S(1)}, u32[]{:S(2)}, u32[]{:S(2)}) %collective-permute-start.7) | collective-permute-done | bytes 81952 | tf_op jit(solution)/shard_map/ppermute | solution.py:19
  300.2 0.7 add_multiply_fusion
  300.9 72.6 %all-reduce.37.cloned.1.call-done = f32[289,16,128]{2,1,0:T(8,128)} async-done(((f32[289,16,128]{2,1,0:T(8,128)}), f32[289,16,128]{2,1,0:T(8,128)}) %all-reduce.37.cloned.1.call-update) | async-done | bytes 2367504
  373.5 2.2 dynamic-slice_multiply_fusion
  (760 shorter events, 106.5 us)
Async XLA Ops:
  7.2 28.3 %copy-start = (bf16[20,16,128]{2,1,0:T(8,128)(2,1)S(1)}, bf16[20,16,128]{2,1,0:T(8,128)(2,1)}, u32[]{:S(2)}) copy-start(bf16[20,16,128]{2,1,0:T(8,128)(2,1)} %param.14) | copy-start | bytes 245764
  7.2 29.8 %copy-start.1 = (bf16[16,128]{1,0:T(8,128)(2,1)S(1)}, bf16[16,128]{1,0:T(8,128)(2,1)}, u32[]{:S(2)}) copy-start(bf16[16,128]{1,0:T(8,128)(2,1)} %param.15) | copy-start | bytes 12292
  7.2 28.4 %copy-start.2 = (bf16[16,128]{1,0:T(8,128)(2,1)S(1)}, bf16[16,128]{1,0:T(8,128)(2,1)}, u32[]{:S(2)}) copy-start(bf16[16,128]{1,0:T(8,128)(2,1)} %param.16) | copy-start | bytes 12292
  7.2 45.5 %all-gather.2.cloned.1.call-start = ((), (), s32[]{:S(2)}) async-start(), calls=%async_computation | async-start | bytes 1515520 | tf_op jit(solution)/shard_map/all_gather | solution.py:34
  9.0 364.5 %all-reduce.37.cloned.1.call-start = ((), (), s32[]{:S(2)}) async-start(), calls=%async_computation.1 | async-start | bytes 4734976
  10.1 10.2 %collective-permute-start = (bf16[21,16,8]{2,1,0:T(8,128)(2,1)S(1)}, bf16[21,16,8]{2,1,0:T(8,128)(2,1)S(1)}, u32[]{:S(2)}, u32[]{:S(2)}) collective-permute-start(bf16[21,16,8]{2,1,0:T(8,128)(2,1)S(1)} %get-tuple-element.303), channel_id=1, source_target_pairs={{0,32},{32,64},{64,96},{96,128},{128,160},{160,192},{192,224},{224... | collective-permute-start | bytes 16136 | tf_op jit(solution)/shard_map/ppermute | solution.py:17
  14.1 7.7 %collective-permute-start.1 = (bf16[21,16,8]{2,1,0:T(8,128)(2,1)S(1)}, bf16[21,16,8]{2,1,0:T(8,128)(2,1)S(1)}, u32[]{:S(2)}, u32[]{:S(2)}) collective-permute-start(bf16[21,16,8]{2,1,0:T(8,128)(2,1)S(1)} %get-tuple-element.304), channel_id=1, source_target_pairs={{32,0},{64,32},{96,64},{128,96},{160,128},{192,160},{224,192},{256... | collective-permute-start | bytes 16136 | tf_op jit(solution)/shard_map/ppermute | solution.py:19
  22.9 12.7 %collective-permute-start.2 = (bf16[21,8,144]{2,1,0:T(8,128)(2,1)S(1)}, bf16[21,8,144]{2,1,0:T(8,128)(2,1)S(1)}, u32[]{:S(2)}, u32[]{:S(2)}) collective-permute-start(bf16[21,8,144]{2,1,0:T(8,128)(2,1)S(1)} %get-tuple-element.301), channel_id=1, source_target_pairs={{0,4},{4,8},{8,12},{12,16},{16,20},{20,24},{24,28},{28,0},{1,5},{5... | collective-permute-start | bytes 145160 | tf_op jit(solution)/shard_map/ppermute | solution.py:17
  26.9 10.1 %collective-permute-start.3 = (bf16[21,8,144]{2,1,0:T(8,128)(2,1)S(1)}, bf16[21,8,144]{2,1,0:T(8,128)(2,1)S(1)}, u32[]{:S(2)}, u32[]{:S(2)}) collective-permute-start(bf16[21,8,144]{2,1,0:T(8,128)(2,1)S(1)} %get-tuple-element.302), channel_id=1, source_target_pairs={{4,0},{8,4},{12,8},{16,12},{20,16},{24,20},{28,24},{0,28},{5,1},{9... | collective-permute-start | bytes 145160 | tf_op jit(solution)/shard_map/ppermute | solution.py:19
  261.5 17.9 %collective-permute-start.4 = (f32[20,32,8]{2,1,0:T(8,128)S(1)}, f32[20,32,8]{2,1,0:T(8,128)S(1)}, u32[]{:S(2)}, u32[]{:S(2)}) collective-permute-start(f32[20,32,8]{2,1,0:T(8,128)S(1)} %get-tuple-element.298), channel_id=1, source_target_pairs={{0,32},{32,64},{64,96},{96,128},{128,160},{160,192},{192,224},{224... | collective-permute-start | bytes 61448 | tf_op jit(solution)/shard_map/ppermute | solution.py:17
  264.8 18.4 %collective-permute-start.5 = (f32[20,32,8]{2,1,0:T(8,128)S(1)}, f32[20,32,8]{2,1,0:T(8,128)S(1)}, u32[]{:S(2)}, u32[]{:S(2)}) collective-permute-start(f32[20,32,8]{2,1,0:T(8,128)S(1)} %get-tuple-element.297), channel_id=1, source_target_pairs={{32,0},{64,32},{96,64},{128,96},{160,128},{192,160},{224,192},{256... | collective-permute-start | bytes 61448 | tf_op jit(solution)/shard_map/ppermute | solution.py:19
  289.6 6.7 %collective-permute-start.6 = (f32[20,8,128]{2,1,0:T(8,128)S(1)}, f32[20,8,128]{2,1,0:T(8,128)S(1)}, u32[]{:S(2)}, u32[]{:S(2)}) collective-permute-start(f32[20,8,128]{2,1,0:T(8,128)S(1)} %get-tuple-element.300), channel_id=1, source_target_pairs={{0,4},{4,8},{8,12},{12,16},{16,20},{20,24},{24,28},{1,5},{5,9},{9,... | collective-permute-start | bytes 245768 | tf_op jit(solution)/shard_map/ppermute | solution.py:17
  295.0 5.2 %collective-permute-start.7 = (f32[20,8,128]{2,1,0:T(8,128)S(1)}, f32[20,8,128]{2,1,0:T(8,128)S(1)}, u32[]{:S(2)}, u32[]{:S(2)}) collective-permute-start(f32[20,8,128]{2,1,0:T(8,128)S(1)} %get-tuple-element.299), channel_id=1, source_target_pairs={{4,0},{8,4},{12,8},{16,12},{20,16},{24,20},{28,24},{5,1},{9,5},{13... | collective-permute-start | bytes 245768 | tf_op jit(solution)/shard_map/ppermute | solution.py:19
Sparse Core Ops, SparseCore 0:
  10.7 41.9 all-gather.1
  257.3 116.1 all-reduce.36
where the time goes:
time: 384 us; the launch traced here: 383 us
  waiting for transfers between devices  103 us (27%)
  local copies, waits for them, and re-layouts  99.5 us (26%)
  other arithmetic  71.5 us (19%)
  loops' own time  56.3 us (15%)
  starting transfers between devices  36.8 us (10%)
  between operations  15 us (4%)
    unnamed x3, waiting for transfers between devices  72.6 us
    while x544, local copies, waits for them, and re-layouts  63.6 us
    another operation x1, loops' own time, body(): lax.scan(step, init, jnp.arange(SPAN, dtype=jnp.int32))  56.3 us
    dynamic_update_slice x34, other arithmetic, body(): lax.scan(step, init, jnp.arange(SPAN, dtype=jnp.int32))  49.4 us
    ppermute x4, starting transfers between devices, extended_2(): lax.ppermute(head, axis, [((i + 1) % count, i) for i in range(ends)])  22.2 us
    all_gather x1, waiting for transfers between devices, body(): taper_full = lax.all_gather(taper, 'mem', axis=1, tiled=True)  15.5 us
    ppermute x4, starting transfers between devices, extended_2(): lax.ppermute(tail, axis, [(i, (i + 1) % count) for i in range(ends)])  14.5 us
    dynamic_slice x17, local copies, waits for them, and re-layouts, body(): lax.scan(step, init, jnp.arange(SPAN, dtype=jnp.int32))  9.9 us
  transfers between devices with their start and end apart: 10, of which 6 were waited for; matrix products, arithmetic and copies ran while one was open for 5% of the time, Pallas kernels for 0%

commit v1 on v0

v1 whole, which is shorter than its diff:
```python
import functools

import jax
import jax.numpy as jnp
from jax import lax
from jax.experimental import pallas as pl
from jax.experimental.pallas import tpu as pltpu
from jax.sharding import PartitionSpec as P

SPAN = 17
RIM = 8
TAPS = SPAN * SPAN
ROWS = 4
CLAT = 16
LON = 128
WIN = ROWS + 2 * RIM
RING = CLAT + RIM
GROUP = 20
MEMBERS = 80
DEPTH = 88
PART = GROUP * CLAT + 2 * GROUP
EDGES = 64
TAPE = 24
HALO = 3 * LON
LATROWS = MEMBERS * RIM + MEMBERS + RIM + 8
F32 = jnp.float32
BF16 = jnp.bfloat16
SMEM = pltpu.SMEM
VMEM = pltpu.VMEM


def lanes(shape):
    return lax.broadcasted_iota(jnp.int32, shape, len(shape) - 1)


def rows_of(shape):
    return lax.broadcasted_iota(jnp.int32, shape, len(shape) - 2)


def call(kernel, out_shape, scratch, *args):
    specs = [pl.BlockSpec(memory_space=SMEM)] + [pl.BlockSpec(memory_space=VMEM)] * (len(args) - 1)
    return pl.pallas_call(
        kernel,
        out_shape=out_shape,
        in_specs=specs,
        out_specs=jax.tree.map(lambda _: pl.BlockSpec(memory_space=VMEM), out_shape),
        scratch_shapes=scratch,
        compiler_params=pltpu.CompilerParams(vmem_limit_bytes=48 * 2**20),
    )(*args)


def shape(*dims, dtype=F32):
    return jax.ShapeDtypeStruct(dims, dtype)


def unpack_taper(taper_ref, wide):
    for tap in range(TAPS):
        wide[tap * ROWS : tap * ROWS + ROWS] = taper_ref[tap].astype(F32)


def edges_kernel(mem_ref, x_ref, v_ref, c_ref, taper_ref, left_ref, right_ref, wide, cells):
    unpack_taper(taper_ref, wide)
    cells[0 : GROUP * CLAT] = x_ref[...].astype(F32).reshape(GROUP * CLAT, LON)
    cells[GROUP * CLAT : (GROUP + 1) * CLAT] = v_ref[...].astype(F32)
    cells[(GROUP + 1) * CLAT : (GROUP + 2) * CLAT] = c_ref[...].astype(F32)
    cells[(GROUP + 2) * CLAT :] = jnp.zeros((2 * CLAT, LON), F32)
    lane = lanes((TAPE, LON))
    left = jnp.zeros((TAPE, LON), F32)
    right = jnp.zeros((TAPE, LON), F32)
    for lat in range(CLAT):
        part = cells[pl.ds(lat, TAPE, stride=CLAT), :]
        mine = lane // RIM == lat
        left = jnp.where(mine, pltpu.roll(part, RIM * lat, 1), left)
        right = jnp.where(mine, pltpu.roll(part, (RIM * lat + RIM) % LON, 1), right)
    left_ref[0:TAPE] = left.astype(BF16)
    right_ref[0:TAPE] = right.astype(BF16)
    lane = lanes((8, LON))
    row = rows_of((8, LON))
    for block in range(5):
        left = jnp.zeros((8, LON), F32)
        right = jnp.zeros((8, LON), F32)
        for sub in range(4):
            a = block * 4 + sub
            if a >= SPAN:
                continue
            for i in range(ROWS):
                to = sub * 32 + i * RIM
                mine = lane // RIM == to // RIM
                part = wide[pl.ds(a * SPAN * ROWS + i, 8, stride=ROWS), :]
                left = jnp.where(mine, pltpu.roll(part, to, 1), left)
                part = wide[pl.ds((a * SPAN + 9) * ROWS + i, 8, stride=ROWS), :]
                right = jnp.where(mine, pltpu.roll(part, (to + RIM) % LON, 1), right)
        for bit in (1, 2, 4):
            moved = pltpu.roll(left, bit, 0)
            moved = jnp.where(row >= bit, moved, 0.0)
            left = jnp.where((lane & bit) != 0, moved, left)
            moved = pltpu.roll(right, 8 - bit, 0)
            moved = jnp.where(row < 8 - bit, moved, 0.0)
            right = jnp.where(((7 - lane) & bit) != 0, moved, right)
        at = TAPE + 8 * block
        left_ref[at : at + 8] = left.astype(BF16)
        right_ref[at : at + 8] = right.astype(BF16)


def edge_messages(mem, anomalies, vector, cotangent, taper):
    return call(
        edges_kernel,
        (shape(EDGES, LON, dtype=BF16),) * 2,
        [
            VMEM((TAPS * ROWS + 4, LON), F32),
            VMEM(((GROUP + 4) * CLAT, LON), F32),
        ],
        mem,
        anomalies,
        vector,
        cotangent,
        taper,
    )


def ring_row(mem, j):
    lat = ROWS * mem - RIM + j
    return jnp.where(lat < 0, lat + RING, lat)


def halo_row(side, ring):
    inside = side * LON + RIM * ring
    outside = 2 * LON + side * (LON // 2) + RIM * (ring - CLAT)
    return pl.multiple_of(jnp.where(ring < CLAT, inside, outside), 8)


def bands_kernel(mem_ref, taper_ref, band_ref, rim_ref, wide, narrow):
    mem = mem_ref[0]
    unpack_taper(taper_ref, wide)
    narrow[...] = jnp.zeros(narrow.shape, F32)
    for i in range(ROWS):
        for j in range(WIN):
            if j < i or j > i + SPAN - 1:
                band_ref[j * LON : (j + 1) * LON, i * LON : (i + 1) * LON] = jnp.zeros(
                    (LON, LON), BF16
                )
    lane = lanes((24, LON))
    row = rows_of((24, LON))
    group = lanes((8, LON)) // 8
    zero = jnp.zeros((8, LON), F32)

    @pl.loop(0, SPAN)
    def _(a):
        for i in range(ROWS):
            taps = wide[pl.ds(a * SPAN * ROWS + i, 24, stride=ROWS), :]
            taps = jnp.where(row < SPAN, taps, 0.0)
            for bit in (1, 2, 4):
                taps = jnp.where((lane & bit) != 0, pltpu.roll(taps, bit, 0), taps)
            low, mid, high = taps[0:8], taps[8:16], taps[16:24]
            parts = []
            for block in range(CLAT):
                part = jnp.where(group == block, mid, zero)
                if block < 15:
                    part = jnp.where(group == block + 1, low, part)
                if block > 0:
                    part = jnp.where(group == block - 1, high, part)
                parts.append(part)
            band_ref[pl.ds(pl.multiple_of((a + i) * LON, LON), LON), i * LON : (i + 1) * LON] = (
                jnp.concatenate(parts, 0).astype(BF16)
            )
            ring = ring_row(mem, a + i)
            narrow[pl.ds(halo_row(0, ring), 8), i * LON : (i + 1) * LON] = jnp.where(
                group == 15, high, zero
            )
            narrow[pl.ds(halo_row(1, ring), 8), i * LON : (i + 1) * LON] = jnp.where(
                group == 0, low, zero
            )

    rim_ref[...] = narrow[...].astype(BF16)


def bands(mem, taper):
    return call(
        bands_kernel,
        (shape(WIN * LON, ROWS * LON, dtype=BF16), shape(HALO, ROWS * LON, dtype=BF16)),
        [VMEM((1184, LON), F32), VMEM((HALO, ROWS * LON), F32)],
        mem,
        taper,
    )


def split(value):
    high = value.astype(BF16)
    return high, (value - high.astype(F32)).astype(BF16)


def gathered_rows(wide, start, stride):
    parts = [wide[pl.ds(g * PART + start, GROUP, stride=stride), :] for g in range(4)]
    return jnp.concatenate(parts, 0)


def push_kernel(
    mem_ref, x_ref, c_ref, left_ref, right_ref, band_ref, out_ref, rim_ref, wide, c32, scaled, corner
):
    mem = mem_ref[0]
    wide[...] = x_ref[...].astype(F32)
    c32[...] = c_ref[...].astype(F32)
    for i in range(ROWS):
        own = gathered_rows(wide, ROWS * mem + i, CLAT) * c32[pl.ds(ROWS * mem + i, 1), :]
        high, low = split(own)
        scaled[0:MEMBERS, i * LON : (i + 1) * LON] = high
        scaled[MEMBERS:, i * LON : (i + 1) * LON] = low
    lane = lanes((MEMBERS, LON))
    east = gathered_rows(wide, GROUP * CLAT, 1) * right_ref[16:24].astype(F32)[5:6]
    west = gathered_rows(wide, GROUP * CLAT + GROUP, 1) * left_ref[16:24].astype(F32)[5:6]
    east = pltpu.roll(east, (LON - 32 * mem) % LON, 1)
    west = pltpu.roll(west, (LON + 32 - 32 * mem) % LON, 1)
    high, low = split(jnp.where(lane < 32, east, jnp.where(lane < 64, west, 0.0)))
    scaled[0:MEMBERS, ROWS * LON :] = high
    scaled[MEMBERS:, ROWS * LON :] = low
    lane = lanes((8, LON))
    corner[...] = jnp.zeros(corner.shape, BF16)
    tiles = []
    for side, ref in ((0, right_ref), (1, left_ref)):
        packed = ref[TAPE:EDGES].astype(F32)
        tiles.append(
            [
                pltpu.roll(packed[8 * (a // 4) : 8 * (a // 4) + 8], (LON + 32 * side - 32 * (a % 4)) % LON, 1)
                for a in range(SPAN)
            ]
        )
    zero = jnp.zeros((8, LON), F32)
    for j in range(WIN):
        edge = []
        for side in range(2):
            tile = zero
            for i in range(ROWS):
                if 0 <= j - i < SPAN:
                    tile = jnp.where(lane // RIM == 4 * side + i, tiles[side][j - i], tile)
            edge.append(tile)
        corner[j * LON : j * LON + 16] = jnp.concatenate([edge[1], zero], 0).astype(BF16)
        corner[j * LON + 112 : j * LON + 128] = jnp.concatenate([zero, edge[0]], 0).astype(BF16)
    unused = jnp.where(mem < 2, jnp.where(mem == 0, 12, 16), jnp.where(mem == 2, 20, 0))
    zeros = jnp.zeros((MEMBERS, LON), F32)
    for extra in range(4):
        ring = unused + extra

        @pl.when(ring < CLAT)
        def _():
            out_ref[pl.ds(ring, MEMBERS, stride=CLAT), :] = zeros

        @pl.when(ring >= CLAT)
        def _():
            rim_ref[pl.ds(ring - CLAT, MEMBERS, stride=RIM), :] = zeros

    @pl.loop(0, WIN)
    def _(j):
        at = pl.multiple_of(j * LON, LON)
        both = lax.dot_general(
            scaled[:, : ROWS * LON],
            band_ref[pl.ds(at, LON), :],
            (((1,), (1,)), ((), ())),
            preferred_element_type=F32,
        )
        both = both + lax.dot_general(
            scaled[:, ROWS * LON :],
            corner[pl.ds(at, LON), :],
            (((1,), (1,)), ((), ())),
            preferred_element_type=F32,
        )
        total = both[:MEMBERS] + both[MEMBERS:]
        ring = ring_row(mem, j)

        @pl.when(ring < CLAT)
        def _():
            out_ref[pl.ds(ring, MEMBERS, stride=CLAT), :] = total

        @pl.when(ring >= CLAT)
        def _():
            rim_ref[pl.ds(ring - CLAT, MEMBERS, stride=RIM), :] = total


def push(mem, gathered, cotangent, from_left, from_right, band):
    return call(
        push_kernel,
        (shape(MEMBERS * CLAT, LON), shape(MEMBERS * RIM, LON)),
        [
            VMEM((4 * PART, LON), F32),
            VMEM((CLAT, LON), F32),
            VMEM((2 * MEMBERS, (ROWS + 1) * LON), BF16),
            VMEM((WIN * LON, LON), BF16),
        ],
        mem,
        gathered,
        cotangent,
        from_left,
        from_right,
        band,
    )


def own_kernel(
    mem_ref, x_ref, lat_ref, v_ref, c_ref, left_ref, right_ref, band_ref, rim_ref, push_ref,
    taper_ref, out_ref,
    wide, wide_lat, v32, c32, window, own, scaled, turned, product, shifted, flat,
):
    mem = mem_ref[0]
    wide[...] = x_ref[...].astype(F32)
    wide_lat[...] = lat_ref[...].astype(F32)
    v32[...] = v_ref[...].astype(F32)
    c32[...] = c_ref[...].astype(F32)
    pad = jnp.zeros((DEPTH - MEMBERS - 1, LON), F32)
    base = MEMBERS * RIM

    def put(at, field, weight):
        high, low = split(field * weight)
        scaled[0:MEMBERS, at : at + LON] = high
        scaled[MEMBERS:, at : at + LON] = low
        whole = jnp.concatenate([field, weight, pad], 0)
        turned[at : at + LON, :] = whole.T.astype(BF16)

    for j in range(WIN):
        ring = ring_row(mem, j)

        @pl.when(ring < CLAT)
        def _():
            window[j, 0:MEMBERS] = gathered_rows(wide, ring, CLAT)
            window[j, MEMBERS : MEMBERS + 1] = v32[pl.ds(ring, 1), :]

        @pl.when(ring >= CLAT)
        def _():
            window[j, 0:MEMBERS] = wide_lat[pl.ds(ring - CLAT, MEMBERS, stride=RIM), :]
            window[j, MEMBERS : MEMBERS + 1] = wide_lat[pl.ds(base + MEMBERS + ring - CLAT, 1), :]

    for j in range(WIN):
        put(j * LON, window[j, 0:MEMBERS], window[j, MEMBERS : MEMBERS + 1])
    main = WIN * LON
    put(main, gathered_rows(wide, GROUP * CLAT, 1), right_ref[16:24].astype(F32)[4:5])
    put(main + LON, gathered_rows(wide, GROUP * CLAT + GROUP, 1), left_ref[16:24].astype(F32)[4:5])
    put(
        main + 2 * LON,
        wide_lat[base : base + MEMBERS],
        wide_lat[base + MEMBERS + RIM : base + MEMBERS + RIM + 1],
    )
    for i in range(ROWS):
        own[0:MEMBERS, i * LON : (i + 1) * LON] = gathered_rows(wide, ROWS * mem + i, CLAT).astype(BF16)
        own[MEMBERS:, i * LON : (i + 1) * LON] = jnp.zeros((DEPTH - MEMBERS, LON), BF16)
    own[:, ROWS * LON :] = jnp.where(rows_of((DEPTH, LON)) == MEMBERS, 1.0, 0.0).astype(BF16)

    both = jnp.dot(scaled[:, :main], band_ref[...], preferred_element_type=F32)
    both = both + jnp.dot(scaled[:, main:], rim_ref[...], preferred_element_type=F32)
    total = both[:MEMBERS] + both[MEMBERS:]
    share = 1.0 / (MEMBERS - 1)
    for row in range(CLAT):
        out_ref[pl.ds(row, MEMBERS, stride=CLAT), :] = push_ref[
            pl.ds(row, MEMBERS, stride=CLAT), :
        ] * (v32[row : row + 1] * share)
    for i in range(ROWS):
        at = pl.ds(ROWS * mem + i, MEMBERS, stride=CLAT)
        c_row = c32[pl.ds(ROWS * mem + i, 1), :] * share
        out_ref[at, :] = out_ref[at, :] + total[:, i * LON : (i + 1) * LON] * c_row

    step = 2 * LON
    for at in range(0, main + HALO, LON):
        product[at : at + LON] = jnp.dot(turned[at : at + LON], own[...], preferred_element_type=F32)

    lane = lanes((8, LON))
    wide_lane = lanes((24, LON))

    def diagonals(j, ring, column):
        at = pl.ds(column, LON)
        cells = [product[pl.ds(halo_row(1, ring), 8), column : column + LON]]
        for block in range(CLAT):
            cells.append(
                product[pl.ds(pl.multiple_of(j * LON + 8 * block, 8), 8), column : column + LON]
            )
        cells.append(product[pl.ds(halo_row(0, ring), 8), column : column + LON])
        for bit in (8, 4, 2, 1):
            take = (lane & (8 * bit)) != 0
            cells = [jnp.where(take, cells[s + bit], cells[s]) for s in range(len(cells) - bit)]
        taps = jnp.concatenate(cells, 0)
        for bit in (1, 2, 4):
            taps = jnp.where((wide_lane & bit) != 0, pltpu.roll(taps, 24 - bit, 0), taps)
        return taps

    def halo_row(side, ring):
        inside = side * LON + RIM * ring
        outside = 2 * LON + side * (LON // 2) + RIM * (ring - CLAT)
        return pl.multiple_of(main + jnp.where(ring < CLAT, inside, outside), 8)

    @pl.loop(0, WIN)
    def _(j):
        shifted[j] = diagonals(j, ring_row(mem, j), ROWS * LON)

    @pl.loop(0, SPAN)
    def _(a):
        for i in range(ROWS):
            taps = diagonals(a + i, ring_row(mem, a + i), i * LON)
            c_row = c32[pl.ds(ROWS * mem + i, 1), :] * share
            taps = taps * shifted[a + i] * c_row
            flat[pl.ds(a * SPAN * ROWS + i, SPAN, stride=ROWS), :] = taps[0:SPAN]

    for tap in range(TAPS):
        taper_ref[tap] = flat[tap * ROWS : tap * ROWS + ROWS]


def own_rows(mem, gathered, lat_halo, vector, cotangent, from_left, from_right, band, rim, pushed):
    return call(
        own_kernel,
        (shape(TAPS, ROWS, LON), shape(MEMBERS * CLAT, LON)),
        [
            VMEM((4 * PART, LON), F32),
            VMEM((LATROWS, LON), F32),
            VMEM((CLAT, LON), F32),
            VMEM((CLAT, LON), F32),
            VMEM((WIN, DEPTH, LON), F32),
            VMEM((DEPTH, (ROWS + 1) * LON), BF16),
            VMEM((2 * MEMBERS, WIN * LON + HALO), BF16),
            VMEM((WIN * LON + HALO, DEPTH), BF16),
            VMEM((WIN * LON + HALO, (ROWS + 1) * LON), F32),
            VMEM((WIN, 24, LON), F32),
            VMEM((TAPS * ROWS, LON), F32),
        ],
        mem,
        gathered,
        lat_halo,
        vector,
        cotangent,
        from_left,
        from_right,
        band,
        rim,
        pushed,
    )


def body(anomalies, vector, cotangent, taper):
    mem = lax.axis_index("mem")
    index = mem.astype(jnp.int32).reshape(1)
    bands_of_lat = lax.axis_size("lat")
    strips = lax.axis_size("lon")
    upper = mem < 2

    left, right = edge_messages(index, anomalies, vector, cotangent, taper)
    ring = [(i, (i + 1) % strips) for i in range(strips)]
    from_left = lax.ppermute(right, "lon", ring)
    from_right = lax.ppermute(left, "lon", [(b, a) for a, b in ring])
    band, rim = bands(index, taper)

    message = jnp.concatenate(
        [anomalies.reshape(GROUP * CLAT, LON), from_right[:GROUP], from_left[:GROUP]], 0
    )
    gathered = lax.all_gather(message, "mem", axis=0, tiled=True)

    down = [(4 * z + m, 4 * z + 4 + m) for z in range(bands_of_lat - 1) for m in (0, 1)]
    up = [(4 * z + 4 + m, 4 * z + m) for z in range(bands_of_lat - 1) for m in (2, 3)]
    groups = gathered.reshape(4, PART, LON)
    first = jnp.where(upper, RIM, 0)
    cells = lax.dynamic_slice_in_dim(
        groups[:, : GROUP * CLAT].reshape(MEMBERS, CLAT, LON), first, RIM, 1
    ).reshape(MEMBERS * RIM, LON)
    east = groups[:, GROUP * CLAT : GROUP * CLAT + GROUP].reshape(MEMBERS, LON)
    west = groups[:, GROUP * CLAT + GROUP :].reshape(MEMBERS, LON)
    east = jnp.concatenate([east, from_right[GROUP : GROUP + 1]], 0)
    west = jnp.concatenate([west, from_left[GROUP : GROUP + 1]], 0)
    half = LON // 2
    sides = jnp.where(
        upper,
        jnp.concatenate([east[:, half:], west[:, half:]], 1),
        jnp.concatenate([east[:, :half], west[:, :half]], 1),
    )
    v_rows = lax.dynamic_slice_in_dim(vector, first, RIM, 0)
    lat_message = jnp.concatenate(
        [cells, sides[:MEMBERS], v_rows, sides[MEMBERS:], jnp.zeros((7, LON), BF16)], 0
    )
    lat_halo = lax.ppermute(lat_message, ("lat", "mem"), down + up)

    pushed, pushed_out = push(index, gathered, cotangent, from_left, from_right, band)
    back = lax.ppermute(pushed_out, ("lat", "mem"), [(b, a) for a, b in down + up])

    grad_taper, partial = own_rows(
        index, gathered, lat_halo, vector, cotangent, from_left, from_right, band, rim, pushed
    )

    share = vector.astype(F32) / (MEMBERS - 1)
    back = back.reshape(MEMBERS, RIM, LON)
    none = jnp.zeros_like(back)
    placed = jnp.where(
        upper, jnp.concatenate([none, back], 1), jnp.concatenate([back, none], 1)
    )
    partial = partial.reshape(MEMBERS, CLAT, LON) + placed * share[None]
    pairs = partial.reshape(2, 2, GROUP, CLAT, LON)
    core = mem % 2
    far = mem // 2
    keep = lax.dynamic_index_in_dim(pairs, core, 1, keepdims=False)
    send = lax.dynamic_index_in_dim(pairs, 1 - core, 1, keepdims=False)
    keep = keep + lax.ppermute(send, "mem", [(0, 1), (1, 0), (2, 3), (3, 2)])
    mine = lax.dynamic_index_in_dim(keep, far, 0, keepdims=False)
    send = lax.dynamic_index_in_dim(keep, 1 - far, 0, keepdims=False)
    grad_anomalies = mine + lax.ppermute(send, "mem", [(0, 2), (2, 0), (1, 3), (3, 1)])
    return grad_taper, grad_anomalies


def solution(mesh):
    placed = (
        P("mem", "lat", "lon"),
        P("lat", "lon"),
        P("lat", "lon"),
        P(None, ("lat", "mem"), "lon"),
    )
    return jax.shard_map(
        body,
        mesh=mesh,
        in_specs=placed,
        out_specs=(P(None, ("lat", "mem"), "lon"), P("mem", "lat", "lon")),
        check_vma=False,
    )
```

time: 384 us -> 85.3 us (0.22)
  the two profiles are of different devices: /device:TPU:1 before, /device:TPU:192 now
where the time goes in v1:
time: 85.3 us; the launch traced here: 84.6 us
  starting transfers between devices  26.7 us (31%)
  waiting for transfers between devices  18.4 us (22%)
  Pallas kernels  13.4 us (16%)
  local copies, waits for them, and re-layouts  11.7 us (14%)
  blocking collectives  10.6 us (12%)
  other arithmetic  2.96 us (3%)
  between operations  0.91 us (1%)
    pallas_call x4, Pallas kernels, call(): pl.pallas_call(kernel, out_shape=out_shape, in_specs=specs, out_specs=jax...  13.4 us
    all_gather x1, blocking collectives, body(): gathered = lax.all_gather(message, 'mem', axis=0, tiled=True)  10.6 us
    ppermute x1, starting transfers between devices, body(): lax.ppermute(send, 'mem', [(0, 2), (2, 0), (1, 3), (3, 1)])  7.75 us
    ppermute x1, starting transfers between devices, body(): from_right = lax.ppermute(left, 'lon', [(b, a) for a, b in ring])  7.7 us
    ppermute x1, waiting for transfers between devices, body(): lax.ppermute(send, 'mem', [(0, 2), (2, 0), (1, 3), (3, 1)])  7.38 us
    unnamed x20, local copies, waits for them, and re-layouts  6.82 us
    ppermute x1, starting transfers between devices, body(): lat_halo = lax.ppermute(lat_message, ('lat', 'mem'), down + up)  5.48 us
    ppermute x1, waiting for transfers between devices, body(): lat_halo = lax.ppermute(lat_message, ('lat', 'mem'), down + up)  4.75 us
  transfers between devices with their start and end apart: 6, of which 4 were waited for; matrix products, arithmetic and copies ran while one was open for 6% of the time, Pallas kernels for 9%

profile of v1, /device:TPU:192, one launch (start us, length us, event | category | flops | bytes accessed | tf_op | source)
XLA Modules:
  0.0 84.6 jit_solution(14055035632347432083)
XLA Ops:
  0.6 0.0 copy-start
  0.6 1.0 %copy-done = bf16[289,4,128]{2,1,0:T(4,128)(2,1)S(1)} copy-done((bf16[289,4,128]{2,1,0:T(4,128)(2,1)S(1)}, bf16[289,4,128]{2,1,0:T(4,128)(2,1)}, u32[]{:S(2)}) %copy-start) | copy-done | bytes 295960
  1.6 0.0 copy-start.4
  1.6 0.9 %copy-done.4 = bf16[20,16,128]{2,1,0:T(8,128)(2,1)S(1)} copy-done((bf16[20,16,128]{2,1,0:T(8,128)(2,1)S(1)}, bf16[20,16,128]{2,1,0:T(8,128)(2,1)}, u32[]{:S(2)}) %copy-start.4) | copy-done | bytes 81944
  2.5 0.0 copy-start.5
  2.5 0.7 copy-done.5
  3.2 0.0 copy-start.7
  3.2 0.7 copy-done.7
  3.9 0.3 shard_map.59
  4.1 7.7 %collective-permute-start = (bf16[64,128]{1,0:T(8,128)(2,1)S(1)}, bf16[64,128]{1,0:T(8,128)(2,1)S(1)}, u32[]{:S(2)}, u32[]{:S(2)}) collective-permute-start(bf16[64,128]{1,0:T(8,128)(2,1)S(1)} %get-tuple-element.10), channel_id=1, source_target_pairs={{32,0},{64,32},{96,64},{128,96},{160,128},{192,160},{224,192},{256... | collective-permute-start | bytes 49160 | tf_op jit(solution)/shard_map/ppermute | solution.py:442
  11.9 1.9 %collective-permute-start.1 = (bf16[64,128]{1,0:T(8,128)(2,1)S(1)}, bf16[64,128]{1,0:T(8,128)(2,1)S(1)}, u32[]{:S(2)}, u32[]{:S(2)}) collective-permute-start(bf16[64,128]{1,0:T(8,128)(2,1)S(1)} %get-tuple-element.11), channel_id=1, source_target_pairs={{0,32},{32,64},{64,96},{96,128},{128,160},{160,192},{192,224},{224... | collective-permute-start | bytes 49160 | tf_op jit(solution)/shard_map/ppermute | solution.py:441
  13.8 0.7 constant_dynamic-slice_fusion
  14.5 0.0 copy-start.1
  14.5 1.0 %copy-done.1 = bf16[289,4,128]{2,1,0:T(4,128)(2,1)S(1)} copy-done((bf16[289,4,128]{2,1,0:T(4,128)(2,1)S(1)}, bf16[289,4,128]{2,1,0:T(4,128)(2,1)}, u32[]{:S(2)}) %copy-start.1) | copy-done | bytes 295960
  15.4 1.3 %shard_map.60 = (bf16[2560,512]{1,0:T(8,128)(2,1)S(1)}, bf16[384,512]{1,0:T(8,128)(2,1)S(1)}) custom-call(s32[1]{0:T(128)} %bitcast.mem_ref, bf16[289,4,128]{2,1,0:T(4,128)(2,1)S(1)} %copy-done.1), custom_call_target="tpu_custom_call" | custom-call | tf_op jit(solution)/shard_map/pallas_call | solution.py:42
  16.7 0.0 collective-permute-done.right_ref
  16.7 4.7 %collective-permute-done.1.left_ref = bf16[64,128]{1,0:T(8,128)(2,1)S(1)} collective-permute-done((bf16[64,128]{1,0:T(8,128)(2,1)S(1)}, bf16[64,128]{1,0:T(8,128)(2,1)S(1)}, u32[]{:S(2)}, u32[]{:S(2)}) %collective-permute-start.1) | collective-permute-done | bytes 16416 | tf_op jit(solution)/shard_map/ppermute | solution.py:441
  21.4 0.9 %pad_maximum_fusion = bf16[360,128]{1,0:T(8,128)(2,1)S(1)} fusion(bf16[20,128]{1,0:T(8,128)(2,1)S(1)} %slice.53, bf16[20,128]{1,0:T(8,128)(2,1)S(1)} %slice.52, bf16[320,128]{1,0:T(8,128)(2,1)} %bitcast.20), kind=kLoop, calls=%fused_computation.6 | loop fusion | flops 276480 | bytes 184320 | tf_op jit(solution)/shard_map/concatenate | solution.py:445
  22.3 0.0 copy-start.6
  22.3 0.0 copy-start.9
  22.3 10.6 %all_gather.3.x_ref = bf16[1440,128]{1,0:T(8,128)(2,1)S(1)} all-gather(bf16[360,128]{1,0:T(8,128)(2,1)S(1)} %pad_maximum_fusion), channel_id=1, replica_groups=mesh['lon'=16,'lat'=8,'mem'=4] {'mem'}, dimensions={0}, use_global_device_ids=true | all-gather | bytes 460800 | tf_op jit(solution)/shard_map/all_gather | solution.py:448
  33.0 0.1 fusion.2
  33.1 0.1 fusion.5
  33.2 0.0 copy-start.8
  33.3 0.7 copy-done.8
  33.9 5.6 %shard_map.61 = (f32[1280,128]{1,0:T(8,128)S(1)}, f32[640,128]{1,0:T(8,128)}) custom-call(s32[1]{0:T(128)} %bitcast.mem_ref, bf16[1440,128]{1,0:T(8,128)(2,1)S(1)} %all_gather.3.x_ref, bf16[16,128]{1,0:T(8,128)(2,1)S(1)} %copy-done.8, bf16[64,128]{1,0:T(8,128)(2,1)S(1)} %collective-permute-done.1.left_ref, ...), custom_call_target="tpu_custom_call" | custom-call | tf_op jit(solution)/shard_map/pallas_call | solution.py:42
  39.6 0.0 copy-start.2
  39.6 0.9 %copy-done.2 = f32[1280,128]{1,0:T(8,128)} copy-done((f32[1280,128]{1,0:T(8,128)}, f32[1280,128]{1,0:T(8,128)S(1)}, u32[]{:S(2)}) %copy-start.2) | copy-done | bytes 655384
  40.4 1.9 %collective-permute-start.3 = (f32[640,128]{1,0:T(8,128)}, f32[640,128]{1,0:T(8,128)}, u32[]{:S(2)}, u32[]{:S(2)}) collective-permute-start(f32[640,128]{1,0:T(8,128)} %get-tuple-element.17), channel_id=1, source_target_pairs={{4,0},{5,1},{8,4},{9,5},{12,8},{13,9},{16,12},{17,13},{20,16},{21,... | collective-permute-start | bytes 983048 | tf_op jit(solution)/shard_map/ppermute | solution.py:474
  42.4 0.7 dynamic-slice_bitcast_fusion.2
  43.0 3.4 %concatenate.29 = bf16[736,128]{1,0:T(8,128)(2,1)} concatenate(bf16[640,128]{1,0:T(8,128)(2,1)} %dynamic-slice_bitcast_fusion.2, bf16[80,128]{1,0:T(8,128)(2,1)S(1)} %slice.63, bf16[8,128]{1,0:T(8,128)(2,1)S(1)} %constant_dynamic-slice_fusion, bf16[1,128]{1,0:T(2,128)(2,1)S(1)} %slice.64, bf16[7,128]{1,0:T(8,128)(2,1)S(1)} %broadcast_in_dim.2), dimensions={0} | concatenate | bytes 376832 | tf_op jit(solution)/shard_map/concatenate | solution.py:468
  46.4 5.5 %collective-permute-start.2 = (bf16[736,128]{1,0:T(8,128)(2,1)}, bf16[736,128]{1,0:T(8,128)(2,1)S(1)}, u32[]{:S(2)}, u32[]{:S(2)}) collective-permute-start(bf16[736,128]{1,0:T(8,128)(2,1)} %concatenate.29), channel_id=1, source_target_pairs={{0,4},{1,5},{4,8},{5,9},{8,12},{9,13},{12,16},{13,17},{16,20},{17,... | collective-permute-start | bytes 565256 | tf_op jit(solution)/shard_map/ppermute | solution.py:471
  51.9 0.0 copy-done.6
  51.9 4.8 %collective-permute-done.2.lat_ref = bf16[736,128]{1,0:T(8,128)(2,1)S(1)} collective-permute-done((bf16[736,128]{1,0:T(8,128)(2,1)}, bf16[736,128]{1,0:T(8,128)(2,1)S(1)}, u32[]{:S(2)}, u32[]{:S(2)}) %collective-permute-start.2) | collective-permute-done | bytes 188448 | tf_op jit(solution)/shard_map/ppermute | solution.py:471
  56.7 0.0 copy-done.9
  56.7 0.0 copy-start.3
  56.7 1.1 %copy-done.3 = f32[1280,128]{1,0:T(8,128)S(1)} copy-done((f32[1280,128]{1,0:T(8,128)S(1)}, f32[1280,128]{1,0:T(8,128)}, u32[]{:S(2)}) %copy-start.3) | copy-done | bytes 655384
  57.8 6.2 %shard_map.62 = (f32[289,4,128]{2,1,0:T(4,128)}, f32[1280,128]{1,0:T(8,128)S(1)}) custom-call(s32[1]{0:T(128)} %bitcast.mem_ref, bf16[1440,128]{1,0:T(8,128)(2,1)S(1)} %all_gather.3.x_ref, bf16[736,128]{1,0:T(8,128)(2,1)S(1)} %collective-permute-done.2.lat_ref, bf16[16,128]{1,0:T(8,128)(2,1)S(1)} %copy-done.6, bf16[16,128]{1,0:T(8,128)(2,1)S(1)} %copy-done.9, ...), custom_call_target="tpu_custom_call" | custom-call | tf_op jit(solution)/shard_map/pallas_call | solution.py:42
  64.0 0.0 collective-permute-done.3
  64.0 1.2 %multiply_add_fusion = f32[80,16,128]{2,1,0:T(8,128)S(1)} fusion(f32[80,16,128]{2,1,0:T(8,128)S(1)} %bitcast.19, f32[80,8,128]{2,1,0:T(8,128)} %bitcast.6, f32[16,128]{1,0:T(8,128)S(1)} %convert_multiply_fusion, pred[]{:T(512)S(6)} %lt.25), kind=kLoop, calls=%fused_computation | loop fusion | flops 491520 | bytes 1646593 | tf_op jit(solution)/shard_map/add | solution.py:486
  65.2 1.9 %collective-permute-start.4 = (f32[2,20,16,128]{3,2,1,0:T(8,128)S(1)}, f32[2,20,16,128]{3,2,1,0:T(8,128)S(1)}, u32[]{:S(2)}, u32[]{:S(2)}) collective-permute-start(f32[2,20,16,128]{3,2,1,0:T(8,128)S(1)} %dynamic-slice_bitcast_fusion), channel_id=1, source_target_pairs={{0,1},{1,0},{2,3},{3,2},{4,5},{5,4},{6,7},{7,6},{8,9},{9,8},{10,11... | collective-permute-start | bytes 983048 | tf_op jit(solution)/shard_map/ppermute | solution.py:492
  67.2 1.6 %collective-permute-done.4 = f32[2,20,16,128]{3,2,1,0:T(8,128)S(1)} collective-permute-done((f32[2,20,16,128]{3,2,1,0:T(8,128)S(1)}, f32[2,20,16,128]{3,2,1,0:T(8,128)S(1)}, u32[]{:S(2)}, u32[]{:S(2)}) %collective-permute-start.4) | collective-permute-done | bytes 327712 | tf_op jit(solution)/shard_map/ppermute | solution.py:492
  68.8 7.7 %collective-permute-start.5 = (f32[20,16,128]{2,1,0:T(8,128)S(1)}, f32[20,16,128]{2,1,0:T(8,128)S(1)}, u32[]{:S(2)}, u32[]{:S(2)}) collective-permute-start(f32[20,16,128]{2,1,0:T(8,128)S(1)} %dynamic-slice_bitcast_fusion.1), channel_id=1, source_target_pairs={{0,2},{2,0},{1,3},{3,1},{4,6},{6,4},{5,7},{7,5},{8,10},{10,8},{9,1... | collective-permute-start | bytes 491528 | tf_op jit(solution)/shard_map/ppermute | solution.py:495
  76.6 7.4 %collective-permute-done.5 = f32[20,16,128]{2,1,0:T(8,128)S(1)} collective-permute-done((f32[20,16,128]{2,1,0:T(8,128)S(1)}, f32[20,16,128]{2,1,0:T(8,128)S(1)}, u32[]{:S(2)}, u32[]{:S(2)}) %collective-permute-start.5) | collective-permute-done | bytes 163872 | tf_op jit(solution)/shard_map/ppermute | solution.py:495
  83.9 0.7 bitcast_add_fusion.1
  (15 shorter events, 0.2 us)
Async XLA Ops:
  0.6 1.0 %copy-start = (bf16[289,4,128]{2,1,0:T(4,128)(2,1)S(1)}, bf16[289,4,128]{2,1,0:T(4,128)(2,1)}, u32[]{:S(2)}) copy-start(bf16[289,4,128]{2,1,0:T(4,128)(2,1)} %taper_ref.3) | copy-start | bytes 887812
  1.6 0.9 %copy-start.4 = (bf16[20,16,128]{2,1,0:T(8,128)(2,1)S(1)}, bf16[20,16,128]{2,1,0:T(8,128)(2,1)}, u32[]{:S(2)}) copy-start(bf16[20,16,128]{2,1,0:T(8,128)(2,1)} %x_ref.1) | copy-start | bytes 245764
  2.5 0.7 copy-start.5
  3.2 0.7 copy-start.7
  4.1 12.6 %collective-permute-start = (bf16[64,128]{1,0:T(8,128)(2,1)S(1)}, bf16[64,128]{1,0:T(8,128)(2,1)S(1)}, u32[]{:S(2)}, u32[]{:S(2)}) collective-permute-start(bf16[64,128]{1,0:T(8,128)(2,1)S(1)} %get-tuple-element.10), channel_id=1, source_target_pairs={{32,0},{64,32},{96,64},{128,96},{160,128},{192,160},{224,192},{256... | collective-permute-start | bytes 49160 | tf_op jit(solution)/shard_map/ppermute | solution.py:442
  11.9 9.5 %collective-permute-start.1 = (bf16[64,128]{1,0:T(8,128)(2,1)S(1)}, bf16[64,128]{1,0:T(8,128)(2,1)S(1)}, u32[]{:S(2)}, u32[]{:S(2)}) collective-permute-start(bf16[64,128]{1,0:T(8,128)(2,1)S(1)} %get-tuple-element.11), channel_id=1, source_target_pairs={{0,32},{32,64},{64,96},{96,128},{128,160},{160,192},{192,224},{224... | collective-permute-start | bytes 49160 | tf_op jit(solution)/shard_map/ppermute | solution.py:441
  14.5 1.0 %copy-start.1 = (bf16[289,4,128]{2,1,0:T(4,128)(2,1)S(1)}, bf16[289,4,128]{2,1,0:T(4,128)(2,1)}, u32[]{:S(2)}) copy-start(bf16[289,4,128]{2,1,0:T(4,128)(2,1)} %taper_ref.3) | copy-start | bytes 887812
  22.3 29.6 %copy-start.6 = (bf16[16,128]{1,0:T(8,128)(2,1)S(1)}, bf16[16,128]{1,0:T(8,128)(2,1)}, u32[]{:S(2)}) copy-start(bf16[16,128]{1,0:T(8,128)(2,1)} %v_ref.3) | copy-start | bytes 12292
  22.3 34.4 %copy-start.9 = (bf16[16,128]{1,0:T(8,128)(2,1)S(1)}, bf16[16,128]{1,0:T(8,128)(2,1)}, u32[]{:S(2)}) copy-start(bf16[16,128]{1,0:T(8,128)(2,1)} %c_ref.5) | copy-start | bytes 12292
  33.2 0.7 copy-start.8
  39.6 0.9 %copy-start.2 = (f32[1280,128]{1,0:T(8,128)}, f32[1280,128]{1,0:T(8,128)S(1)}, u32[]{:S(2)}) copy-start(f32[1280,128]{1,0:T(8,128)S(1)} %get-tuple-element.14.push_ref) | copy-start | bytes 1966084
  40.4 23.6 %collective-permute-start.3 = (f32[640,128]{1,0:T(8,128)}, f32[640,128]{1,0:T(8,128)}, u32[]{:S(2)}, u32[]{:S(2)}) collective-permute-start(f32[640,128]{1,0:T(8,128)} %get-tuple-element.17), channel_id=1, source_target_pairs={{4,0},{5,1},{8,4},{9,5},{12,8},{13,9},{16,12},{17,13},{20,16},{21,... | collective-permute-start | bytes 983048 | tf_op jit(solution)/shard_map/ppermute | solution.py:474
  46.4 10.3 %collective-permute-start.2 = (bf16[736,128]{1,0:T(8,128)(2,1)}, bf16[736,128]{1,0:T(8,128)(2,1)S(1)}, u32[]{:S(2)}, u32[]{:S(2)}) collective-permute-start(bf16[736,128]{1,0:T(8,128)(2,1)} %concatenate.29), channel_id=1, source_target_pairs={{0,4},{1,5},{4,8},{5,9},{8,12},{9,13},{12,16},{13,17},{16,20},{17,... | collective-permute-start | bytes 565256 | tf_op jit(solution)/shard_map/ppermute | solution.py:471
  56.7 1.1 %copy-start.3 = (f32[1280,128]{1,0:T(8,128)S(1)}, f32[1280,128]{1,0:T(8,128)}, u32[]{:S(2)}) copy-start(f32[1280,128]{1,0:T(8,128)} %copy-done.2) | copy-start | bytes 1966084
  65.2 3.5 %collective-permute-start.4 = (f32[2,20,16,128]{3,2,1,0:T(8,128)S(1)}, f32[2,20,16,128]{3,2,1,0:T(8,128)S(1)}, u32[]{:S(2)}, u32[]{:S(2)}) collective-permute-start(f32[2,20,16,128]{3,2,1,0:T(8,128)S(1)} %dynamic-slice_bitcast_fusion), channel_id=1, source_target_pairs={{0,1},{1,0},{2,3},{3,2},{4,5},{5,4},{6,7},{7,6},{8,9},{9,8},{10,11... | collective-permute-start | bytes 983048 | tf_op jit(solution)/shard_map/ppermute | solution.py:492
  68.8 15.1 %collective-permute-start.5 = (f32[20,16,128]{2,1,0:T(8,128)S(1)}, f32[20,16,128]{2,1,0:T(8,128)S(1)}, u32[]{:S(2)}, u32[]{:S(2)}) collective-permute-start(f32[20,16,128]{2,1,0:T(8,128)S(1)} %dynamic-slice_bitcast_fusion.1), channel_id=1, source_target_pairs={{0,2},{2,0},{1,3},{3,1},{4,6},{6,4},{5,7},{7,5},{8,10},{10,8},{9,1... | collective-permute-start | bytes 491528 | tf_op jit(solution)/shard_map/ppermute | solution.py:495

commit v2 on v1

v2 whole, which is shorter than its diff:
```python
import jax
import jax.numpy as jnp
from jax import lax
from jax.experimental import pallas as pl
from jax.experimental.pallas import tpu as pltpu
from jax.sharding import PartitionSpec as P

SPAN = 17
RIM = 8
TAPS = SPAN * SPAN
ROWS = 4
CLAT = 16
LON = 128
WIN = ROWS + 2 * RIM
RING = CLAT + RIM
GROUP = 20
MEMBERS = 80
DEPTH = 88
CELLS = GROUP * CLAT
EDGES = 64
TAPE = 24
PART = CELLS + 2 * EDGES
HALO = 3 * LON
MAIN = WIN * LON
LATROWS = MEMBERS * RIM + MEMBERS + RIM + 8
TAPE_ROWS = 1184
F32 = jnp.float32
BF16 = jnp.bfloat16
SMEM = pltpu.SMEM
VMEM = pltpu.VMEM
SHARE = 1.0 / (MEMBERS - 1)


def lanes(shape):
    return lax.broadcasted_iota(jnp.int32, shape, len(shape) - 1)


def rows_of(shape):
    return lax.broadcasted_iota(jnp.int32, shape, len(shape) - 2)


def shape(*dims, dtype=F32):
    return jax.ShapeDtypeStruct(dims, dtype)


def call(kernel, out_shape, scratch, *args, spaces=None, limit=16, flops=0):
    if spaces is None:
        spaces = [SMEM] + [VMEM] * (len(args) - 1)
    return pl.pallas_call(
        kernel,
        out_shape=out_shape,
        in_specs=[pl.BlockSpec(memory_space=space) for space in spaces],
        out_specs=jax.tree.map(lambda _: pl.BlockSpec(memory_space=VMEM), out_shape),
        scratch_shapes=scratch,
        compiler_params=pltpu.CompilerParams(vmem_limit_bytes=limit * 2**20),
        cost_estimate=pl.CostEstimate(flops=flops, bytes_accessed=2**20, transcendentals=0),
    )(*args)


def edges_kernel(
    index_ref, own_ref, taper_ref, first_ref, second_ref, wide, fields, cells
):
    for tap in range(TAPS):
        wide[tap * ROWS : tap * ROWS + ROWS] = taper_ref[tap].astype(F32)
    wide[TAPS * ROWS :] = jnp.zeros((TAPE_ROWS - TAPS * ROWS, LON), F32)
    own = own_ref[...].astype(F32)
    fields[...] = own[CELLS:]
    cells[0 : CELLS + 2 * CLAT] = own
    cells[CELLS + 2 * CLAT :] = jnp.zeros((2 * CLAT, LON), F32)
    lane = lanes((TAPE, LON))
    left = jnp.zeros((TAPE, LON), F32)
    right = jnp.zeros((TAPE, LON), F32)
    for lat in range(CLAT):
        part = cells[pl.ds(lat, TAPE, stride=CLAT), :]
        mine = lane // RIM == lat
        left = jnp.where(mine, pltpu.roll(part, RIM * lat, 1), left)
        right = jnp.where(mine, pltpu.roll(part, (RIM * lat + RIM) % LON, 1), right)
    left_rows = [left]
    right_rows = [right]
    lane = lanes((8, LON))
    row = rows_of((8, LON))
    for block in range(5):
        left = jnp.zeros((8, LON), F32)
        right = jnp.zeros((8, LON), F32)
        for sub in range(4):
            a = block * 4 + sub
            if a >= SPAN:
                continue
            for i in range(ROWS):
                to = sub * 32 + i * RIM
                mine = lane // RIM == to // RIM
                part = wide[pl.ds(a * SPAN * ROWS + i, 8, stride=ROWS), :]
                left = jnp.where(mine, pltpu.roll(part, to, 1), left)
                part = wide[pl.ds((a * SPAN + 9) * ROWS + i, 8, stride=ROWS), :]
                right = jnp.where(mine, pltpu.roll(part, (to + RIM) % LON, 1), right)
        for bit in (1, 2, 4):
            moved = pltpu.roll(left, bit, 0)
            moved = jnp.where(row >= bit, moved, 0.0)
            left = jnp.where((lane & bit) != 0, moved, left)
            moved = pltpu.roll(right, 8 - bit, 0)
            moved = jnp.where(row < 8 - bit, moved, 0.0)
            right = jnp.where(((7 - lane) & bit) != 0, moved, right)
        left_rows.append(left)
        right_rows.append(right)
    left = jnp.concatenate(left_rows, 0)
    right = jnp.concatenate(right_rows, 0)
    odd = index_ref[3] > 0
    first_ref[...] = jnp.where(odd, right, left).astype(BF16)
    second_ref[...] = jnp.where(odd, left, right).astype(BF16)


def edge_messages(index, own, taper):
    return call(
        edges_kernel,
        (
            shape(EDGES, LON, dtype=BF16),
            shape(EDGES, LON, dtype=BF16),
            shape(TAPE_ROWS, LON),
            shape(2 * CLAT, LON),
        ),
        [VMEM(((GROUP + 4) * CLAT, LON), F32)],
        index,
        own,
        taper,
    )


def message_kernel(index_ref, own_ref, first_ref, second_ref, out_ref):
    out_ref[0:CELLS] = own_ref[0:CELLS]
    odd = index_ref[3]
    east = pl.multiple_of(CELLS + (1 - odd) * EDGES, EDGES)
    west = pl.multiple_of(CELLS + odd * EDGES, EDGES)
    out_ref[pl.ds(east, EDGES)] = first_ref[...]
    out_ref[pl.ds(west, EDGES)] = second_ref[...]


def ring_row(mem, j):
    lat = ROWS * mem - RIM + j
    return jnp.where(lat < 0, lat + RING, lat)


def halo_row(side, ring):
    inside = side * LON + RIM * ring
    outside = 2 * LON + side * (LON // 2) + RIM * (ring - CLAT)
    return jnp.where(ring < CLAT, inside, outside)


def bands_kernel(index_ref, wide, band_ref, rim_ref, narrow):
    mem = index_ref[0]
    narrow[...] = jnp.zeros(narrow.shape, F32)
    for i in range(ROWS):
        for j in range(WIN):
            if j < i or j > i + SPAN - 1:
                band_ref[j * LON : (j + 1) * LON, i * LON : (i + 1) * LON] = jnp.zeros(
                    (LON, LON), BF16
                )
    lane = lanes((24, LON))
    row = rows_of((24, LON))
    group = lanes((8, LON)) // 8
    zero = jnp.zeros((8, LON), F32)

    @pl.loop(0, SPAN)
    def _(a):
        for i in range(ROWS):
            taps = wide[pl.ds(a * SPAN * ROWS + i, 24, stride=ROWS), :]
            taps = jnp.where(row < SPAN, taps, 0.0)
            for bit in (1, 2, 4):
                taps = jnp.where((lane & bit) != 0, pltpu.roll(taps, bit, 0), taps)
            low, mid, high = taps[0:8], taps[8:16], taps[16:24]
            parts = []
            for block in range(CLAT):
                part = jnp.where(group == block, mid, zero)
                if block < 15:
                    part = jnp.where(group == block + 1, low, part)
                if block > 0:
                    part = jnp.where(group == block - 1, high, part)
                parts.append(part)
            band_ref[pl.ds(pl.multiple_of((a + i) * LON, LON), LON), i * LON : (i + 1) * LON] = (
                jnp.concatenate(parts, 0).astype(BF16)
            )
            ring = ring_row(mem, a + i)
            east = pl.multiple_of(halo_row(0, ring), 8)
            west = pl.multiple_of(halo_row(1, ring), 8)
            narrow[pl.ds(east, 8), i * LON : (i + 1) * LON] = jnp.where(group == 15, high, zero)
            narrow[pl.ds(west, 8), i * LON : (i + 1) * LON] = jnp.where(group == 0, low, zero)

    rim_ref[...] = narrow[...].astype(BF16)


def bands(index, wide):
    return call(
        bands_kernel,
        (shape(MAIN, ROWS * LON, dtype=BF16), shape(HALO, ROWS * LON, dtype=BF16)),
        [VMEM((HALO, ROWS * LON), F32)],
        index,
        wide,
    )


def split(value):
    high = value.astype(BF16)
    return high, (value - high.astype(F32)).astype(BF16)


def gathered_rows(wide, start, stride):
    parts = [wide[pl.ds(g * PART + start, GROUP, stride=stride), :] for g in range(4)]
    return jnp.concatenate(parts, 0)


def halo_cells(index_ref, wide, side):
    flip = index_ref[1 + side]
    parts = []
    for g in range(4):
        part = jnp.where(flip > 0, (g + 2) % 4, g)
        at = pl.multiple_of(part * PART + CELLS + side * EDGES, 8)
        parts.append(wide[pl.ds(at, GROUP), :])
    return jnp.concatenate(parts, 0)


def halo_field(wide, side, which):
    at = CELLS + side * EDGES + 16
    return wide[at : at + 8][4 + which : 5 + which]


def lat_kernel(index_ref, x_ref, fields, out_ref, wide, rows):
    mem = index_ref[0]
    wide[...] = x_ref[...].astype(F32)
    first = jnp.where(mem < 2, RIM, 0)
    for m in range(MEMBERS):
        at = pl.multiple_of((m // GROUP) * PART + (m % GROUP) * CLAT + first, 8)
        rows[m * RIM : m * RIM + RIM] = wide[pl.ds(at, RIM), :]
    lane = lanes((MEMBERS + 8, LON))
    pad = jnp.zeros((7, LON), F32)
    sides = []
    for side in range(2):
        cells = [halo_cells(index_ref, wide, side), halo_field(wide, side, 0), pad]
        sides.append(jnp.concatenate(cells, 0))
    half = LON // 2
    low = jnp.where(lane < half, sides[0], pltpu.roll(sides[1], half, 1))
    high = jnp.where(lane < half, pltpu.roll(sides[0], half, 1), sides[1])
    both = jnp.where(mem < 2, high, low)
    base = MEMBERS * RIM
    rows[base : base + MEMBERS] = both[:MEMBERS]
    rows[base + MEMBERS : base + MEMBERS + RIM] = fields[pl.ds(pl.multiple_of(first, 8), RIM), :]
    rows[base + MEMBERS + RIM :] = both[MEMBERS:]
    out_ref[...] = rows[...].astype(BF16)


def lat_message(index, gathered, fields):
    return call(
        lat_kernel,
        shape(LATROWS, LON, dtype=BF16),
        [VMEM((4 * PART, LON), F32), VMEM((LATROWS, LON), F32)],
        index,
        gathered,
        fields,
    )


def rim_steps(mem):
    first = jnp.where(mem < 2, 0, jnp.where(mem == 2, 4, 3))
    return first, jnp.where((mem == 0) | (mem == 3), 2, 1)


def block_steps(mem):
    first = jnp.where(mem == 0, 2, jnp.where(mem == 1, 1, 0))
    return first, jnp.where((mem == 0) | (mem == 3), 3, 4)


def pushes(scaled, corner, band_ref, step):
    at = pl.ds(pl.multiple_of(step * STEP * LON, LON), STEP * LON)
    both = lax.dot_general(
        scaled[:, : ROWS * LON],
        band_ref[at, :],
        (((1,), (1,)), ((), ())),
        preferred_element_type=F32,
    )
    both = both + lax.dot_general(
        scaled[:, ROWS * LON :],
        corner[at, :],
        (((1,), (1,)), ((), ())),
        preferred_element_type=F32,
    )
    return both[:MEMBERS] + both[MEMBERS:]


def rim_push_kernel(index_ref, x_ref, fields, band_ref, rim_ref, scaled, corner, wide):
    mem = index_ref[0]
    wide[...] = x_ref[...].astype(F32)
    for i in range(ROWS):
        own = gathered_rows(wide, ROWS * mem + i, CLAT) * fields[pl.ds(CLAT + ROWS * mem + i, 1), :]
        high, low = split(own)
        scaled[0:MEMBERS, i * LON : (i + 1) * LON] = high
        scaled[MEMBERS:, i * LON : (i + 1) * LON] = low
    lane = lanes((MEMBERS, LON))
    east = halo_cells(index_ref, wide, 0) * halo_field(wide, 0, 1)
    west = halo_cells(index_ref, wide, 1) * halo_field(wide, 1, 1)
    east = pltpu.roll(east, (LON - 32 * mem) % LON, 1)
    west = pltpu.roll(west, (LON + 32 - 32 * mem) % LON, 1)
    high, low = split(jnp.where(lane < 32, east, jnp.where(lane < 64, west, 0.0)))
    scaled[0:MEMBERS, ROWS * LON :] = high
    scaled[MEMBERS:, ROWS * LON :] = low
    lane = lanes((8, LON))
    corner[...] = jnp.zeros(corner.shape, BF16)
    tiles = []
    for side in range(2):
        part = jnp.where(index_ref[1 + side] > 0, (mem + 2) % 4, mem)
        at = pl.multiple_of(part * PART + CELLS + side * EDGES + TAPE, 8)
        packed = wide[pl.ds(at, EDGES - TAPE), :]
        tiles.append(
            [
                pltpu.roll(
                    packed[8 * (a // 4) : 8 * (a // 4) + 8],
                    (LON + 32 * side - 32 * (a % 4)) % LON,
                    1,
                )
                for a in range(SPAN)
            ]
        )
    zero = jnp.zeros((8, LON), F32)
    for j in range(WIN):
        edge = []
        for side in range(2):
            tile = zero
            for i in range(ROWS):
                if 0 <= j - i < SPAN:
                    tile = jnp.where(lane // RIM == 4 * side + i, tiles[side][j - i], tile)
            edge.append(tile)
        corner[j * LON : j * LON + 16] = jnp.concatenate([edge[1], zero], 0).astype(BF16)
        corner[j * LON + 112 : j * LON + 128] = jnp.concatenate([zero, edge[0]], 0).astype(BF16)
    zeros = jnp.zeros((MEMBERS, LON), F32)

    @pl.when((mem == 1) | (mem == 2))
    def _():
        first = jnp.where(mem == 1, 0, ROWS)
        for k in range(ROWS):
            rim_ref[pl.ds(first + k, MEMBERS, stride=RIM), :] = zeros

    first, steps = rim_steps(mem)

    @pl.loop(first, first + steps)
    def _(step):
        total = pushes(scaled, corner, band_ref, step)
        for k in range(STEP):
            row = ring_row(mem, step * STEP + k) - CLAT
            rim_ref[pl.ds(row, MEMBERS, stride=RIM), :] = total[:, k * LON : (k + 1) * LON]


def block_push_kernel(index_ref, scaled, corner, band_ref, out_ref):
    mem = index_ref[0]
    zeros = jnp.zeros((MEMBERS, LON), F32)

    @pl.when((mem == 0) | (mem == 3))
    def _():
        first = jnp.where(mem == 0, CLAT - ROWS, 0)
        for k in range(ROWS):
            out_ref[pl.ds(first + k, MEMBERS, stride=CLAT), :] = zeros

    first, steps = block_steps(mem)

    @pl.loop(first, first + steps)
    def _(step):
        total = pushes(scaled, corner, band_ref, step)
        for k in range(STEP):
            row = ring_row(mem, step * STEP + k)
            out_ref[pl.ds(row, MEMBERS, stride=CLAT), :] = total[:, k * LON : (k + 1) * LON]


STEP = 4


def rim_push(index, gathered, fields, band):
    return call(
        rim_push_kernel,
        (
            shape(MEMBERS * RIM, LON),
            shape(2 * MEMBERS, (ROWS + 1) * LON, dtype=BF16),
            shape(MAIN, LON, dtype=BF16),
        ),
        [VMEM((4 * PART, LON), F32)],
        index,
        gathered,
        fields,
        band,
        flops=4 * 10**9,
    )


def block_push(index, scaled, corner, band):
    return call(
        block_push_kernel,
        shape(MEMBERS * CLAT, LON),
        [],
        index,
        scaled,
        corner,
        band,
        flops=4 * 10**9,
    )


def first_kernel(
    index_ref, x_ref, lat_ref, fields, band_ref, rim_ref, push_ref,
    out_ref, window, halos,
    wide, wide_lat, scaled,
):
    mem = index_ref[0]
    wide[...] = x_ref[...].astype(F32)
    wide_lat[...] = lat_ref[...].astype(F32)
    base = MEMBERS * RIM
    pad = jnp.zeros((DEPTH - MEMBERS - 1, LON), F32)
    for j in range(WIN):
        ring = ring_row(mem, j)

        @pl.when(ring < CLAT)
        def _():
            window[j, 0:MEMBERS] = gathered_rows(wide, ring, CLAT)
            window[j, MEMBERS:] = jnp.concatenate([fields[pl.ds(ring, 1), :], pad], 0)

        @pl.when(ring >= CLAT)
        def _():
            window[j, 0:MEMBERS] = wide_lat[pl.ds(ring - CLAT, MEMBERS, stride=RIM), :]
            row = wide_lat[pl.ds(base + MEMBERS + ring - CLAT, 1), :]
            window[j, MEMBERS:] = jnp.concatenate([row, pad], 0)

    for side in range(2):
        halos[side, 0:MEMBERS] = halo_cells(index_ref, wide, side)
        halos[side, MEMBERS:] = jnp.concatenate([halo_field(wide, side, 0), pad], 0)
    halos[2, 0:MEMBERS] = wide_lat[base : base + MEMBERS]
    last = wide_lat[base + MEMBERS + RIM : base + MEMBERS + RIM + 1]
    halos[2, MEMBERS:] = jnp.concatenate([last, pad], 0)

    def put(at, cells):
        high, low = split(cells[0:MEMBERS] * cells[MEMBERS : MEMBERS + 1])
        scaled[0:MEMBERS, at : at + LON] = high
        scaled[MEMBERS:, at : at + LON] = low

    for j in range(WIN):
        put(j * LON, window[j])
    for k in range(3):
        put(MAIN + k * LON, halos[k])
    both = jnp.dot(scaled[:, :MAIN], band_ref[...], preferred_element_type=F32)
    both = both + jnp.dot(scaled[:, MAIN:], rim_ref[...], preferred_element_type=F32)
    total = both[:MEMBERS] + both[MEMBERS:]
    v_rows = fields[0:CLAT] * SHARE
    for m in range(MEMBERS):
        at = m * CLAT
        out_ref[at : at + CLAT] = push_ref[at : at + CLAT] * v_rows
    for i in range(ROWS):
        at = pl.ds(ROWS * mem + i, MEMBERS, stride=CLAT)
        c_row = fields[pl.ds(CLAT + ROWS * mem + i, 1), :] * SHARE
        out_ref[at, :] = out_ref[at, :] + total[:, i * LON : (i + 1) * LON] * c_row


def first_sum(index, gathered, lat_halo, fields, band, rim, pushed):
    return call(
        first_kernel,
        (shape(MEMBERS * CLAT, LON), shape(WIN, DEPTH, LON), shape(3, DEPTH, LON)),
        [
            VMEM((4 * PART, LON), F32),
            VMEM((LATROWS, LON), F32),
            VMEM((2 * MEMBERS, MAIN + HALO), BF16),
        ],
        index,
        gathered,
        lat_halo,
        fields,
        band,
        rim,
        pushed,
        flops=4 * 10**9,
    )


def near_kernel(index_ref, part_ref, back_ref, fields, keep_ref, send_ref):
    mem = index_ref[0]
    core = mem % 2
    first = pl.multiple_of(jnp.where(mem < 2, RIM, 0), 8)
    v_rows = fields[pl.ds(first, RIM), :] * SHARE
    for half in range(2):
        for take, target in ((core, keep_ref), (1 - core, send_ref)):
            at = pl.multiple_of((2 * half + take) * CELLS, 8)
            target[half * CELLS : (half + 1) * CELLS] = part_ref[pl.ds(at, CELLS), :]
            at = pl.multiple_of((2 * half + take) * GROUP * RIM, 8)
            more = back_ref[pl.ds(at, GROUP * RIM), :]
            for m in range(GROUP):
                to = pl.ds(pl.multiple_of(half * CELLS + m * CLAT + first, 8), RIM)
                target[to, :] = target[to, :] + more[m * RIM : (m + 1) * RIM] * v_rows


def near_parts(index, partial, back, fields):
    return call(
        near_kernel,
        (shape(2 * CELLS, LON), shape(2 * CELLS, LON)),
        [],
        index,
        partial,
        back,
        fields,
    )


def far_kernel(index_ref, keep_ref, more_ref, mine_ref, send_ref):
    far = index_ref[0] // 2
    at = pl.ds(pl.multiple_of(far * CELLS, 8), CELLS)
    mine_ref[...] = keep_ref[at, :] + more_ref[at, :]
    at = pl.ds(pl.multiple_of((1 - far) * CELLS, 8), CELLS)
    send = keep_ref[at, :] + more_ref[at, :]
    largest = jnp.full((16, LON), jnp.max(jnp.abs(send)), F32)
    power = jnp.clip(jnp.round(jnp.log2(largest)) - 8.0, -120.0, 100.0)
    send_ref[0:CELLS] = send * jnp.exp2(-power)[0:1]
    send_ref[CELLS:] = power


def far_parts(index, keep, more):
    return call(far_kernel, (shape(CELLS, LON), shape(CELLS + 16, LON)), [], index, keep, more)


def taper_part(index_ref, window, halos, fields, flat, own, turned, product, shifted, taps_of):
    mem = index_ref[0]
    used = range(taps_of[0], taps_of[-1] + ROWS)
    for j in used:
        turned[j * LON : (j + 1) * LON, :] = window[j].T.astype(BF16)
    for k in range(3):
        turned[MAIN + k * LON : MAIN + (k + 1) * LON, :] = halos[k].T.astype(BF16)
    keep = rows_of((DEPTH, LON)) < MEMBERS
    for i in range(ROWS):
        own[:, i * LON : (i + 1) * LON] = jnp.where(keep, window[RIM + i], 0.0).astype(BF16)
    own[:, ROWS * LON :] = jnp.where(rows_of((DEPTH, LON)) == MEMBERS, 1.0, 0.0).astype(BF16)
    for j in [*used, WIN, WIN + 1, WIN + 2]:
        at = j * LON
        product[at : at + LON] = jnp.dot(turned[at : at + LON], own[...], preferred_element_type=F32)
    lane = lanes((8, LON))
    wide_lane = lanes((24, LON))

    def diagonals(j, column):
        ring = ring_row(mem, j)
        east = pl.multiple_of(MAIN + halo_row(0, ring), 8)
        west = pl.multiple_of(MAIN + halo_row(1, ring), 8)
        cells = [product[pl.ds(west, 8), column : column + LON]]
        for block in range(CLAT):
            at = pl.multiple_of(j * LON + 8 * block, 8)
            cells.append(product[pl.ds(at, 8), column : column + LON])
        cells.append(product[pl.ds(east, 8), column : column + LON])
        for bit in (8, 4, 2, 1):
            take = (lane & (8 * bit)) != 0
            cells = [jnp.where(take, cells[s + bit], cells[s]) for s in range(len(cells) - bit)]
        taps = jnp.concatenate(cells, 0)
        for bit in (1, 2, 4):
            taps = jnp.where((wide_lane & bit) != 0, pltpu.roll(taps, 24 - bit, 0), taps)
        return taps

    @pl.loop(used[0], used[-1] + 1)
    def _(j):
        shifted[j] = diagonals(j, ROWS * LON)

    @pl.loop(taps_of[0], taps_of[-1] + 1)
    def _(a):
        for i in range(ROWS):
            c_row = fields[pl.ds(CLAT + ROWS * mem + i, 1), :] * SHARE
            taps = diagonals(a + i, i * LON) * shifted[a + i] * c_row
            flat[pl.ds(a * SPAN * ROWS + i, SPAN, stride=ROWS), :] = taps[0:SPAN]


EARLY = 9


def early_kernel(index_ref, window, halos, fields, flat, *scratch):
    taper_part(index_ref, window, halos, fields, flat, *scratch, range(EARLY))


def late_kernel(index_ref, window, halos, fields, early, taper_ref, flat, *scratch):
    taper_part(index_ref, window, halos, fields, flat, *scratch, range(EARLY, SPAN))
    for tap in range(TAPS):
        source = early if tap < EARLY * SPAN else flat
        taper_ref[tap] = source[tap * ROWS : tap * ROWS + ROWS]


def taper_scratch():
    return [
        VMEM((DEPTH, (ROWS + 1) * LON), BF16),
        VMEM((MAIN + HALO, DEPTH), BF16),
        VMEM((MAIN + HALO, (ROWS + 1) * LON), F32),
        VMEM((WIN, 24, LON), F32),
    ]


def early_taps(index, window, halos, fields):
    return call(
        early_kernel, shape(EARLY * SPAN * ROWS, LON), taper_scratch(),
        index, window, halos, fields, limit=24, flops=3 * 10**9,
    )


def late_taps(index, window, halos, fields, early):
    return call(
        late_kernel, shape(TAPS, ROWS, LON), [VMEM((TAPS * ROWS, LON), F32), *taper_scratch()],
        index, window, halos, fields, early, limit=24, flops=3 * 10**9,
    )


def body(anomalies, vector, cotangent, taper):
    mem = lax.axis_index("mem").astype(jnp.int32)
    strip = lax.axis_index("lon")
    blocks = lax.axis_size("lat")
    strips = lax.axis_size("lon")
    index = jnp.stack(
        [
            mem,
            (strip == strips - 1).astype(jnp.int32),
            (strip == 0).astype(jnp.int32),
            (strip % 2).astype(jnp.int32),
        ]
    )
    own = jnp.concatenate([anomalies.reshape(CELLS, LON), vector, cotangent], 0)
    first, second, wide, fields = edge_messages(index, own, taper)
    swaps = ([], [])
    for s in range(strips):
        for m in range(4):
            here = 4 * s + m
            there = here + 4 if s < strips - 1 else (m + 2) % 4
            swaps[1 - s % 2].extend([(here, there), (there, here)])
    first = lax.ppermute(first, ("lon", "mem"), swaps[0])
    second = lax.ppermute(second, ("lon", "mem"), swaps[1])
    band, rim = bands(index, wide)
    first, second, band, rim = lax.optimization_barrier((first, second, band, rim))
    message = call(
        message_kernel, shape(PART, LON, dtype=BF16), [], index, own, first, second
    )
    gathered = lax.all_gather(message, "mem", axis=0, tiled=True)

    down = [(4 * z + m, 4 * z + 4 + m) for z in range(blocks - 1) for m in (0, 1)]
    up = [(4 * z + 4 + m, 4 * z + m) for z in range(blocks - 1) for m in (2, 3)]
    message = lat_message(index, gathered, fields)
    message, gathered = lax.optimization_barrier((message, gathered))
    lat_halo = lax.ppermute(message, ("lat", "mem"), down + up)
    pushed_out, scaled, corner = rim_push(index, gathered, fields, band)
    back = lax.ppermute(pushed_out, ("lat", "mem"), [(b, a) for a, b in down + up])
    pushed = block_push(index, scaled, corner, band)
    partial, window, halos = first_sum(index, gathered, lat_halo, fields, band, rim, pushed)
    early = early_taps(index, window, halos, fields)
    back, early = lax.optimization_barrier((back, early))
    keep, send = near_parts(index, partial, back, fields)
    more = lax.ppermute(send, "mem", [(0, 1), (1, 0), (2, 3), (3, 2)])
    mine, send = far_parts(index, keep, more)
    half = lax.ppermute(send.astype(jnp.float16), "mem", [(0, 2), (2, 0), (1, 3), (3, 1)])
    mine, early = lax.optimization_barrier((mine, early))
    grad_taper = late_taps(index, window, halos, fields, early)
    more = half.astype(F32)
    grad_anomalies = mine + more[:CELLS] * jnp.exp2(more[CELLS : CELLS + 1])
    grad_anomalies = grad_anomalies.reshape(GROUP, CLAT, LON)
    return grad_taper, grad_anomalies


def solution(mesh):
    placed = (
        P("mem", "lat", "lon"),
        P("lat", "lon"),
        P("lat", "lon"),
        P(None, ("lat", "mem"), "lon"),
    )
    return jax.shard_map(
        body,
        mesh=mesh,
        in_specs=placed,
        out_specs=(P(None, ("lat", "mem"), "lon"), P("mem", "lat", "lon")),
        check_vma=False,
    )
```

time: 85.3 us -> 65.4 us (0.77)
  the two profiles are of different devices: /device:TPU:192 before, /device:TPU:201 now
where the time goes in v2:
time: 65.4 us; the launch traced here: 65.1 us
  starting transfers between devices  19.2 us (29%)
  Pallas kernels  16.9 us (26%)
  blocking collectives  15.5 us (24%)
  waiting for transfers between devices  9.85 us (15%)
  other arithmetic  1.73 us (3%)
  local copies, waits for them, and re-layouts  0.96 us (1%)
  between operations  0.8 us (1%)
    pallas_call x11, Pallas kernels, call(): pl.pallas_call(kernel, out_shape=out_shape, in_specs=[pl.BlockSpec(memory...  16.9 us
    all_gather x1, blocking collectives, body(): gathered = lax.all_gather(message, 'mem', axis=0, tiled=True)  15.5 us
    ppermute x1, waiting for transfers between devices, body(): lax.ppermute(send.astype(jnp.float16), 'mem', [(0, 2), (2, 0), (1, 3), (3...  5.36 us
    ppermute x1, starting transfers between devices, body(): lat_halo = lax.ppermute(message, ('lat', 'mem'), down + up)  5.21 us
    ppermute x1, starting transfers between devices, body(): first = lax.ppermute(first, ('lon', 'mem'), swaps[0])  4.27 us
    ppermute x1, starting transfers between devices, body(): more = lax.ppermute(send, 'mem', [(0, 1), (1, 0), (2, 3), (3, 2)])  3.61 us
    ppermute x1, waiting for transfers between devices, body(): lax.ppermute(pushed_out, ('lat', 'mem'), [(b, a) for a, b in down + up])  2.52 us
    ppermute x1, starting transfers between devices, body(): lax.ppermute(send.astype(jnp.float16), 'mem', [(0, 2), (2, 0), (1, 3), (3...  2.27 us
  transfers between devices with their start and end apart: 6, of which 4 were waited for; matrix products, arithmetic and copies ran while one was open for 0% of the time, Pallas kernels for 21%

profile of v2, /device:TPU:201, one launch (start us, length us, event | category | flops | bytes accessed | tf_op | source)
XLA Modules:
  0.0 65.1 jit_solution(3431090617589500642)
XLA Ops:
  0.6 0.9 %pad_maximum_fusion.own_ref = bf16[352,128]{1,0:T(8,128)(2,1)S(1)} fusion(bf16[16,128]{1,0:T(8,128)(2,1)} %param.6, bf16[16,128]{1,0:T(8,128)(2,1)} %param.5, bf16[320,128]{1,0:T(8,128)(2,1)} %bitcast.9), kind=kLoop, calls=%fused_computation.2 | loop fusion | flops 270336 | bytes 180224 | tf_op jit(solution)/shard_map/concatenate | solution.py:615
  1.6 0.1 pad_add_fusion.index_ref
  1.7 0.0 copy-start
  1.7 1.0 %copy-done = bf16[289,4,128]{2,1,0:T(4,128)(2,1)S(1)} copy-done((bf16[289,4,128]{2,1,0:T(4,128)(2,1)S(1)}, bf16[289,4,128]{2,1,0:T(4,128)(2,1)}, u32[]{:S(2)}) %copy-start) | copy-done | bytes 295960
  2.6 0.8 %shard_map.59 = (bf16[64,128]{1,0:T(8,128)(2,1)S(1)}, bf16[64,128]{1,0:T(8,128)(2,1)S(1)}, f32[1184,128]{1,0:T(8,128)S(1)}, f32[32,128]{1,0:T(8,128)S(1)}) custom-call(s32[4]{0:T(128)S(1)} %pad_add_fusion.index_ref, bf16[352,128]{1,0:T(8,128)(2,1)S(1)} %pad_maximum_fusion.own_ref, bf16[289,4,128]{2,1,0:T(4,128)(2,1)S(1)} %copy-done), custom_call_target="tpu_custom_call" | custom-call | bytes 1048576 | tf_op jit(solution)/shard_map/pallas_call | solution.py:49
  3.4 4.3 %collective-permute-start = (bf16[64,128]{1,0:T(8,128)(2,1)S(1)}, bf16[64,128]{1,0:T(8,128)(2,1)S(1)}, u32[]{:S(2)}, u32[]{:S(2)}) collective-permute-start(bf16[64,128]{1,0:T(8,128)(2,1)S(1)} %get-tuple-element.28), channel_id=1, source_target_pairs={{32,64},{64,32},{33,65},{65,33},{34,66},{66,34},{35,67},{67,35},{9... | collective-permute-start | bytes 49160 | tf_op jit(solution)/shard_map/ppermute | solution.py:623
  7.7 2.0 %collective-permute-start.1 = (bf16[64,128]{1,0:T(8,128)(2,1)S(1)}, bf16[64,128]{1,0:T(8,128)(2,1)S(1)}, u32[]{:S(2)}, u32[]{:S(2)}) collective-permute-start(bf16[64,128]{1,0:T(8,128)(2,1)S(1)} %get-tuple-element.29), channel_id=1, source_target_pairs={{0,32},{32,0},{1,33},{33,1},{2,34},{34,2},{3,35},{35,3},{64,96},{9... | collective-permute-start | bytes 49160 | tf_op jit(solution)/shard_map/ppermute | solution.py:624
  9.7 1.8 %shard_map.60 = (bf16[2560,512]{1,0:T(8,128)(2,1)S(1)}, bf16[384,512]{1,0:T(8,128)(2,1)S(1)}) custom-call(s32[4]{0:T(128)S(1)} %pad_add_fusion.index_ref, f32[1184,128]{1,0:T(8,128)S(1)} %get-tuple-element.30.wide), custom_call_target="tpu_custom_call" | custom-call | bytes 1048576 | tf_op jit(solution)/shard_map/pallas_call | solution.py:49
  11.5 0.0 collective-permute-done.first_ref
  11.5 0.7 %collective-permute-done.1.second_ref = bf16[64,128]{1,0:T(8,128)(2,1)S(1)} collective-permute-done((bf16[64,128]{1,0:T(8,128)(2,1)S(1)}, bf16[64,128]{1,0:T(8,128)(2,1)S(1)}, u32[]{:S(2)}, u32[]{:S(2)}) %collective-permute-start.1) | collective-permute-done | bytes 16416 | tf_op jit(solution)/shard_map/ppermute | solution.py:624
  12.2 0.5 shard_map.61
  12.8 15.5 %all_gather.3.x_ref = bf16[1792,128]{1,0:T(8,128)(2,1)S(1)} all-gather(bf16[448,128]{1,0:T(8,128)(2,1)S(1)} %shard_map.61), channel_id=1, replica_groups=mesh['lon'=16,'lat'=8,'mem'=4] {'mem'}, dimensions={0}, use_global_device_ids=true | all-gather | bytes 573440 | tf_op jit(solution)/shard_map/all_gather | solution.py:630
  28.3 0.7 shard_map.62
  29.0 5.2 %collective-permute-start.2 = (bf16[736,128]{1,0:T(8,128)(2,1)S(1)}, bf16[736,128]{1,0:T(8,128)(2,1)S(1)}, u32[]{:S(2)}, u32[]{:S(2)}) collective-permute-start(bf16[736,128]{1,0:T(8,128)(2,1)S(1)} %shard_map.62), channel_id=1, source_target_pairs={{0,4},{1,5},{4,8},{5,9},{8,12},{9,13},{12,16},{13,17},{16,20},{17,... | collective-permute-start | bytes 565256 | tf_op jit(solution)/shard_map/ppermute | solution.py:636
  34.2 1.3 %shard_map.63 = (f32[640,128]{1,0:T(8,128)S(1)}, bf16[160,640]{1,0:T(8,128)(2,1)S(1)}, bf16[2560,128]{1,0:T(8,128)(2,1)S(1)}) custom-call(s32[4]{0:T(128)S(1)} %pad_add_fusion.index_ref, bf16[1792,128]{1,0:T(8,128)(2,1)S(1)} %all_gather.3.x_ref, f32[32,128]{1,0:T(8,128)S(1)} %get-tuple-element.35.fields, bf16[2560,512]{1,0:T(8,128)(2,1)S(1)} %get-tuple-element.38.band_ref), custom_call_target="tpu_custom_call" | custom-call | flops 4000000000 | bytes 1048576 | tf_op jit(solution)/shard_map/pallas_call | solution.py:49
  35.5 1.9 %collective-permute-start.3 = (f32[640,128]{1,0:T(8,128)S(1)}, f32[640,128]{1,0:T(8,128)S(1)}, u32[]{:S(2)}, u32[]{:S(2)}) collective-permute-start(f32[640,128]{1,0:T(8,128)S(1)} %get-tuple-element.45), channel_id=1, source_target_pairs={{4,0},{5,1},{8,4},{9,5},{12,8},{13,9},{16,12},{17,13},{20,16},{21,... | collective-permute-start | bytes 983048 | tf_op jit(solution)/shard_map/ppermute | solution.py:638
  37.4 2.3 %shard_map.64.push_ref = f32[1280,128]{1,0:T(8,128)S(1)} custom-call(s32[4]{0:T(128)S(1)} %pad_add_fusion.index_ref, bf16[160,640]{1,0:T(8,128)(2,1)S(1)} %get-tuple-element.40.scaled, bf16[2560,128]{1,0:T(8,128)(2,1)S(1)} %get-tuple-element.41.corner, bf16[2560,512]{1,0:T(8,128)(2,1)S(1)} %get-tuple-element.38.band_ref), custom_call_target="tpu_custom_call" | custom-call | flops 4000000000 | bytes 1048576 | tf_op jit(solution)/shard_map/pallas_call | solution.py:49
  39.7 0.0 collective-permute-done.2.lat_ref
  39.7 2.0 %shard_map.65 = (f32[1280,128]{1,0:T(8,128)S(1)}, f32[20,88,128]{2,1,0:T(8,128)S(1)}, f32[3,88,128]{2,1,0:T(8,128)S(1)}) custom-call(s32[4]{0:T(128)S(1)} %pad_add_fusion.index_ref, bf16[1792,128]{1,0:T(8,128)(2,1)S(1)} %all_gather.3.x_ref, bf16[736,128]{1,0:T(8,128)(2,1)S(1)} %collective-permute-done.2.lat_ref, f32[32,128]{1,0:T(8,128)S(1)} %get-tuple-element.35.fields, ...), custom_call_target="tpu_custom_call" | custom-call | flops 4000000000 | bytes 1048576 | tf_op jit(solution)/shard_map/pallas_call | solution.py:49
  41.7 2.8 %shard_map.66.early = f32[612,128]{1,0:T(8,128)S(1)} custom-call(s32[4]{0:T(128)S(1)} %pad_add_fusion.index_ref, f32[20,88,128]{2,1,0:T(8,128)S(1)} %get-tuple-element.42.window, f32[3,88,128]{2,1,0:T(8,128)S(1)} %get-tuple-element.43.halos, f32[32,128]{1,0:T(8,128)S(1)} %get-tuple-element.35.fields), custom_call_target="tpu_custom_call" | custom-call | flops 3000000000 | bytes 1048576 | tf_op jit(solution)/shard_map/pallas_call | solution.py:49
  44.5 2.5 %collective-permute-done.3.back_ref = f32[640,128]{1,0:T(8,128)S(1)} collective-permute-done((f32[640,128]{1,0:T(8,128)S(1)}, f32[640,128]{1,0:T(8,128)S(1)}, u32[]{:S(2)}, u32[]{:S(2)}) %collective-permute-start.3) | collective-permute-done | bytes 327712 | tf_op jit(solution)/shard_map/ppermute | solution.py:638
  47.0 0.6 shard_map.67
  47.7 3.6 %collective-permute-start.4 = (f32[640,128]{1,0:T(8,128)S(1)}, f32[640,128]{1,0:T(8,128)S(1)}, u32[]{:S(2)}, u32[]{:S(2)}) collective-permute-start(f32[640,128]{1,0:T(8,128)S(1)} %get-tuple-element.48), channel_id=1, source_target_pairs={{0,1},{1,0},{2,3},{3,2},{4,5},{5,4},{6,7},{7,6},{8,9},{9,8},{10,11... | collective-permute-start | bytes 983048 | tf_op jit(solution)/shard_map/ppermute | solution.py:644
  51.3 1.2 %collective-permute-done.4.more_ref = f32[640,128]{1,0:T(8,128)S(1)} collective-permute-done((f32[640,128]{1,0:T(8,128)S(1)}, f32[640,128]{1,0:T(8,128)S(1)}, u32[]{:S(2)}, u32[]{:S(2)}) %collective-permute-start.4) | collective-permute-done | bytes 327712 | tf_op jit(solution)/shard_map/ppermute | solution.py:644
  52.5 0.7 %shard_map.68 = (f32[320,128]{1,0:T(8,128)S(1)}, f32[336,128]{1,0:T(8,128)S(1)}) custom-call(s32[4]{0:T(128)S(1)} %pad_add_fusion.index_ref, f32[640,128]{1,0:T(8,128)S(1)} %get-tuple-element.47.keep_ref, f32[640,128]{1,0:T(8,128)S(1)} %collective-permute-done.4.more_ref), custom_call_target="tpu_custom_call" | custom-call | bytes 1048576 | tf_op jit(solution)/shard_map/pallas_call | solution.py:49
  53.3 2.3 %collective-permute-start.5 = (f16[336,128]{1,0:T(8,128)(2,1)S(1)}, f16[336,128]{1,0:T(8,128)(2,1)S(1)}, u32[]{:S(2)}, u32[]{:S(2)}) collective-permute-start(f16[336,128]{1,0:T(8,128)(2,1)S(1)} %convert_element_type.8), channel_id=1, source_target_pairs={{0,2},{2,0},{1,3},{3,1},{4,6},{6,4},{5,7},{7,5},{8,10},{10,8},{9,1... | collective-permute-start | bytes 258056 | tf_op jit(solution)/shard_map/ppermute | solution.py:646
  55.6 3.5 %shard_map.69 = f32[289,4,128]{2,1,0:T(4,128)} custom-call(s32[4]{0:T(128)S(1)} %pad_add_fusion.index_ref, f32[20,88,128]{2,1,0:T(8,128)S(1)} %get-tuple-element.42.window, f32[3,88,128]{2,1,0:T(8,128)S(1)} %get-tuple-element.43.halos, f32[32,128]{1,0:T(8,128)S(1)} %get-tuple-element.35.fields, f32[612,128]{1,0:T(8,128)S(1)} %shard_map.66.early), custom_call_target="tpu_custom_call" | custom-call | flops 3000000000 | bytes 1048576 | tf_op jit(solution)/shard_map/pallas_call | solution.py:49
  59.0 5.4 %collective-permute-done.5 = f16[336,128]{1,0:T(8,128)(2,1)S(1)} collective-permute-done((f16[336,128]{1,0:T(8,128)(2,1)S(1)}, f16[336,128]{1,0:T(8,128)(2,1)S(1)}, u32[]{:S(2)}, u32[]{:S(2)}) %collective-permute-start.5) | collective-permute-done | bytes 86048 | tf_op jit(solution)/shard_map/ppermute | solution.py:646
  64.4 0.7 %fusion = f32[320,128]{1,0:T(8,128)} fusion(f32[320,128]{1,0:T(8,128)S(1)} %get-tuple-element.52, f32[336,128]{1,0:T(8,128)S(1)} %convert_element_type.9, f32[128]{0:T(128)S(1)} %fusion.2), kind=kLoop, calls=%fused_computation.1 | loop fusion | flops 81920 | bytes 492032 | tf_op jit(solution)/shard_map/add | solution.py:650
  (3 shorter events, 0.0 us)
Async XLA Ops:
  1.7 1.0 %copy-start = (bf16[289,4,128]{2,1,0:T(4,128)(2,1)S(1)}, bf16[289,4,128]{2,1,0:T(4,128)(2,1)}, u32[]{:S(2)}) copy-start(bf16[289,4,128]{2,1,0:T(4,128)(2,1)} %taper_ref.1) | copy-start | bytes 887812
  3.4 8.0 %collective-permute-start = (bf16[64,128]{1,0:T(8,128)(2,1)S(1)}, bf16[64,128]{1,0:T(8,128)(2,1)S(1)}, u32[]{:S(2)}, u32[]{:S(2)}) collective-permute-start(bf16[64,128]{1,0:T(8,128)(2,1)S(1)} %get-tuple-element.28), channel_id=1, source_target_pairs={{32,64},{64,32},{33,65},{65,33},{34,66},{66,34},{35,67},{67,35},{9... | collective-permute-start | bytes 49160 | tf_op jit(solution)/shard_map/ppermute | solution.py:623
  7.7 4.5 %collective-permute-start.1 = (bf16[64,128]{1,0:T(8,128)(2,1)S(1)}, bf16[64,128]{1,0:T(8,128)(2,1)S(1)}, u32[]{:S(2)}, u32[]{:S(2)}) collective-permute-start(bf16[64,128]{1,0:T(8,128)(2,1)S(1)} %get-tuple-element.29), channel_id=1, source_target_pairs={{0,32},{32,0},{1,33},{33,1},{2,34},{34,2},{3,35},{35,3},{64,96},{9... | collective-permute-start | bytes 49160 | tf_op jit(solution)/shard_map/ppermute | solution.py:624
  29.0 10.7 %collective-permute-start.2 = (bf16[736,128]{1,0:T(8,128)(2,1)S(1)}, bf16[736,128]{1,0:T(8,128)(2,1)S(1)}, u32[]{:S(2)}, u32[]{:S(2)}) collective-permute-start(bf16[736,128]{1,0:T(8,128)(2,1)S(1)} %shard_map.62), channel_id=1, source_target_pairs={{0,4},{1,5},{4,8},{5,9},{8,12},{9,13},{12,16},{13,17},{16,20},{17,... | collective-permute-start | bytes 565256 | tf_op jit(solution)/shard_map/ppermute | solution.py:636
  35.5 11.5 %collective-permute-start.3 = (f32[640,128]{1,0:T(8,128)S(1)}, f32[640,128]{1,0:T(8,128)S(1)}, u32[]{:S(2)}, u32[]{:S(2)}) collective-permute-start(f32[640,128]{1,0:T(8,128)S(1)} %get-tuple-element.45), channel_id=1, source_target_pairs={{4,0},{5,1},{8,4},{9,5},{12,8},{13,9},{16,12},{17,13},{20,16},{21,... | collective-permute-start | bytes 983048 | tf_op jit(solution)/shard_map/ppermute | solution.py:638
  47.7 4.9 %collective-permute-start.4 = (f32[640,128]{1,0:T(8,128)S(1)}, f32[640,128]{1,0:T(8,128)S(1)}, u32[]{:S(2)}, u32[]{:S(2)}) collective-permute-start(f32[640,128]{1,0:T(8,128)S(1)} %get-tuple-element.48), channel_id=1, source_target_pairs={{0,1},{1,0},{2,3},{3,2},{4,5},{5,4},{6,7},{7,6},{8,9},{9,8},{10,11... | collective-permute-start | bytes 983048 | tf_op jit(solution)/shard_map/ppermute | solution.py:644
  53.3 11.1 %collective-permute-start.5 = (f16[336,128]{1,0:T(8,128)(2,1)S(1)}, f16[336,128]{1,0:T(8,128)(2,1)S(1)}, u32[]{:S(2)}, u32[]{:S(2)}) collective-permute-start(f16[336,128]{1,0:T(8,128)(2,1)S(1)} %convert_element_type.8), channel_id=1, source_target_pairs={{0,2},{2,0},{1,3},{3,1},{4,6},{6,4},{5,7},{7,5},{8,10},{10,8},{9,1... | collective-permute-start | bytes 258056 | tf_op jit(solution)/shard_map/ppermute | solution.py:646

commit v3 on v2

--- a/solution.py
+++ b/solution.py
@@ -22,11 +22,11 @@
 PART = CELLS + 2 * EDGES
 HALO = 3 * LON
 MAIN = WIN * LON
+BACK = MEMBERS * RIM
 LATROWS = MEMBERS * RIM + MEMBERS + RIM + 8
 TAPE_ROWS = 1184
 F32 = jnp.float32
 BF16 = jnp.bfloat16
-SMEM = pltpu.SMEM
 VMEM = pltpu.VMEM
 SHARE = 1.0 / (MEMBERS - 1)
 
@@ -43,13 +43,11 @@
     return jax.ShapeDtypeStruct(dims, dtype)
 
 
-def call(kernel, out_shape, scratch, *args, spaces=None, limit=16, flops=0):
-    if spaces is None:
-        spaces = [SMEM] + [VMEM] * (len(args) - 1)
+def call(kernel, out_shape, scratch, *args, limit=16, flops=0):
     return pl.pallas_call(
         kernel,
         out_shape=out_shape,
-        in_specs=[pl.BlockSpec(memory_space=space) for space in spaces],
+        in_specs=[pl.BlockSpec(memory_space=VMEM)] * len(args),
         out_specs=jax.tree.map(lambda _: pl.BlockSpec(memory_space=VMEM), out_shape),
         scratch_shapes=scratch,
         compiler_params=pltpu.CompilerParams(vmem_limit_bytes=limit * 2**20),
@@ -58,7 +56,7 @@
 
 
 def edges_kernel(
-    index_ref, own_ref, taper_ref, first_ref, second_ref, wide, fields, cells
+    own_ref, taper_ref, first_ref, second_ref, wide, fields, cells
 ):
     for tap in range(TAPS):
         wide[tap * ROWS : tap * ROWS + ROWS] = taper_ref[tap].astype(F32)
@@ -104,12 +102,12 @@
         right_rows.append(right)
     left = jnp.concatenate(left_rows, 0)
     right = jnp.concatenate(right_rows, 0)
-    odd = index_ref[3] > 0
+    odd = lax.axis_index("lon") % 2 == 1
     first_ref[...] = jnp.where(odd, right, left).astype(BF16)
     second_ref[...] = jnp.where(odd, left, right).astype(BF16)
 
 
-def edge_messages(index, own, taper):
+def edge_messages(own, taper):
     return call(
         edges_kernel,
         (
@@ -119,15 +117,14 @@
             shape(2 * CLAT, LON),
         ),
         [VMEM(((GROUP + 4) * CLAT, LON), F32)],
-        index,
         own,
         taper,
     )
 
 
-def message_kernel(index_ref, own_ref, first_ref, second_ref, out_ref):
+def message_kernel(own_ref, first_ref, second_ref, out_ref):
     out_ref[0:CELLS] = own_ref[0:CELLS]
-    odd = index_ref[3]
+    odd = lax.axis_index("lon") % 2
     east = pl.multiple_of(CELLS + (1 - odd) * EDGES, EDGES)
     west = pl.multiple_of(CELLS + odd * EDGES, EDGES)
     out_ref[pl.ds(east, EDGES)] = first_ref[...]
@@ -145,8 +142,8 @@
     return jnp.where(ring < CLAT, inside, outside)
 
 
-def bands_kernel(index_ref, wide, band_ref, rim_ref, narrow):
-    mem = index_ref[0]
+def bands_kernel(wide, band_ref, rim_ref, narrow):
+    mem = lax.axis_index("mem")
     narrow[...] = jnp.zeros(narrow.shape, F32)
     for i in range(ROWS):
         for j in range(WIN):
@@ -187,12 +184,11 @@
     rim_ref[...] = narrow[...].astype(BF16)
 
 
-def bands(index, wide):
+def bands(wide):
     return call(
         bands_kernel,
         (shape(MAIN, ROWS * LON, dtype=BF16), shape(HALO, ROWS * LON, dtype=BF16)),
         [VMEM((HALO, ROWS * LON), F32)],
-        index,
         wide,
     )
 
@@ -207,51 +203,64 @@
     return jnp.concatenate(parts, 0)
 
 
-def halo_cells(index_ref, wide, side):
-    flip = index_ref[1 + side]
+def over_seam(side):
+    last = lax.axis_size("lon") - 1
+    return lax.axis_index("lon") == (0 if side else last)
+
+
+def halo_cells(wide, side, pitch=PART):
+    flip = over_seam(side)
     parts = []
     for g in range(4):
-        part = jnp.where(flip > 0, (g + 2) % 4, g)
-        at = pl.multiple_of(part * PART + CELLS + side * EDGES, 8)
+        part = jnp.where(flip, (g + 2) % 4, g)
+        at = pl.multiple_of(part * pitch + pitch - 2 * EDGES + side * EDGES, 8)
         parts.append(wide[pl.ds(at, GROUP), :])
     return jnp.concatenate(parts, 0)
 
 
-def halo_field(wide, side, which):
-    at = CELLS + side * EDGES + 16
+def halo_field(wide, side, which, pitch=PART):
+    at = pitch - 2 * EDGES + side * EDGES + 16
     return wide[at : at + 8][4 + which : 5 + which]
 
 
-def lat_kernel(index_ref, x_ref, fields, out_ref, wide, rows):
-    mem = index_ref[0]
-    wide[...] = x_ref[...].astype(F32)
-    first = jnp.where(mem < 2, RIM, 0)
-    for m in range(MEMBERS):
-        at = pl.multiple_of((m // GROUP) * PART + (m % GROUP) * CLAT + first, 8)
-        rows[m * RIM : m * RIM + RIM] = wide[pl.ds(at, RIM), :]
+def lat_kernel(x_ref, fields, out_ref, halos, rows):
+    mem = lax.axis_index("mem")
+    upper = mem < 2
+    first = jnp.where(upper, RIM, 0)
+    for m in range(0, MEMBERS, 2):
+        at = (m // GROUP) * PART + (m % GROUP) * CLAT
+        pair = x_ref[at : at + 2 * CLAT].astype(F32)
+        one = jnp.where(upper, pair[RIM:CLAT], pair[0:RIM])
+        two = jnp.where(upper, pair[CLAT + RIM :], pair[CLAT : CLAT + RIM])
+        out_ref[m * RIM : m * RIM + CLAT] = jnp.concatenate([one, two], 0).astype(BF16)
+    for g in range(4):
+        at = g * 2 * EDGES
+        halos[at : at + 2 * EDGES] = x_ref[g * PART + CELLS : (g + 1) * PART].astype(F32)
     lane = lanes((MEMBERS + 8, LON))
     pad = jnp.zeros((7, LON), F32)
     sides = []
     for side in range(2):
-        cells = [halo_cells(index_ref, wide, side), halo_field(wide, side, 0), pad]
+        cells = [
+            halo_cells(halos, side, 2 * EDGES),
+            halo_field(halos, side, 0, 2 * EDGES),
+            pad,
+        ]
         sides.append(jnp.concatenate(cells, 0))
     half = LON // 2
     low = jnp.where(lane < half, sides[0], pltpu.roll(sides[1], half, 1))
     high = jnp.where(lane < half, pltpu.roll(sides[0], half, 1), sides[1])
     both = jnp.where(mem < 2, high, low)
-    base = MEMBERS * RIM
-    rows[base : base + MEMBERS] = both[:MEMBERS]
-    rows[base + MEMBERS : base + MEMBERS + RIM] = fields[pl.ds(pl.multiple_of(first, 8), RIM), :]
-    rows[base + MEMBERS + RIM :] = both[MEMBERS:]
-    out_ref[...] = rows[...].astype(BF16)
-
-
-def lat_message(index, gathered, fields):
+    rows[0:MEMBERS] = both[:MEMBERS]
+    rows[MEMBERS : MEMBERS + RIM] = fields[pl.ds(pl.multiple_of(first, 8), RIM), :]
+    rows[MEMBERS + RIM :] = both[MEMBERS:]
+    out_ref[MEMBERS * RIM :] = rows[...].astype(BF16)
+
+
+def lat_message(gathered, fields):
     return call(
         lat_kernel,
         shape(LATROWS, LON, dtype=BF16),
-        [VMEM((4 * PART, LON), F32), VMEM((LATROWS, LON), F32)],
-        index,
+        [VMEM((8 * EDGES, LON), F32), VMEM((LATROWS - MEMBERS * RIM, LON), F32)],
         gathered,
         fields,
     )
@@ -284,8 +293,23 @@
     return both[:MEMBERS] + both[MEMBERS:]
 
 
-def rim_push_kernel(index_ref, x_ref, fields, band_ref, rim_ref, scaled, corner, wide):
-    mem = index_ref[0]
+def by_core(mem, members):
+    even = jnp.concatenate([members[0:GROUP], members[2 * GROUP : 3 * GROUP]], 0)
+    odd = jnp.concatenate([members[GROUP : 2 * GROUP], members[3 * GROUP :]], 0)
+    first = mem % 2 == 0
+    return jnp.where(first, even, odd), jnp.where(first, odd, even)
+
+
+def scale_down(ref, rows):
+    values = ref[0:rows]
+    largest = jnp.full((16, LON), jnp.max(jnp.abs(values)), F32)
+    power = jnp.clip(jnp.round(jnp.log2(largest)) - 8.0, -120.0, 100.0)
+    ref[0:rows] = values * jnp.exp2(-power)[0:1]
+    ref[rows : rows + 16] = power
+
+
+def rim_push_kernel(x_ref, fields, band_ref, rim_ref, scaled, corner, wide):
+    mem = lax.axis_index("mem")
     wide[...] = x_ref[...].astype(F32)
     for i in range(ROWS):
         own = gathered_rows(wide, ROWS * mem + i, CLAT) * fields[pl.ds(CLAT + ROWS * mem + i, 1), :]
@@ -293,8 +317,8 @@
         scaled[0:MEMBERS, i * LON : (i + 1) * LON] = high
         scaled[MEMBERS:, i * LON : (i + 1) * LON] = low
     lane = lanes((MEMBERS, LON))
-    east = halo_cells(index_ref, wide, 0) * halo_field(wide, 0, 1)
-    west = halo_cells(index_ref, wide, 1) * halo_field(wide, 1, 1)
+    east = halo_cells(wide, 0) * halo_field(wide, 0, 1)
+    west = halo_cells(wide, 1) * halo_field(wide, 1, 1)
     east = pltpu.roll(east, (LON - 32 * mem) % LON, 1)
     west = pltpu.roll(west, (LON + 32 - 32 * mem) % LON, 1)
     high, low = split(jnp.where(lane < 32, east, jnp.where(lane < 64, west, 0.0)))
@@ -304,7 +328,7 @@
     corner[...] = jnp.zeros(corner.shape, BF16)
     tiles = []
     for side in range(2):
-        part = jnp.where(index_ref[1 + side] > 0, (mem + 2) % 4, mem)
+        part = jnp.where(over_seam(side), (mem + 2) % 4, mem)
         at = pl.multiple_of(part * PART + CELLS + side * EDGES + TAPE, 8)
         packed = wide[pl.ds(at, EDGES - TAPE), :]
         tiles.append(
@@ -342,12 +366,14 @@
     def _(step):
         total = pushes(scaled, corner, band_ref, step)
         for k in range(STEP):
-            row = ring_row(mem, step * STEP + k) - CLAT
-            rim_ref[pl.ds(row, MEMBERS, stride=RIM), :] = total[:, k * LON : (k + 1) * LON]
-
-
-def block_push_kernel(index_ref, scaled, corner, band_ref, out_ref):
-    mem = index_ref[0]
+            row = pl.ds(ring_row(mem, step * STEP + k) - CLAT, MEMBERS, stride=RIM)
+            rim_ref[row, :] = total[:, k * LON : (k + 1) * LON]
+
+    scale_down(rim_ref, BACK)
+
+
+def block_push_kernel(scaled, corner, band_ref, out_ref):
+    mem = lax.axis_index("mem")
     zeros = jnp.zeros((MEMBERS, LON), F32)
 
     @pl.when((mem == 0) | (mem == 3))
@@ -369,43 +395,41 @@
 STEP = 4
 
 
-def rim_push(index, gathered, fields, band):
+def rim_push(gathered, fields, band):
     return call(
         rim_push_kernel,
         (
-            shape(MEMBERS * RIM, LON),
+            shape(BACK + 16, LON),
             shape(2 * MEMBERS, (ROWS + 1) * LON, dtype=BF16),
             shape(MAIN, LON, dtype=BF16),
+            shape(4 * PART, LON),
         ),
-        [VMEM((4 * PART, LON), F32)],
-        index,
+        [],
         gathered,
         fields,
         band,
-        flops=4 * 10**9,
-    )
-
-
-def block_push(index, scaled, corner, band):
+        flops=10**6,
+    )
+
+
+def block_push(scaled, corner, band):
     return call(
         block_push_kernel,
         shape(MEMBERS * CLAT, LON),
         [],
-        index,
         scaled,
         corner,
         band,
-        flops=4 * 10**9,
+        flops=10**6,
     )
 
 
 def first_kernel(
-    index_ref, x_ref, lat_ref, fields, band_ref, rim_ref, push_ref,
-    out_ref, window, halos,
-    wide, wide_lat, scaled,
+    wide, lat_ref, fields, band_ref, rim_ref, push_ref,
+    keep_ref, send_ref, window, halos,
+    wide_lat, scaled,
 ):
-    mem = index_ref[0]
-    wide[...] = x_ref[...].astype(F32)
+    mem = lax.axis_index("mem")
     wide_lat[...] = lat_ref[...].astype(F32)
     base = MEMBERS * RIM
     pad = jnp.zeros((DEPTH - MEMBERS - 1, LON), F32)
@@ -424,7 +448,7 @@
             window[j, MEMBERS:] = jnp.concatenate([row, pad], 0)
 
     for side in range(2):
-        halos[side, 0:MEMBERS] = halo_cells(index_ref, wide, side)
+        halos[side, 0:MEMBERS] = halo_cells(wide, side)
         halos[side, MEMBERS:] = jnp.concatenate([halo_field(wide, side, 0), pad], 0)
     halos[2, 0:MEMBERS] = wide_lat[base : base + MEMBERS]
     last = wide_lat[base + MEMBERS + RIM : base + MEMBERS + RIM + 1]
@@ -443,81 +467,85 @@
     both = both + jnp.dot(scaled[:, MAIN:], rim_ref[...], preferred_element_type=F32)
     total = both[:MEMBERS] + both[MEMBERS:]
     v_rows = fields[0:CLAT] * SHARE
-    for m in range(MEMBERS):
-        at = m * CLAT
-        out_ref[at : at + CLAT] = push_ref[at : at + CLAT] * v_rows
+    core = mem % 2
+    for half in range(2):
+        for take, target in ((core, keep_ref), (1 - core, send_ref)):
+            for m in range(GROUP):
+                at = pl.multiple_of((2 * half + take) * CELLS + m * CLAT, 8)
+                to = half * CELLS + m * CLAT
+                target[to : to + CLAT] = push_ref[pl.ds(at, CLAT), :] * v_rows
     for i in range(ROWS):
-        at = pl.ds(ROWS * mem + i, MEMBERS, stride=CLAT)
+        at = pl.ds(ROWS * mem + i, 2 * GROUP, stride=CLAT)
         c_row = fields[pl.ds(CLAT + ROWS * mem + i, 1), :] * SHARE
-        out_ref[at, :] = out_ref[at, :] + total[:, i * LON : (i + 1) * LON] * c_row
-
-
-def first_sum(index, gathered, lat_halo, fields, band, rim, pushed):
+        keep, send = by_core(mem, total[:, i * LON : (i + 1) * LON] * c_row)
+        keep_ref[at, :] = keep_ref[at, :] + keep
+        send_ref[at, :] = send_ref[at, :] + send
+
+
+def first_sum(wide, lat_halo, fields, band, rim, pushed):
     return call(
         first_kernel,
-        (shape(MEMBERS * CLAT, LON), shape(WIN, DEPTH, LON), shape(3, DEPTH, LON)),
+        (
+            shape(2 * CELLS, LON),
+            shape(2 * CELLS, LON),
+            shape(WIN, DEPTH, LON),
+            shape(3, DEPTH, LON),
+        ),
         [
-            VMEM((4 * PART, LON), F32),
             VMEM((LATROWS, LON), F32),
             VMEM((2 * MEMBERS, MAIN + HALO), BF16),
         ],
-        index,
-        gathered,
+        wide,
         lat_halo,
         fields,
         band,
         rim,
         pushed,
-        flops=4 * 10**9,
-    )
-
-
-def near_kernel(index_ref, part_ref, back_ref, fields, keep_ref, send_ref):
-    mem = index_ref[0]
-    core = mem % 2
-    first = pl.multiple_of(jnp.where(mem < 2, RIM, 0), 8)
-    v_rows = fields[pl.ds(first, RIM), :] * SHARE
+        flops=10**6,
+    )
+
+
+def add_back(mem, take, half, at, back_ref, fields, target):
+    first = jnp.where(mem < 2, RIM, 0)
+    rows = fields[pl.ds(pl.multiple_of(first, 8), RIM), :] * SHARE
+    rows = rows * jnp.exp2(back_ref[BACK : BACK + 1])
+    start = (2 * half + take) * GROUP * RIM
+    for m in range(GROUP):
+        source = pl.ds(pl.multiple_of(start + m * RIM, 8), RIM)
+        to = pl.ds(pl.multiple_of(at + m * CLAT + first, 8), RIM)
+        target[to, :] = target[to, :] + back_ref[source, :] * rows
+
+
+def near_kernel(part_ref, back_ref, fields, send_ref):
+    mem = lax.axis_index("mem")
+    send_ref[...] = part_ref[...]
     for half in range(2):
-        for take, target in ((core, keep_ref), (1 - core, send_ref)):
-            at = pl.multiple_of((2 * half + take) * CELLS, 8)
-            target[half * CELLS : (half + 1) * CELLS] = part_ref[pl.ds(at, CELLS), :]
-            at = pl.multiple_of((2 * half + take) * GROUP * RIM, 8)
-            more = back_ref[pl.ds(at, GROUP * RIM), :]
-            for m in range(GROUP):
-                to = pl.ds(pl.multiple_of(half * CELLS + m * CLAT + first, 8), RIM)
-                target[to, :] = target[to, :] + more[m * RIM : (m + 1) * RIM] * v_rows
-
-
-def near_parts(index, partial, back, fields):
-    return call(
-        near_kernel,
-        (shape(2 * CELLS, LON), shape(2 * CELLS, LON)),
-        [],
-        index,
-        partial,
-        back,
-        fields,
-    )
-
-
-def far_kernel(index_ref, keep_ref, more_ref, mine_ref, send_ref):
-    far = index_ref[0] // 2
-    at = pl.ds(pl.multiple_of(far * CELLS, 8), CELLS)
-    mine_ref[...] = keep_ref[at, :] + more_ref[at, :]
-    at = pl.ds(pl.multiple_of((1 - far) * CELLS, 8), CELLS)
-    send = keep_ref[at, :] + more_ref[at, :]
-    largest = jnp.full((16, LON), jnp.max(jnp.abs(send)), F32)
-    power = jnp.clip(jnp.round(jnp.log2(largest)) - 8.0, -120.0, 100.0)
-    send_ref[0:CELLS] = send * jnp.exp2(-power)[0:1]
-    send_ref[CELLS:] = power
-
-
-def far_parts(index, keep, more):
-    return call(far_kernel, (shape(CELLS, LON), shape(CELLS + 16, LON)), [], index, keep, more)
-
-
-def taper_part(index_ref, window, halos, fields, flat, own, turned, product, shifted, taps_of):
-    mem = index_ref[0]
+        add_back(mem, 1 - mem % 2, half, half * CELLS, back_ref, fields, send_ref)
+
+
+def near_parts(part, back, fields):
+    return call(near_kernel, shape(2 * CELLS, LON), [], part, back, fields)
+
+
+def far_kernel(keep_ref, more_ref, back_ref, fields, mine_ref, send_ref):
+    mem = lax.axis_index("mem")
+    far = mem // 2
+    for take, target in ((far, mine_ref), (1 - far, send_ref)):
+        at = pl.ds(pl.multiple_of(take * CELLS, 8), CELLS)
+        target[0:CELLS] = keep_ref[at, :] + more_ref[at, :]
+        add_back(mem, mem % 2, take, 0, back_ref, fields, target)
+    scale_down(send_ref, CELLS)
+
+
+def far_parts(keep, more, back, fields):
+    return call(
+        far_kernel, (shape(CELLS, LON), shape(CELLS + 16, LON)), [],
+        keep, more, back, fields,
+    )
+
+
+def taper_part(window, halos, fields, flat, own, turned, product, shifted, taps_of):
+    mem = lax.axis_index("mem")
     used = range(taps_of[0], taps_of[-1] + ROWS)
     for j in used:
         turned[j * LON : (j + 1) * LON, :] = window[j].T.astype(BF16)
@@ -562,15 +590,15 @@
             flat[pl.ds(a * SPAN * ROWS + i, SPAN, stride=ROWS), :] = taps[0:SPAN]
 
 
-EARLY = 9
-
-
-def early_kernel(index_ref, window, halos, fields, flat, *scratch):
-    taper_part(index_ref, window, halos, fields, flat, *scratch, range(EARLY))
-
-
-def late_kernel(index_ref, window, halos, fields, early, taper_ref, flat, *scratch):
-    taper_part(index_ref, window, halos, fields, flat, *scratch, range(EARLY, SPAN))
+EARLY = 2
+
+
+def early_kernel(window, halos, fields, flat, *scratch):
+    taper_part(window, halos, fields, flat, *scratch, range(EARLY))
+
+
+def late_kernel(window, halos, fields, early, taper_ref, flat, *scratch):
+    taper_part(window, halos, fields, flat, *scratch, range(EARLY, SPAN))
     for tap in range(TAPS):
         source = early if tap < EARLY * SPAN else flat
         taper_ref[tap] = source[tap * ROWS : tap * ROWS + ROWS]
@@ -585,35 +613,25 @@
     ]
 
 
-def early_taps(index, window, halos, fields):
+def early_taps(window, halos, fields):
     return call(
         early_kernel, shape(EARLY * SPAN * ROWS, LON), taper_scratch(),
-        index, window, halos, fields, limit=24, flops=3 * 10**9,
-    )
-
-
-def late_taps(index, window, halos, fields, early):
+        window, halos, fields, limit=24, flops=2 * 10**10,
+    )
+
+
+def late_taps(window, halos, fields, early):
     return call(
         late_kernel, shape(TAPS, ROWS, LON), [VMEM((TAPS * ROWS, LON), F32), *taper_scratch()],
-        index, window, halos, fields, early, limit=24, flops=3 * 10**9,
+        window, halos, fields, early, limit=24, flops=10**6,
     )
 
 
 def body(anomalies, vector, cotangent, taper):
-    mem = lax.axis_index("mem").astype(jnp.int32)
-    strip = lax.axis_index("lon")
     blocks = lax.axis_size("lat")
     strips = lax.axis_size("lon")
-    index = jnp.stack(
-        [
-            mem,
-            (strip == strips - 1).astype(jnp.int32),
-            (strip == 0).astype(jnp.int32),
-            (strip % 2).astype(jnp.int32),
-        ]
-    )
     own = jnp.concatenate([anomalies.reshape(CELLS, LON), vector, cotangent], 0)
-    first, second, wide, fields = edge_messages(index, own, taper)
+    first, second, wide, fields = edge_messages(own, taper)
     swaps = ([], [])
     for s in range(strips):
         for m in range(4):
@@ -622,30 +640,37 @@
             swaps[1 - s % 2].extend([(here, there), (there, here)])
     first = lax.ppermute(first, ("lon", "mem"), swaps[0])
     second = lax.ppermute(second, ("lon", "mem"), swaps[1])
-    band, rim = bands(index, wide)
+    band, rim = bands(wide)
     first, second, band, rim = lax.optimization_barrier((first, second, band, rim))
     message = call(
-        message_kernel, shape(PART, LON, dtype=BF16), [], index, own, first, second
+        message_kernel, shape(PART, LON, dtype=BF16), [], own, first, second
     )
     gathered = lax.all_gather(message, "mem", axis=0, tiled=True)
 
     down = [(4 * z + m, 4 * z + 4 + m) for z in range(blocks - 1) for m in (0, 1)]
     up = [(4 * z + 4 + m, 4 * z + m) for z in range(blocks - 1) for m in (2, 3)]
-    message = lat_message(index, gathered, fields)
+    message = lat_message(gathered, fields)
     message, gathered = lax.optimization_barrier((message, gathered))
     lat_halo = lax.ppermute(message, ("lat", "mem"), down + up)
-    pushed_out, scaled, corner = rim_push(index, gathered, fields, band)
-    back = lax.ppermute(pushed_out, ("lat", "mem"), [(b, a) for a, b in down + up])
-    pushed = block_push(index, scaled, corner, band)
-    partial, window, halos = first_sum(index, gathered, lat_halo, fields, band, rim, pushed)
-    early = early_taps(index, window, halos, fields)
-    back, early = lax.optimization_barrier((back, early))
-    keep, send = near_parts(index, partial, back, fields)
+    pushed_out, scaled, corner, wide = rim_push(gathered, fields, band)
+    back = lax.ppermute(
+        pushed_out.astype(jnp.float16), ("lat", "mem"), [(b, a) for a, b in down + up]
+    )
+    pushed = block_push(scaled, corner, band)
+    keep, send, window, halos = first_sum(
+        wide, lat_halo, fields, band, rim, pushed
+    )
+    back, send = lax.optimization_barrier((back, send))
+    back = back.astype(F32)
+    send = near_parts(send, back, fields)
+    send, window = lax.optimization_barrier((send, window))
     more = lax.ppermute(send, "mem", [(0, 1), (1, 0), (2, 3), (3, 2)])
-    mine, send = far_parts(index, keep, more)
+    early = early_taps(window, halos, fields)
+    more, early = lax.optimization_barrier((more, early))
+    mine, send = far_parts(keep, more, back, fields)
     half = lax.ppermute(send.astype(jnp.float16), "mem", [(0, 2), (2, 0), (1, 3), (3, 1)])
     mine, early = lax.optimization_barrier((mine, early))
-    grad_taper = late_taps(index, window, halos, fields, early)
+    grad_taper = late_taps(window, halos, fields, early)
     more = half.astype(F32)
     grad_anomalies = mine + more[:CELLS] * jnp.exp2(more[CELLS : CELLS + 1])
     grad_anomalies = grad_anomalies.reshape(GROUP, CLAT, LON)

time: 65.4 us -> 58.8 us (0.90)
  Pallas kernels: 16.9 us -> 11.1 us
  waiting for transfers between devices: 9.85 us -> 9.13 us
    pallas_call x11, Pallas kernels: 16.9 us -> 11.1 us  [call(): pl.pallas_call(kernel, out_shape=out_shape, in_specs=[pl.BlockSpec(memory...]
    ppermute x1, waiting for transfers between devices: 1.23 us -> 0.26 us  [body(): more = lax.ppermute(send, 'mem', [(0, 1), (1, 0), (2, 3), (3, 2)])]
    ppermute x1, waiting for transfers between devices: 5.36 us -> 4.57 us  [body(): lax.ppermute(send.astype(jnp.float16), 'mem', [(0, 2), (2, 0), (1, 3), (3...]
  transfers between devices with their start and end apart: 6 -> 6, of which waited for: 4 -> 4; matrix products, arithmetic and copies ran while one was open for 0% -> 0% of each run, Pallas kernels for 21% -> 18%
where the time goes in v3:
time: 58.8 us; the launch traced here: 58.5 us
  starting transfers between devices  19.2 us (33%)
  blocking collectives  15.5 us (26%)
  Pallas kernels  11.1 us (19%)
  waiting for transfers between devices  9.13 us (16%)
  other arithmetic  1.7 us (3%)
  local copies, waits for them, and re-layouts  0.96 us (2%)
  between operations  0.79 us (1%)
    all_gather x1, blocking collectives, body(): gathered = lax.all_gather(message, 'mem', axis=0, tiled=True)  15.5 us
    pallas_call x11, Pallas kernels, call(): pl.pallas_call(kernel, out_shape=out_shape, in_specs=[pl.BlockSpec(memory...  11.1 us
    ppermute x1, starting transfers between devices, body(): lat_halo = lax.ppermute(message, ('lat', 'mem'), down + up)  5.21 us
    ppermute x1, waiting for transfers between devices, body(): lax.ppermute(send.astype(jnp.float16), 'mem', [(0, 2), (2, 0), (1, 3), (3...  4.57 us
    ppermute x1, starting transfers between devices, body(): first = lax.ppermute(first, ('lon', 'mem'), swaps[0])  4.27 us
    ppermute x1, starting transfers between devices, body(): more = lax.ppermute(send, 'mem', [(0, 1), (1, 0), (2, 3), (3, 2)])  3.6 us
    ppermute x1, waiting for transfers between devices, body(): lax.ppermute(pushed_out.astype(jnp.float16), ('lat', 'mem'), [(b, a) for...  3.01 us
    ppermute x1, starting transfers between devices, body(): lax.ppermute(send.astype(jnp.float16), 'mem', [(0, 2), (2, 0), (1, 3), (3...  2.27 us
  transfers between devices with their start and end apart: 6, of which 4 were waited for; matrix products, arithmetic and copies ran while one was open for 0% of the time, Pallas kernels for 18%

profile of v3, /device:TPU:201, one launch (start us, length us, event | category | flops | bytes accessed | tf_op | source)
XLA Modules:
  0.0 58.5 jit_solution(12612125419393840781)
XLA Ops:
  0.6 0.9 %pad_maximum_fusion.own_ref = bf16[352,128]{1,0:T(8,128)(2,1)S(1)} fusion(bf16[16,128]{1,0:T(8,128)(2,1)} %param.6, bf16[16,128]{1,0:T(8,128)(2,1)} %param.5, bf16[320,128]{1,0:T(8,128)(2,1)} %bitcast.5), kind=kLoop, calls=%fused_computation.2 | loop fusion | flops 270336 | bytes 180224 | tf_op jit(solution)/shard_map/concatenate | solution.py:633
  1.6 0.0 copy-start
  1.6 1.0 %copy-done = bf16[289,4,128]{2,1,0:T(4,128)(2,1)S(1)} copy-done((bf16[289,4,128]{2,1,0:T(4,128)(2,1)S(1)}, bf16[289,4,128]{2,1,0:T(4,128)(2,1)}, u32[]{:S(2)}) %copy-start) | copy-done | bytes 295960
  2.5 0.3 shard_map.59
  2.8 4.3 %collective-permute-start = (bf16[64,128]{1,0:T(8,128)(2,1)S(1)}, bf16[64,128]{1,0:T(8,128)(2,1)S(1)}, u32[]{:S(2)}, u32[]{:S(2)}) collective-permute-start(bf16[64,128]{1,0:T(8,128)(2,1)S(1)} %get-tuple-element.32), channel_id=1, source_target_pairs={{32,64},{64,32},{33,65},{65,33},{34,66},{66,34},{35,67},{67,35},{9... | collective-permute-start | bytes 49160 | tf_op jit(solution)/shard_map/ppermute | solution.py:641
  7.1 2.0 %collective-permute-start.1 = (bf16[64,128]{1,0:T(8,128)(2,1)S(1)}, bf16[64,128]{1,0:T(8,128)(2,1)S(1)}, u32[]{:S(2)}, u32[]{:S(2)}) collective-permute-start(bf16[64,128]{1,0:T(8,128)(2,1)S(1)} %get-tuple-element.33), channel_id=1, source_target_pairs={{0,32},{32,0},{1,33},{33,1},{2,34},{34,2},{3,35},{35,3},{64,96},{9... | collective-permute-start | bytes 49160 | tf_op jit(solution)/shard_map/ppermute | solution.py:642
  9.1 1.2 %shard_map.60 = (bf16[2560,512]{1,0:T(8,128)(2,1)S(1)}, bf16[384,512]{1,0:T(8,128)(2,1)S(1)}) custom-call(f32[1184,128]{1,0:T(8,128)S(1)} %get-tuple-element.34.wide), custom_call_target="tpu_custom_call" | custom-call | bytes 1048576 | tf_op jit(solution)/shard_map/pallas_call | solution.py:47
  10.3 0.0 collective-permute-done.first_ref
  10.3 1.3 %collective-permute-done.1.second_ref = bf16[64,128]{1,0:T(8,128)(2,1)S(1)} collective-permute-done((bf16[64,128]{1,0:T(8,128)(2,1)S(1)}, bf16[64,128]{1,0:T(8,128)(2,1)S(1)}, u32[]{:S(2)}, u32[]{:S(2)}) %collective-permute-start.1) | collective-permute-done | bytes 16416 | tf_op jit(solution)/shard_map/ppermute | solution.py:642
  11.6 15.5 %all_gather.3.x_ref = bf16[1792,128]{1,0:T(8,128)(2,1)S(1)} all-gather(bf16[448,128]{1,0:T(8,128)(2,1)S(1)} %shard_map.61), channel_id=1, replica_groups=mesh['lon'=16,'lat'=8,'mem'=4] {'mem'}, dimensions={0}, use_global_device_ids=true | all-gather | bytes 573440 | tf_op jit(solution)/shard_map/all_gather | solution.py:648
  27.1 0.1 shard_map.62
  27.2 5.2 %collective-permute-start.3 = (bf16[736,128]{1,0:T(8,128)(2,1)S(1)}, bf16[736,128]{1,0:T(8,128)(2,1)S(1)}, u32[]{:S(2)}, u32[]{:S(2)}) collective-permute-start(bf16[736,128]{1,0:T(8,128)(2,1)S(1)} %shard_map.62), channel_id=1, source_target_pairs={{0,4},{1,5},{4,8},{5,9},{8,12},{9,13},{12,16},{13,17},{16,20},{17,... | collective-permute-start | bytes 565256 | tf_op jit(solution)/shard_map/ppermute | solution.py:654
  32.4 0.9 %shard_map.63 = (f32[656,128]{1,0:T(8,128)S(1)}, bf16[160,640]{1,0:T(8,128)(2,1)S(1)}, bf16[2560,128]{1,0:T(8,128)(2,1)S(1)}, f32[1792,128]{1,0:T(8,128)S(1)}) custom-call(bf16[1792,128]{1,0:T(8,128)(2,1)S(1)} %all_gather.3.x_ref, f32[32,128]{1,0:T(8,128)S(1)} %get-tuple-element.39.fields, bf16[2560,512]{1,0:T(8,128)(2,1)S(1)} %get-tuple-element.41.band_ref), custom_call_target="tpu_custom_call" | custom-call | flops 1000000 | bytes 1048576 | tf_op jit(solution)/shard_map/pallas_call | solution.py:47
  33.4 1.9 %collective-permute-start.2 = (f16[656,128]{1,0:T(8,128)(2,1)S(1)}, f16[656,128]{1,0:T(8,128)(2,1)S(1)}, u32[]{:S(2)}, u32[]{:S(2)}) collective-permute-start(f16[656,128]{1,0:T(8,128)(2,1)S(1)} %convert_element_type.12), channel_id=1, source_target_pairs={{4,0},{5,1},{8,4},{9,5},{12,8},{13,9},{16,12},{17,13},{20,16},{21,... | collective-permute-start | bytes 503816 | tf_op jit(solution)/shard_map/ppermute | solution.py:656
  35.3 1.7 %shard_map.64.push_ref = f32[1280,128]{1,0:T(8,128)S(1)} custom-call(bf16[160,640]{1,0:T(8,128)(2,1)S(1)} %get-tuple-element.46.scaled, bf16[2560,128]{1,0:T(8,128)(2,1)S(1)} %get-tuple-element.47.corner, bf16[2560,512]{1,0:T(8,128)(2,1)S(1)} %get-tuple-element.41.band_ref), custom_call_target="tpu_custom_call" | custom-call | flops 1000000 | bytes 1048576 | tf_op jit(solution)/shard_map/pallas_call | solution.py:47
  37.0 0.0 collective-permute-done.3.lat_ref
  37.0 1.4 %shard_map.65 = (f32[640,128]{1,0:T(8,128)S(1)}, f32[640,128]{1,0:T(8,128)S(1)}, f32[20,88,128]{2,1,0:T(8,128)S(1)}, f32[3,88,128]{2,1,0:T(8,128)S(1)}) custom-call(f32[1792,128]{1,0:T(8,128)S(1)} %get-tuple-element.43.wide, bf16[736,128]{1,0:T(8,128)(2,1)S(1)} %collective-permute-done.3.lat_ref, f32[32,128]{1,0:T(8,128)S(1)} %get-tuple-element.39.fields, ...), custom_call_target="tpu_custom_call" | custom-call | flops 1000000 | bytes 1048576 | tf_op jit(solution)/shard_map/pallas_call | solution.py:47
  38.5 3.0 %collective-permute-done.2 = f16[656,128]{1,0:T(8,128)(2,1)S(1)} collective-permute-done((f16[656,128]{1,0:T(8,128)(2,1)S(1)}, f16[656,128]{1,0:T(8,128)(2,1)S(1)}, u32[]{:S(2)}, u32[]{:S(2)}) %collective-permute-start.2) | collective-permute-done | bytes 167968 | tf_op jit(solution)/shard_map/ppermute | solution.py:656
  41.6 3.6 %collective-permute-start.4 = (f32[640,128]{1,0:T(8,128)S(1)}, f32[640,128]{1,0:T(8,128)S(1)}, u32[]{:S(2)}, u32[]{:S(2)}) collective-permute-start(f32[640,128]{1,0:T(8,128)S(1)} %shard_map.66), channel_id=1, source_target_pairs={{0,1},{1,0},{2,3},{3,2},{4,5},{5,4},{6,7},{7,6},{8,9},{9,8},{10,11... | collective-permute-start | bytes 983048 | tf_op jit(solution)/shard_map/ppermute | solution.py:667
  45.2 1.0 %shard_map.67.early = f32[136,128]{1,0:T(8,128)S(1)} custom-call(f32[20,88,128]{2,1,0:T(8,128)S(1)} %get-tuple-element.52.window, f32[3,88,128]{2,1,0:T(8,128)S(1)} %get-tuple-element.53.halos, f32[32,128]{1,0:T(8,128)S(1)} %get-tuple-element.39.fields), custom_call_target="tpu_custom_call" | custom-call | flops 20000000000 | bytes 1048576 | tf_op jit(solution)/shard_map/pallas_call | solution.py:47
  46.1 0.3 collective-permute-done.4.more_ref
  46.4 0.2 shard_map.68
  46.7 2.3 %collective-permute-start.5 = (f16[336,128]{1,0:T(8,128)(2,1)S(1)}, f16[336,128]{1,0:T(8,128)(2,1)S(1)}, u32[]{:S(2)}, u32[]{:S(2)}) collective-permute-start(f16[336,128]{1,0:T(8,128)(2,1)S(1)} %convert_element_type.14), channel_id=1, source_target_pairs={{0,2},{2,0},{1,3},{3,1},{4,6},{6,4},{5,7},{7,5},{8,10},{10,8},{9,1... | collective-permute-start | bytes 258056 | tf_op jit(solution)/shard_map/ppermute | solution.py:671
  49.0 4.2 %shard_map.69 = f32[289,4,128]{2,1,0:T(4,128)} custom-call(f32[20,88,128]{2,1,0:T(8,128)S(1)} %get-tuple-element.52.window, f32[3,88,128]{2,1,0:T(8,128)S(1)} %get-tuple-element.53.halos, f32[32,128]{1,0:T(8,128)S(1)} %get-tuple-element.39.fields, f32[136,128]{1,0:T(8,128)S(1)} %shard_map.67.early), custom_call_target="tpu_custom_call" | custom-call | flops 1000000 | bytes 1048576 | tf_op jit(solution)/shard_map/pallas_call | solution.py:47
  53.2 4.6 %collective-permute-done.5 = f16[336,128]{1,0:T(8,128)(2,1)S(1)} collective-permute-done((f16[336,128]{1,0:T(8,128)(2,1)S(1)}, f16[336,128]{1,0:T(8,128)(2,1)S(1)}, u32[]{:S(2)}, u32[]{:S(2)}) %collective-permute-start.5) | collective-permute-done | bytes 86048 | tf_op jit(solution)/shard_map/ppermute | solution.py:671
  57.8 0.7 %fusion = f32[320,128]{1,0:T(8,128)} fusion(f32[320,128]{1,0:T(8,128)S(1)} %get-tuple-element.60, f32[336,128]{1,0:T(8,128)S(1)} %convert_element_type.15, f32[128]{0:T(128)S(1)} %fusion.2), kind=kLoop, calls=%fused_computation.1 | loop fusion | flops 81920 | bytes 492032 | tf_op jit(solution)/shard_map/add | solution.py:675
  (7 shorter events, 0.1 us)
Async XLA Ops:
  1.6 1.0 %copy-start = (bf16[289,4,128]{2,1,0:T(4,128)(2,1)S(1)}, bf16[289,4,128]{2,1,0:T(4,128)(2,1)}, u32[]{:S(2)}) copy-start(bf16[289,4,128]{2,1,0:T(4,128)(2,1)} %taper_ref.1) | copy-start | bytes 887812
  2.8 7.5 %collective-permute-start = (bf16[64,128]{1,0:T(8,128)(2,1)S(1)}, bf16[64,128]{1,0:T(8,128)(2,1)S(1)}, u32[]{:S(2)}, u32[]{:S(2)}) collective-permute-start(bf16[64,128]{1,0:T(8,128)(2,1)S(1)} %get-tuple-element.32), channel_id=1, source_target_pairs={{32,64},{64,32},{33,65},{65,33},{34,66},{66,34},{35,67},{67,35},{9... | collective-permute-start | bytes 49160 | tf_op jit(solution)/shard_map/ppermute | solution.py:641
  7.1 4.5 %collective-permute-start.1 = (bf16[64,128]{1,0:T(8,128)(2,1)S(1)}, bf16[64,128]{1,0:T(8,128)(2,1)S(1)}, u32[]{:S(2)}, u32[]{:S(2)}) collective-permute-start(bf16[64,128]{1,0:T(8,128)(2,1)S(1)} %get-tuple-element.33), channel_id=1, source_target_pairs={{0,32},{32,0},{1,33},{33,1},{2,34},{34,2},{3,35},{35,3},{64,96},{9... | collective-permute-start | bytes 49160 | tf_op jit(solution)/shard_map/ppermute | solution.py:642
  27.2 9.8 %collective-permute-start.3 = (bf16[736,128]{1,0:T(8,128)(2,1)S(1)}, bf16[736,128]{1,0:T(8,128)(2,1)S(1)}, u32[]{:S(2)}, u32[]{:S(2)}) collective-permute-start(bf16[736,128]{1,0:T(8,128)(2,1)S(1)} %shard_map.62), channel_id=1, source_target_pairs={{0,4},{1,5},{4,8},{5,9},{8,12},{9,13},{12,16},{13,17},{16,20},{17,... | collective-permute-start | bytes 565256 | tf_op jit(solution)/shard_map/ppermute | solution.py:654
  33.4 8.1 %collective-permute-start.2 = (f16[656,128]{1,0:T(8,128)(2,1)S(1)}, f16[656,128]{1,0:T(8,128)(2,1)S(1)}, u32[]{:S(2)}, u32[]{:S(2)}) collective-permute-start(f16[656,128]{1,0:T(8,128)(2,1)S(1)} %convert_element_type.12), channel_id=1, source_target_pairs={{4,0},{5,1},{8,4},{9,5},{12,8},{13,9},{16,12},{17,13},{20,16},{21,... | collective-permute-start | bytes 503816 | tf_op jit(solution)/shard_map/ppermute | solution.py:656
  41.6 4.8 %collective-permute-start.4 = (f32[640,128]{1,0:T(8,128)S(1)}, f32[640,128]{1,0:T(8,128)S(1)}, u32[]{:S(2)}, u32[]{:S(2)}) collective-permute-start(f32[640,128]{1,0:T(8,128)S(1)} %shard_map.66), channel_id=1, source_target_pairs={{0,1},{1,0},{2,3},{3,2},{4,5},{5,4},{6,7},{7,6},{8,9},{9,8},{10,11... | collective-permute-start | bytes 983048 | tf_op jit(solution)/shard_map/ppermute | solution.py:667
  46.7 11.1 %collective-permute-start.5 = (f16[336,128]{1,0:T(8,128)(2,1)S(1)}, f16[336,128]{1,0:T(8,128)(2,1)S(1)}, u32[]{:S(2)}, u32[]{:S(2)}) collective-permute-start(f16[336,128]{1,0:T(8,128)(2,1)S(1)} %convert_element_type.14), channel_id=1, source_target_pairs={{0,2},{2,0},{1,3},{3,1},{4,6},{6,4},{5,7},{7,5},{8,10},{10,8},{9,1... | collective-permute-start | bytes 258056 | tf_op jit(solution)/shard_map/ppermute | solution.py:671

commit v4 on v3

--- a/solution.py
+++ b/solution.py
@@ -19,7 +19,7 @@
 CELLS = GROUP * CLAT
 EDGES = 64
 TAPE = 24
-PART = CELLS + 2 * EDGES
+PART = CELLS + 48
 HALO = 3 * LON
 MAIN = WIN * LON
 BACK = MEMBERS * RIM
@@ -122,13 +122,17 @@
     )
 
 
-def message_kernel(own_ref, first_ref, second_ref, out_ref):
+def message_kernel(own_ref, first_ref, second_ref, out_ref, edges):
     out_ref[0:CELLS] = own_ref[0:CELLS]
-    odd = lax.axis_index("lon") % 2
-    east = pl.multiple_of(CELLS + (1 - odd) * EDGES, EDGES)
-    west = pl.multiple_of(CELLS + odd * EDGES, EDGES)
-    out_ref[pl.ds(east, EDGES)] = first_ref[...]
-    out_ref[pl.ds(west, EDGES)] = second_ref[...]
+    first = first_ref[...].astype(F32)
+    second = second_ref[...].astype(F32)
+    odd = lax.axis_index("lon") % 2 == 1
+    east = jnp.where(odd, first, second)
+    west = jnp.where(odd, second, first)
+    edges[0:EDGES] = east
+    edges[EDGES:] = west
+    halos = [east[0:GROUP], west[0:GROUP], jnp.zeros((8, LON), F32)]
+    out_ref[CELLS:] = jnp.concatenate(halos, 0).astype(BF16)
 
 
 def ring_row(mem, j):
@@ -203,27 +207,20 @@
     return jnp.concatenate(parts, 0)
 
 
-def over_seam(side):
-    last = lax.axis_size("lon") - 1
-    return lax.axis_index("lon") == (0 if side else last)
-
-
 def halo_cells(wide, side, pitch=PART):
-    flip = over_seam(side)
     parts = []
     for g in range(4):
-        part = jnp.where(flip, (g + 2) % 4, g)
-        at = pl.multiple_of(part * pitch + pitch - 2 * EDGES + side * EDGES, 8)
-        parts.append(wide[pl.ds(at, GROUP), :])
+        at = (g + 1) * pitch - 48 + side * GROUP
+        parts.append(wide[at : at + GROUP])
     return jnp.concatenate(parts, 0)
 
 
-def halo_field(wide, side, which, pitch=PART):
-    at = pitch - 2 * EDGES + side * EDGES + 16
-    return wide[at : at + 8][4 + which : 5 + which]
-
-
-def lat_kernel(x_ref, fields, out_ref, halos, rows):
+def halo_field(edges, side, which):
+    at = side * EDGES + GROUP + which
+    return edges[at : at + 1]
+
+
+def lat_kernel(x_ref, fields, edges, out_ref, halos, rows):
     mem = lax.axis_index("mem")
     upper = mem < 2
     first = jnp.where(upper, RIM, 0)
@@ -234,17 +231,12 @@
         two = jnp.where(upper, pair[CLAT + RIM :], pair[CLAT : CLAT + RIM])
         out_ref[m * RIM : m * RIM + CLAT] = jnp.concatenate([one, two], 0).astype(BF16)
     for g in range(4):
-        at = g * 2 * EDGES
-        halos[at : at + 2 * EDGES] = x_ref[g * PART + CELLS : (g + 1) * PART].astype(F32)
+        halos[g * 48 : g * 48 + 48] = x_ref[g * PART + CELLS : (g + 1) * PART].astype(F32)
     lane = lanes((MEMBERS + 8, LON))
     pad = jnp.zeros((7, LON), F32)
     sides = []
     for side in range(2):
-        cells = [
-            halo_cells(halos, side, 2 * EDGES),
-            halo_field(halos, side, 0, 2 * EDGES),
-            pad,
-        ]
+        cells = [halo_cells(halos, side, 48), halo_field(edges, side, 0), pad]
         sides.append(jnp.concatenate(cells, 0))
     half = LON // 2
     low = jnp.where(lane < half, sides[0], pltpu.roll(sides[1], half, 1))
@@ -256,13 +248,14 @@
     out_ref[MEMBERS * RIM :] = rows[...].astype(BF16)
 
 
-def lat_message(gathered, fields):
+def lat_message(gathered, fields, edges):
     return call(
         lat_kernel,
         shape(LATROWS, LON, dtype=BF16),
-        [VMEM((8 * EDGES, LON), F32), VMEM((LATROWS - MEMBERS * RIM, LON), F32)],
+        [VMEM((4 * 48, LON), F32), VMEM((LATROWS - MEMBERS * RIM, LON), F32)],
         gathered,
         fields,
+        edges,
     )
 
 
@@ -308,7 +301,7 @@
     ref[rows : rows + 16] = power
 
 
-def rim_push_kernel(x_ref, fields, band_ref, rim_ref, scaled, corner, wide):
+def rim_push_kernel(x_ref, fields, edges, band_ref, rim_ref, scaled, corner, wide):
     mem = lax.axis_index("mem")
     wide[...] = x_ref[...].astype(F32)
     for i in range(ROWS):
@@ -317,8 +310,8 @@
         scaled[0:MEMBERS, i * LON : (i + 1) * LON] = high
         scaled[MEMBERS:, i * LON : (i + 1) * LON] = low
     lane = lanes((MEMBERS, LON))
-    east = halo_cells(wide, 0) * halo_field(wide, 0, 1)
-    west = halo_cells(wide, 1) * halo_field(wide, 1, 1)
+    east = halo_cells(wide, 0) * halo_field(edges, 0, 1)
+    west = halo_cells(wide, 1) * halo_field(edges, 1, 1)
     east = pltpu.roll(east, (LON - 32 * mem) % LON, 1)
     west = pltpu.roll(west, (LON + 32 - 32 * mem) % LON, 1)
     high, low = split(jnp.where(lane < 32, east, jnp.where(lane < 64, west, 0.0)))
@@ -328,9 +321,7 @@
     corner[...] = jnp.zeros(corner.shape, BF16)
     tiles = []
     for side in range(2):
-        part = jnp.where(over_seam(side), (mem + 2) % 4, mem)
-        at = pl.multiple_of(part * PART + CELLS + side * EDGES + TAPE, 8)
-        packed = wide[pl.ds(at, EDGES - TAPE), :]
+        packed = edges[side * EDGES + TAPE : (side + 1) * EDGES]
         tiles.append(
             [
                 pltpu.roll(
@@ -395,7 +386,7 @@
 STEP = 4
 
 
-def rim_push(gathered, fields, band):
+def rim_push(gathered, fields, edges, band):
     return call(
         rim_push_kernel,
         (
@@ -407,6 +398,7 @@
         [],
         gathered,
         fields,
+        edges,
         band,
         flops=10**6,
     )
@@ -425,7 +417,7 @@
 
 
 def first_kernel(
-    wide, lat_ref, fields, band_ref, rim_ref, push_ref,
+    wide, lat_ref, fields, edges, band_ref, rim_ref, push_ref,
     keep_ref, send_ref, window, halos,
     wide_lat, scaled,
 ):
@@ -449,7 +441,7 @@
 
     for side in range(2):
         halos[side, 0:MEMBERS] = halo_cells(wide, side)
-        halos[side, MEMBERS:] = jnp.concatenate([halo_field(wide, side, 0), pad], 0)
+        halos[side, MEMBERS:] = jnp.concatenate([halo_field(edges, side, 0), pad], 0)
     halos[2, 0:MEMBERS] = wide_lat[base : base + MEMBERS]
     last = wide_lat[base + MEMBERS + RIM : base + MEMBERS + RIM + 1]
     halos[2, MEMBERS:] = jnp.concatenate([last, pad], 0)
@@ -482,7 +474,7 @@
         send_ref[at, :] = send_ref[at, :] + send
 
 
-def first_sum(wide, lat_halo, fields, band, rim, pushed):
+def first_sum(wide, lat_halo, fields, edges, band, rim, pushed):
     return call(
         first_kernel,
         (
@@ -498,6 +490,7 @@
         wide,
         lat_halo,
         fields,
+        edges,
         band,
         rim,
         pushed,
@@ -615,14 +608,14 @@
 
 def early_taps(window, halos, fields):
     return call(
-        early_kernel, shape(EARLY * SPAN * ROWS, LON), taper_scratch(),
+        early_kernel, shape(EARLY * SPAN * ROWS + 32, LON), taper_scratch(),
         window, halos, fields, limit=24, flops=2 * 10**10,
     )
 
 
 def late_taps(window, halos, fields, early):
     return call(
-        late_kernel, shape(TAPS, ROWS, LON), [VMEM((TAPS * ROWS, LON), F32), *taper_scratch()],
+        late_kernel, shape(TAPS, ROWS, LON), [VMEM((TAPE_ROWS, LON), F32), *taper_scratch()],
         window, halos, fields, early, limit=24, flops=10**6,
     )
 
@@ -634,31 +627,30 @@
     first, second, wide, fields = edge_messages(own, taper)
     swaps = ([], [])
     for s in range(strips):
-        for m in range(4):
-            here = 4 * s + m
-            there = here + 4 if s < strips - 1 else (m + 2) % 4
-            swaps[1 - s % 2].extend([(here, there), (there, here)])
-    first = lax.ppermute(first, ("lon", "mem"), swaps[0])
-    second = lax.ppermute(second, ("lon", "mem"), swaps[1])
+        there = (s + 1) % strips
+        swaps[1 - s % 2].extend([(s, there), (there, s)])
+    first = lax.ppermute(first, "lon", swaps[0])
+    second = lax.ppermute(second, "lon", swaps[1])
     band, rim = bands(wide)
     first, second, band, rim = lax.optimization_barrier((first, second, band, rim))
-    message = call(
-        message_kernel, shape(PART, LON, dtype=BF16), [], own, first, second
+    message, edges = call(
+        message_kernel, (shape(PART, LON, dtype=BF16), shape(2 * EDGES, LON)), [],
+        own, first, second,
     )
     gathered = lax.all_gather(message, "mem", axis=0, tiled=True)
 
     down = [(4 * z + m, 4 * z + 4 + m) for z in range(blocks - 1) for m in (0, 1)]
     up = [(4 * z + 4 + m, 4 * z + m) for z in range(blocks - 1) for m in (2, 3)]
-    message = lat_message(gathered, fields)
+    message = lat_message(gathered, fields, edges)
     message, gathered = lax.optimization_barrier((message, gathered))
     lat_halo = lax.ppermute(message, ("lat", "mem"), down + up)
-    pushed_out, scaled, corner, wide = rim_push(gathered, fields, band)
+    pushed_out, scaled, corner, wide = rim_push(gathered, fields, edges, band)
     back = lax.ppermute(
         pushed_out.astype(jnp.float16), ("lat", "mem"), [(b, a) for a, b in down + up]
     )
     pushed = block_push(scaled, corner, band)
     keep, send, window, halos = first_sum(
-        wide, lat_halo, fields, band, rim, pushed
+        wide, lat_halo, fields, edges, band, rim, pushed
     )
     back, send = lax.optimization_barrier((back, send))
     back = back.astype(F32)

time: 58.8 us -> 58.5 us (level)
  blocking collectives: 15.5 us -> 14.7 us
    all_gather x1, blocking collectives: 15.5 us -> 14.7 us  [body(): gathered = lax.all_gather(message, 'mem', axis=0, tiled=True)]
where the time goes in v4:
time: 58.5 us; the launch traced here: 57.7 us
  starting transfers between devices  19.1 us (33%)
  blocking collectives  14.7 us (25%)
  Pallas kernels  11.2 us (19%)
  waiting for transfers between devices  9.26 us (16%)
  other arithmetic  1.71 us (3%)
  local copies, waits for them, and re-layouts  0.96 us (2%)
  between operations  0.8 us (1%)
    all_gather x1, blocking collectives, body(): gathered = lax.all_gather(message, 'mem', axis=0, tiled=True)  14.7 us
    pallas_call x11, Pallas kernels, call(): pl.pallas_call(kernel, out_shape=out_shape, in_specs=[pl.BlockSpec(memory...  11.2 us
    ppermute x1, starting transfers between devices, body(): lat_halo = lax.ppermute(message, ('lat', 'mem'), down + up)  5.21 us
    ppermute x1, waiting for transfers between devices, body(): lax.ppermute(send.astype(jnp.float16), 'mem', [(0, 2), (2, 0), (1, 3), (3...  4.72 us
    ppermute x1, starting transfers between devices, body(): first = lax.ppermute(first, 'lon', swaps[0])  4.27 us
    ppermute x1, starting transfers between devices, body(): more = lax.ppermute(send, 'mem', [(0, 1), (1, 0), (2, 3), (3, 2)])  3.61 us
    ppermute x1, waiting for transfers between devices, body(): lax.ppermute(pushed_out.astype(jnp.float16), ('lat', 'mem'), [(b, a) for...  3 us
    ppermute x1, starting transfers between devices, body(): lax.ppermute(send.astype(jnp.float16), 'mem', [(0, 2), (2, 0), (1, 3), (3...  2.14 us
  transfers between devices with their start and end apart: 6, of which 4 were waited for; matrix products, arithmetic and copies ran while one was open for 0% of the time, Pallas kernels for 18%

profile of v4, /device:TPU:201, one launch (start us, length us, event | category | flops | bytes accessed | tf_op | source)
XLA Modules:
  0.0 57.7 jit_solution(16305136373752516666)
XLA Ops:
  0.6 0.9 %pad_maximum_fusion.own_ref = bf16[352,128]{1,0:T(8,128)(2,1)S(1)} fusion(bf16[16,128]{1,0:T(8,128)(2,1)} %param.6, bf16[16,128]{1,0:T(8,128)(2,1)} %param.5, bf16[320,128]{1,0:T(8,128)(2,1)} %bitcast.5), kind=kLoop, calls=%fused_computation.2 | loop fusion | flops 270336 | bytes 180224 | tf_op jit(solution)/shard_map/concatenate | solution.py:626
  1.6 0.0 copy-start
  1.6 1.0 %copy-done = bf16[289,4,128]{2,1,0:T(4,128)(2,1)S(1)} copy-done((bf16[289,4,128]{2,1,0:T(4,128)(2,1)S(1)}, bf16[289,4,128]{2,1,0:T(4,128)(2,1)}, u32[]{:S(2)}) %copy-start) | copy-done | bytes 295960
  2.5 0.3 shard_map.59
  2.8 4.3 %collective-permute-start = (bf16[64,128]{1,0:T(8,128)(2,1)S(1)}, bf16[64,128]{1,0:T(8,128)(2,1)S(1)}, u32[]{:S(2)}, u32[]{:S(2)}) collective-permute-start(bf16[64,128]{1,0:T(8,128)(2,1)S(1)} %get-tuple-element.34), channel_id=1, source_target_pairs={{32,64},{64,32},{96,128},{128,96},{160,192},{192,160},{224,256},{2... | collective-permute-start | bytes 49160 | tf_op jit(solution)/shard_map/ppermute | solution.py:632
  7.1 2.0 %collective-permute-start.1 = (bf16[64,128]{1,0:T(8,128)(2,1)S(1)}, bf16[64,128]{1,0:T(8,128)(2,1)S(1)}, u32[]{:S(2)}, u32[]{:S(2)}) collective-permute-start(bf16[64,128]{1,0:T(8,128)(2,1)S(1)} %get-tuple-element.35), channel_id=1, source_target_pairs={{0,32},{32,0},{64,96},{96,64},{128,160},{160,128},{192,224},{224,1... | collective-permute-start | bytes 49160 | tf_op jit(solution)/shard_map/ppermute | solution.py:633
  9.1 1.2 %shard_map.60 = (bf16[2560,512]{1,0:T(8,128)(2,1)S(1)}, bf16[384,512]{1,0:T(8,128)(2,1)S(1)}) custom-call(f32[1184,128]{1,0:T(8,128)S(1)} %get-tuple-element.36.wide), custom_call_target="tpu_custom_call" | custom-call | bytes 1048576 | tf_op jit(solution)/shard_map/pallas_call | solution.py:47
  10.3 0.0 collective-permute-done.first_ref
  10.3 1.3 %collective-permute-done.1.second_ref = bf16[64,128]{1,0:T(8,128)(2,1)S(1)} collective-permute-done((bf16[64,128]{1,0:T(8,128)(2,1)S(1)}, bf16[64,128]{1,0:T(8,128)(2,1)S(1)}, u32[]{:S(2)}, u32[]{:S(2)}) %collective-permute-start.1) | collective-permute-done | bytes 16416 | tf_op jit(solution)/shard_map/ppermute | solution.py:633
  11.6 14.7 %all_gather.3.x_ref = bf16[1472,128]{1,0:T(8,128)(2,1)S(1)} all-gather(bf16[368,128]{1,0:T(8,128)(2,1)S(1)} %get-tuple-element.41), channel_id=1, replica_groups=mesh['lon'=16,'lat'=8,'mem'=4] {'mem'}, dimensions={0}, use_global_device_ids=true | all-gather | bytes 471040 | tf_op jit(solution)/shard_map/all_gather | solution.py:640
  26.3 0.1 shard_map.62
  26.3 5.2 %collective-permute-start.3 = (bf16[736,128]{1,0:T(8,128)(2,1)S(1)}, bf16[736,128]{1,0:T(8,128)(2,1)S(1)}, u32[]{:S(2)}, u32[]{:S(2)}) collective-permute-start(bf16[736,128]{1,0:T(8,128)(2,1)S(1)} %shard_map.62), channel_id=1, source_target_pairs={{0,4},{1,5},{4,8},{5,9},{8,12},{9,13},{12,16},{13,17},{16,20},{17,... | collective-permute-start | bytes 565256 | tf_op jit(solution)/shard_map/ppermute | solution.py:646
  31.6 0.9 %shard_map.63 = (f32[656,128]{1,0:T(8,128)S(1)}, bf16[160,640]{1,0:T(8,128)(2,1)S(1)}, bf16[2560,128]{1,0:T(8,128)(2,1)S(1)}, f32[1472,128]{1,0:T(8,128)S(1)}) custom-call(bf16[1472,128]{1,0:T(8,128)(2,1)S(1)} %all_gather.3.x_ref, f32[32,128]{1,0:T(8,128)S(1)} %get-tuple-element.42.fields, f32[128,128]{1,0:T(8,128)S(1)} %get-tuple-element.43.edges, ...), custom_call_target="tpu_custom_call" | custom-call | flops 1000000 | bytes 1048576 | tf_op jit(solution)/shard_map/pallas_call | solution.py:47
  32.5 1.9 %collective-permute-start.2 = (f16[656,128]{1,0:T(8,128)(2,1)S(1)}, f16[656,128]{1,0:T(8,128)(2,1)S(1)}, u32[]{:S(2)}, u32[]{:S(2)}) collective-permute-start(f16[656,128]{1,0:T(8,128)(2,1)S(1)} %convert_element_type.12), channel_id=1, source_target_pairs={{4,0},{5,1},{8,4},{9,5},{12,8},{13,9},{16,12},{17,13},{20,16},{21,... | collective-permute-start | bytes 503816 | tf_op jit(solution)/shard_map/ppermute | solution.py:648
  34.5 1.7 %shard_map.64.push_ref = f32[1280,128]{1,0:T(8,128)S(1)} custom-call(bf16[160,640]{1,0:T(8,128)(2,1)S(1)} %get-tuple-element.50.scaled, bf16[2560,128]{1,0:T(8,128)(2,1)S(1)} %get-tuple-element.51.corner, bf16[2560,512]{1,0:T(8,128)(2,1)S(1)} %get-tuple-element.45.band_ref), custom_call_target="tpu_custom_call" | custom-call | flops 1000000 | bytes 1048576 | tf_op jit(solution)/shard_map/pallas_call | solution.py:47
  36.2 0.0 collective-permute-done.3.lat_ref
  36.2 1.4 %shard_map.65 = (f32[640,128]{1,0:T(8,128)S(1)}, f32[640,128]{1,0:T(8,128)S(1)}, f32[20,88,128]{2,1,0:T(8,128)S(1)}, f32[3,88,128]{2,1,0:T(8,128)S(1)}) custom-call(f32[1472,128]{1,0:T(8,128)S(1)} %get-tuple-element.47.wide, bf16[736,128]{1,0:T(8,128)(2,1)S(1)} %collective-permute-done.3.lat_ref, f32[32,128]{1,0:T(8,128)S(1)} %get-tuple-element.42.fields, ...), custom_call_target="tpu_custom_call" | custom-call | flops 1000000 | bytes 1048576 | tf_op jit(solution)/shard_map/pallas_call | solution.py:47
  37.6 3.0 %collective-permute-done.2 = f16[656,128]{1,0:T(8,128)(2,1)S(1)} collective-permute-done((f16[656,128]{1,0:T(8,128)(2,1)S(1)}, f16[656,128]{1,0:T(8,128)(2,1)S(1)}, u32[]{:S(2)}, u32[]{:S(2)}) %collective-permute-start.2) | collective-permute-done | bytes 167968 | tf_op jit(solution)/shard_map/ppermute | solution.py:648
  40.7 3.6 %collective-permute-start.4 = (f32[640,128]{1,0:T(8,128)S(1)}, f32[640,128]{1,0:T(8,128)S(1)}, u32[]{:S(2)}, u32[]{:S(2)}) collective-permute-start(f32[640,128]{1,0:T(8,128)S(1)} %shard_map.66), channel_id=1, source_target_pairs={{0,1},{1,0},{2,3},{3,2},{4,5},{5,4},{6,7},{7,6},{8,9},{9,8},{10,11... | collective-permute-start | bytes 983048 | tf_op jit(solution)/shard_map/ppermute | solution.py:659
  44.3 1.0 %shard_map.67.early = f32[168,128]{1,0:T(8,128)S(1)} custom-call(f32[20,88,128]{2,1,0:T(8,128)S(1)} %get-tuple-element.56.window, f32[3,88,128]{2,1,0:T(8,128)S(1)} %get-tuple-element.57.halos, f32[32,128]{1,0:T(8,128)S(1)} %get-tuple-element.42.fields), custom_call_target="tpu_custom_call" | custom-call | flops 20000000000 | bytes 1048576 | tf_op jit(solution)/shard_map/pallas_call | solution.py:47
  45.3 0.3 collective-permute-done.4.more_ref
  45.6 0.2 shard_map.68
  45.8 2.1 %collective-permute-start.5 = (f16[336,128]{1,0:T(8,128)(2,1)S(1)}, f16[336,128]{1,0:T(8,128)(2,1)S(1)}, u32[]{:S(2)}, u32[]{:S(2)}) collective-permute-start(f16[336,128]{1,0:T(8,128)(2,1)S(1)} %convert_element_type.14), channel_id=1, source_target_pairs={{0,2},{2,0},{1,3},{3,1},{4,6},{6,4},{5,7},{7,5},{8,10},{10,8},{9,1... | collective-permute-start | bytes 258056 | tf_op jit(solution)/shard_map/ppermute | solution.py:663
  48.0 4.2 %shard_map.69 = f32[289,4,128]{2,1,0:T(4,128)} custom-call(f32[20,88,128]{2,1,0:T(8,128)S(1)} %get-tuple-element.56.window, f32[3,88,128]{2,1,0:T(8,128)S(1)} %get-tuple-element.57.halos, f32[32,128]{1,0:T(8,128)S(1)} %get-tuple-element.42.fields, f32[168,128]{1,0:T(8,128)S(1)} %shard_map.67.early), custom_call_target="tpu_custom_call" | custom-call | flops 1000000 | bytes 1048576 | tf_op jit(solution)/shard_map/pallas_call | solution.py:47
  52.2 4.7 %collective-permute-done.5 = f16[336,128]{1,0:T(8,128)(2,1)S(1)} collective-permute-done((f16[336,128]{1,0:T(8,128)(2,1)S(1)}, f16[336,128]{1,0:T(8,128)(2,1)S(1)}, u32[]{:S(2)}, u32[]{:S(2)}) %collective-permute-start.5) | collective-permute-done | bytes 86048 | tf_op jit(solution)/shard_map/ppermute | solution.py:663
  57.0 0.7 %fusion = f32[320,128]{1,0:T(8,128)} fusion(f32[320,128]{1,0:T(8,128)S(1)} %get-tuple-element.64, f32[336,128]{1,0:T(8,128)S(1)} %convert_element_type.15, f32[128]{0:T(128)S(1)} %fusion.2), kind=kLoop, calls=%fused_computation.1 | loop fusion | flops 81920 | bytes 492032 | tf_op jit(solution)/shard_map/add | solution.py:667
  (7 shorter events, 0.2 us)
Async XLA Ops:
  1.6 1.0 %copy-start = (bf16[289,4,128]{2,1,0:T(4,128)(2,1)S(1)}, bf16[289,4,128]{2,1,0:T(4,128)(2,1)}, u32[]{:S(2)}) copy-start(bf16[289,4,128]{2,1,0:T(4,128)(2,1)} %taper_ref.1) | copy-start | bytes 887812
  2.8 7.5 %collective-permute-start = (bf16[64,128]{1,0:T(8,128)(2,1)S(1)}, bf16[64,128]{1,0:T(8,128)(2,1)S(1)}, u32[]{:S(2)}, u32[]{:S(2)}) collective-permute-start(bf16[64,128]{1,0:T(8,128)(2,1)S(1)} %get-tuple-element.34), channel_id=1, source_target_pairs={{32,64},{64,32},{96,128},{128,96},{160,192},{192,160},{224,256},{2... | collective-permute-start | bytes 49160 | tf_op jit(solution)/shard_map/ppermute | solution.py:632
  7.1 4.5 %collective-permute-start.1 = (bf16[64,128]{1,0:T(8,128)(2,1)S(1)}, bf16[64,128]{1,0:T(8,128)(2,1)S(1)}, u32[]{:S(2)}, u32[]{:S(2)}) collective-permute-start(bf16[64,128]{1,0:T(8,128)(2,1)S(1)} %get-tuple-element.35), channel_id=1, source_target_pairs={{0,32},{32,0},{64,96},{96,64},{128,160},{160,128},{192,224},{224,1... | collective-permute-start | bytes 49160 | tf_op jit(solution)/shard_map/ppermute | solution.py:633
  26.3 9.8 %collective-permute-start.3 = (bf16[736,128]{1,0:T(8,128)(2,1)S(1)}, bf16[736,128]{1,0:T(8,128)(2,1)S(1)}, u32[]{:S(2)}, u32[]{:S(2)}) collective-permute-start(bf16[736,128]{1,0:T(8,128)(2,1)S(1)} %shard_map.62), channel_id=1, source_target_pairs={{0,4},{1,5},{4,8},{5,9},{8,12},{9,13},{12,16},{13,17},{16,20},{17,... | collective-permute-start | bytes 565256 | tf_op jit(solution)/shard_map/ppermute | solution.py:646
  32.5 8.1 %collective-permute-start.2 = (f16[656,128]{1,0:T(8,128)(2,1)S(1)}, f16[656,128]{1,0:T(8,128)(2,1)S(1)}, u32[]{:S(2)}, u32[]{:S(2)}) collective-permute-start(f16[656,128]{1,0:T(8,128)(2,1)S(1)} %convert_element_type.12), channel_id=1, source_target_pairs={{4,0},{5,1},{8,4},{9,5},{12,8},{13,9},{16,12},{17,13},{20,16},{21,... | collective-permute-start | bytes 503816 | tf_op jit(solution)/shard_map/ppermute | solution.py:648
  40.7 4.8 %collective-permute-start.4 = (f32[640,128]{1,0:T(8,128)S(1)}, f32[640,128]{1,0:T(8,128)S(1)}, u32[]{:S(2)}, u32[]{:S(2)}) collective-permute-start(f32[640,128]{1,0:T(8,128)S(1)} %shard_map.66), channel_id=1, source_target_pairs={{0,1},{1,0},{2,3},{3,2},{4,5},{5,4},{6,7},{7,6},{8,9},{9,8},{10,11... | collective-permute-start | bytes 983048 | tf_op jit(solution)/shard_map/ppermute | solution.py:659
  45.8 11.1 %collective-permute-start.5 = (f16[336,128]{1,0:T(8,128)(2,1)S(1)}, f16[336,128]{1,0:T(8,128)(2,1)S(1)}, u32[]{:S(2)}, u32[]{:S(2)}) collective-permute-start(f16[336,128]{1,0:T(8,128)(2,1)S(1)} %convert_element_type.14), channel_id=1, source_target_pairs={{0,2},{2,0},{1,3},{3,1},{4,6},{6,4},{5,7},{7,5},{8,10},{10,8},{9,1... | collective-permute-start | bytes 258056 | tf_op jit(solution)/shard_map/ppermute | solution.py:663

commit v5 on v4

--- a/solution.py
+++ b/solution.py
@@ -22,7 +22,7 @@
 PART = CELLS + 48
 HALO = 3 * LON
 MAIN = WIN * LON
-BACK = MEMBERS * RIM
+BACK = 2 * GROUP * RIM
 LATROWS = MEMBERS * RIM + MEMBERS + RIM + 8
 TAPE_ROWS = 1184
 F32 = jnp.float32
@@ -301,7 +301,9 @@
     ref[rows : rows + 16] = power
 
 
-def rim_push_kernel(x_ref, fields, edges, band_ref, rim_ref, scaled, corner, wide):
+def rim_push_kernel(
+    x_ref, fields, edges, band_ref, near_ref, cross_ref, scaled, corner, wide
+):
     mem = lax.axis_index("mem")
     wide[...] = x_ref[...].astype(F32)
     for i in range(ROWS):
@@ -343,24 +345,27 @@
             edge.append(tile)
         corner[j * LON : j * LON + 16] = jnp.concatenate([edge[1], zero], 0).astype(BF16)
         corner[j * LON + 112 : j * LON + 128] = jnp.concatenate([zero, edge[0]], 0).astype(BF16)
-    zeros = jnp.zeros((MEMBERS, LON), F32)
+    zeros = jnp.zeros((2 * GROUP, LON), F32)
 
     @pl.when((mem == 1) | (mem == 2))
     def _():
         first = jnp.where(mem == 1, 0, ROWS)
         for k in range(ROWS):
-            rim_ref[pl.ds(first + k, MEMBERS, stride=RIM), :] = zeros
+            near_ref[pl.ds(first + k, 2 * GROUP, stride=RIM), :] = zeros
+            cross_ref[pl.ds(first + k, 2 * GROUP, stride=RIM), :] = zeros
 
     first, steps = rim_steps(mem)
 
     @pl.loop(first, first + steps)
     def _(step):
-        total = pushes(scaled, corner, band_ref, step)
+        near, cross = by_core(mem, pushes(scaled, corner, band_ref, step))
         for k in range(STEP):
-            row = pl.ds(ring_row(mem, step * STEP + k) - CLAT, MEMBERS, stride=RIM)
-            rim_ref[row, :] = total[:, k * LON : (k + 1) * LON]
-
-    scale_down(rim_ref, BACK)
+            row = pl.ds(ring_row(mem, step * STEP + k) - CLAT, 2 * GROUP, stride=RIM)
+            near_ref[row, :] = near[:, k * LON : (k + 1) * LON]
+            cross_ref[row, :] = cross[:, k * LON : (k + 1) * LON]
+
+    scale_down(near_ref, BACK)
+    scale_down(cross_ref, BACK)
 
 
 def block_push_kernel(scaled, corner, band_ref, out_ref):
@@ -390,6 +395,7 @@
     return call(
         rim_push_kernel,
         (
+            shape(BACK + 16, LON),
             shape(BACK + 16, LON),
             shape(2 * MEMBERS, (ROWS + 1) * LON, dtype=BF16),
             shape(MAIN, LON, dtype=BF16),
@@ -498,42 +504,38 @@
     )
 
 
-def add_back(mem, take, half, at, back_ref, fields, target):
-    first = jnp.where(mem < 2, RIM, 0)
+def merge_kernel(near_ref, cross_ref, fields, out_ref):
+    first = jnp.where(lax.axis_index("mem") < 2, RIM, 0)
     rows = fields[pl.ds(pl.multiple_of(first, 8), RIM), :] * SHARE
-    rows = rows * jnp.exp2(back_ref[BACK : BACK + 1])
-    start = (2 * half + take) * GROUP * RIM
-    for m in range(GROUP):
-        source = pl.ds(pl.multiple_of(start + m * RIM, 8), RIM)
-        to = pl.ds(pl.multiple_of(at + m * CLAT + first, 8), RIM)
-        target[to, :] = target[to, :] + back_ref[source, :] * rows
-
-
-def near_kernel(part_ref, back_ref, fields, send_ref):
-    mem = lax.axis_index("mem")
-    send_ref[...] = part_ref[...]
-    for half in range(2):
-        add_back(mem, 1 - mem % 2, half, half * CELLS, back_ref, fields, send_ref)
-
-
-def near_parts(part, back, fields):
-    return call(near_kernel, shape(2 * CELLS, LON), [], part, back, fields)
-
-
-def far_kernel(keep_ref, more_ref, back_ref, fields, mine_ref, send_ref):
+    near = rows * jnp.exp2(near_ref[BACK : BACK + 1])
+    cross = rows * jnp.exp2(cross_ref[BACK : BACK + 1])
+    for at in range(0, BACK, RIM):
+        out_ref[at : at + RIM] = (
+            near_ref[at : at + RIM] * near + cross_ref[at : at + RIM] * cross
+        )
+
+
+def merged(near, cross, fields):
+    return call(merge_kernel, shape(BACK, LON), [], near, cross, fields, flops=29 * 10**8)
+
+
+def far_kernel(keep_ref, more_ref, back_ref, mine_ref, send_ref):
     mem = lax.axis_index("mem")
     far = mem // 2
+    first = jnp.where(mem < 2, RIM, 0)
     for take, target in ((far, mine_ref), (1 - far, send_ref)):
         at = pl.ds(pl.multiple_of(take * CELLS, 8), CELLS)
         target[0:CELLS] = keep_ref[at, :] + more_ref[at, :]
-        add_back(mem, mem % 2, take, 0, back_ref, fields, target)
+        for m in range(GROUP):
+            source = pl.ds(pl.multiple_of(take * GROUP * RIM + m * RIM, 8), RIM)
+            to = pl.ds(pl.multiple_of(m * CLAT + first, 8), RIM)
+            target[to, :] = target[to, :] + back_ref[source, :]
     scale_down(send_ref, CELLS)
 
 
-def far_parts(keep, more, back, fields):
-    return call(
-        far_kernel, (shape(CELLS, LON), shape(CELLS + 16, LON)), [],
-        keep, more, back, fields,
+def far_parts(keep, more, back):
+    return call(
+        far_kernel, (shape(CELLS, LON), shape(CELLS + 16, LON)), [], keep, more, back
     )
 
 
@@ -609,7 +611,7 @@
 def early_taps(window, halos, fields):
     return call(
         early_kernel, shape(EARLY * SPAN * ROWS + 32, LON), taper_scratch(),
-        window, halos, fields, limit=24, flops=2 * 10**10,
+        window, halos, fields, limit=24, flops=10**6,
     )
 
 
@@ -644,22 +646,20 @@
     message = lat_message(gathered, fields, edges)
     message, gathered = lax.optimization_barrier((message, gathered))
     lat_halo = lax.ppermute(message, ("lat", "mem"), down + up)
-    pushed_out, scaled, corner, wide = rim_push(gathered, fields, edges, band)
-    back = lax.ppermute(
-        pushed_out.astype(jnp.float16), ("lat", "mem"), [(b, a) for a, b in down + up]
-    )
+    near, cross, scaled, corner, wide = rim_push(gathered, fields, edges, band)
+    half = jnp.float16
+    near = lax.ppermute(near.astype(half), ("lat", "mem"), [(b, a) for a, b in down + up])
+    cross = lax.ppermute(cross.astype(half), ("lat", "mem"), [(b, a ^ 1) for a, b in down + up])
     pushed = block_push(scaled, corner, band)
     keep, send, window, halos = first_sum(
         wide, lat_halo, fields, edges, band, rim, pushed
     )
-    back, send = lax.optimization_barrier((back, send))
-    back = back.astype(F32)
-    send = near_parts(send, back, fields)
-    send, window = lax.optimization_barrier((send, window))
     more = lax.ppermute(send, "mem", [(0, 1), (1, 0), (2, 3), (3, 2)])
     early = early_taps(window, halos, fields)
+    near, cross, early = lax.optimization_barrier((near, cross, early))
+    back = merged(near.astype(F32), cross.astype(F32), fields)
     more, early = lax.optimization_barrier((more, early))
-    mine, send = far_parts(keep, more, back, fields)
+    mine, send = far_parts(keep, more, back)
     half = lax.ppermute(send.astype(jnp.float16), "mem", [(0, 2), (2, 0), (1, 3), (3, 1)])
     mine, early = lax.optimization_barrier((mine, early))
     grad_taper = late_taps(window, halos, fields, early)

time: 58.5 us -> 58.5 us (level)
  the two profiles are of different devices: /device:TPU:201 before, /device:TPU:176 now
where the time goes in v5:
time: 58.5 us; the launch traced here: 58.1 us
  starting transfers between devices  23.2 us (40%)
  blocking collectives  11.2 us (19%)
  Pallas kernels  11.1 us (19%)
  waiting for transfers between devices  9.01 us (15%)
  other arithmetic  1.71 us (3%)
  local copies, waits for them, and re-layouts  0.96 us (2%)
  between operations  0.84 us (1%)
    all_gather x1, blocking collectives, body(): gathered = lax.all_gather(message, 'mem', axis=0, tiled=True)  11.2 us
    pallas_call x11, Pallas kernels, call(): pl.pallas_call(kernel, out_shape=out_shape, in_specs=[pl.BlockSpec(memory...  11.1 us
    ppermute x1, waiting for transfers between devices, body(): lax.ppermute(send.astype(jnp.float16), 'mem', [(0, 2), (2, 0), (1, 3), (3...  6 us
    ppermute x1, starting transfers between devices, body(): lax.ppermute(near.astype(half), ('lat', 'mem'), [(b, a) for a, b in down...  5.51 us
    ppermute x1, starting transfers between devices, body(): first = lax.ppermute(first, 'lon', swaps[0])  5.45 us
    ppermute x1, starting transfers between devices, body(): lax.ppermute(cross.astype(half), ('lat', 'mem'), [(b, a ^ 1) for a, b in...  4.59 us
    ppermute x1, waiting for transfers between devices, body(): second = lax.ppermute(second, 'lon', swaps[1])  2.47 us
    ppermute x1, starting transfers between devices, body(): lax.ppermute(send.astype(jnp.float16), 'mem', [(0, 2), (2, 0), (1, 3), (3...  1.92 us
  transfers between devices with their start and end apart: 7, of which 3 were waited for; matrix products, arithmetic and copies ran while one was open for 0% of the time, Pallas kernels for 18%

profile of v5, /device:TPU:176, one launch (start us, length us, event | category | flops | bytes accessed | tf_op | source)
XLA Modules:
  0.0 58.1 jit_solution(10891215426174183406)
XLA Ops:
  0.6 0.9 %pad_maximum_fusion.own_ref = bf16[352,128]{1,0:T(8,128)(2,1)S(1)} fusion(bf16[16,128]{1,0:T(8,128)(2,1)} %param.6, bf16[16,128]{1,0:T(8,128)(2,1)} %param.5, bf16[320,128]{1,0:T(8,128)(2,1)} %bitcast.5), kind=kLoop, calls=%fused_computation.2 | loop fusion | flops 270336 | bytes 180224 | tf_op jit(solution)/shard_map/concatenate | solution.py:628
  1.6 0.0 copy-start
  1.6 1.0 %copy-done = bf16[289,4,128]{2,1,0:T(4,128)(2,1)S(1)} copy-done((bf16[289,4,128]{2,1,0:T(4,128)(2,1)S(1)}, bf16[289,4,128]{2,1,0:T(4,128)(2,1)}, u32[]{:S(2)}) %copy-start) | copy-done | bytes 295960
  2.5 0.3 shard_map.59
  2.8 5.5 %collective-permute-start = (bf16[64,128]{1,0:T(8,128)(2,1)S(1)}, bf16[64,128]{1,0:T(8,128)(2,1)S(1)}, u32[]{:S(2)}, u32[]{:S(2)}) collective-permute-start(bf16[64,128]{1,0:T(8,128)(2,1)S(1)} %get-tuple-element.34), channel_id=1, source_target_pairs={{32,64},{64,32},{96,128},{128,96},{160,192},{192,160},{224,256},{2... | collective-permute-start | bytes 49160 | tf_op jit(solution)/shard_map/ppermute | solution.py:634
  8.3 1.9 %collective-permute-start.1 = (bf16[64,128]{1,0:T(8,128)(2,1)S(1)}, bf16[64,128]{1,0:T(8,128)(2,1)S(1)}, u32[]{:S(2)}, u32[]{:S(2)}) collective-permute-start(bf16[64,128]{1,0:T(8,128)(2,1)S(1)} %get-tuple-element.35), channel_id=1, source_target_pairs={{0,32},{32,0},{64,96},{96,64},{128,160},{160,128},{192,224},{224,1... | collective-permute-start | bytes 49160 | tf_op jit(solution)/shard_map/ppermute | solution.py:635
  10.2 1.2 %shard_map.60 = (bf16[2560,512]{1,0:T(8,128)(2,1)S(1)}, bf16[384,512]{1,0:T(8,128)(2,1)S(1)}) custom-call(f32[1184,128]{1,0:T(8,128)S(1)} %get-tuple-element.36.wide), custom_call_target="tpu_custom_call" | custom-call | bytes 1048576 | tf_op jit(solution)/shard_map/pallas_call | solution.py:47
  11.4 0.0 collective-permute-done.first_ref
  11.4 2.5 %collective-permute-done.1.second_ref = bf16[64,128]{1,0:T(8,128)(2,1)S(1)} collective-permute-done((bf16[64,128]{1,0:T(8,128)(2,1)S(1)}, bf16[64,128]{1,0:T(8,128)(2,1)S(1)}, u32[]{:S(2)}, u32[]{:S(2)}) %collective-permute-start.1) | collective-permute-done | bytes 16416 | tf_op jit(solution)/shard_map/ppermute | solution.py:635
  13.9 11.2 %all_gather.3.x_ref = bf16[1472,128]{1,0:T(8,128)(2,1)S(1)} all-gather(bf16[368,128]{1,0:T(8,128)(2,1)S(1)} %get-tuple-element.41), channel_id=1, replica_groups=mesh['lon'=16,'lat'=8,'mem'=4] {'mem'}, dimensions={0}, use_global_device_ids=true | all-gather | bytes 471040 | tf_op jit(solution)/shard_map/all_gather | solution.py:642
  25.1 0.1 shard_map.62
  25.2 1.9 %collective-permute-start.2 = (bf16[736,128]{1,0:T(8,128)(2,1)S(1)}, bf16[736,128]{1,0:T(8,128)(2,1)S(1)}, u32[]{:S(2)}, u32[]{:S(2)}) collective-permute-start(bf16[736,128]{1,0:T(8,128)(2,1)S(1)} %shard_map.62), channel_id=1, source_target_pairs={{0,4},{1,5},{4,8},{5,9},{8,12},{9,13},{12,16},{13,17},{16,20},{17,... | collective-permute-start | bytes 565256 | tf_op jit(solution)/shard_map/ppermute | solution.py:648
  27.2 0.9 %shard_map.63 = (f32[336,128]{1,0:T(8,128)S(1)}, f32[336,128]{1,0:T(8,128)S(1)}, bf16[160,640]{1,0:T(8,128)(2,1)S(1)}, bf16[2560,128]{1,0:T(8,128)(2,1)S(1)}, f32[1472,128]{1,0:T(8,128)S(1)}) custom-call(bf16[1472,128]{1,0:T(8,128)(2,1)S(1)} %all_gather.3.x_ref, f32[32,128]{1,0:T(8,128)S(1)} %get-tuple-element.42.fields, ...), custom_call_target="tpu_custom_call" | custom-call | flops 1000000 | bytes 1048576 | tf_op jit(solution)/shard_map/pallas_call | solution.py:47
  28.1 4.6 %collective-permute-start.5 = (f16[336,128]{1,0:T(8,128)(2,1)S(1)}, f16[336,128]{1,0:T(8,128)(2,1)S(1)}, u32[]{:S(2)}, u32[]{:S(2)}) collective-permute-start(f16[336,128]{1,0:T(8,128)(2,1)S(1)} %convert_element_type.19), channel_id=1, source_target_pairs={{4,1},{5,0},{8,5},{9,4},{12,9},{13,8},{16,13},{17,12},{20,17},{21,... | collective-permute-start | bytes 258056 | tf_op jit(solution)/shard_map/ppermute | solution.py:652
  32.7 5.5 %collective-permute-start.4 = (f16[336,128]{1,0:T(8,128)(2,1)S(1)}, f16[336,128]{1,0:T(8,128)(2,1)S(1)}, u32[]{:S(2)}, u32[]{:S(2)}) collective-permute-start(f16[336,128]{1,0:T(8,128)(2,1)S(1)} %convert_element_type.18), channel_id=1, source_target_pairs={{4,0},{5,1},{8,4},{9,5},{12,8},{13,9},{16,12},{17,13},{20,16},{21,... | collective-permute-start | bytes 258056 | tf_op jit(solution)/shard_map/ppermute | solution.py:651
  38.3 1.7 %shard_map.64.push_ref = f32[1280,128]{1,0:T(8,128)S(1)} custom-call(bf16[160,640]{1,0:T(8,128)(2,1)S(1)} %get-tuple-element.49.scaled, bf16[2560,128]{1,0:T(8,128)(2,1)S(1)} %get-tuple-element.50.corner, bf16[2560,512]{1,0:T(8,128)(2,1)S(1)} %get-tuple-element.45.band_ref), custom_call_target="tpu_custom_call" | custom-call | flops 1000000 | bytes 1048576 | tf_op jit(solution)/shard_map/pallas_call | solution.py:47
  40.0 0.0 collective-permute-done.2.lat_ref
  40.0 1.4 %shard_map.65 = (f32[640,128]{1,0:T(8,128)S(1)}, f32[640,128]{1,0:T(8,128)S(1)}, f32[20,88,128]{2,1,0:T(8,128)S(1)}, f32[3,88,128]{2,1,0:T(8,128)S(1)}) custom-call(f32[1472,128]{1,0:T(8,128)S(1)} %get-tuple-element.46.wide, bf16[736,128]{1,0:T(8,128)(2,1)S(1)} %collective-permute-done.2.lat_ref, f32[32,128]{1,0:T(8,128)S(1)} %get-tuple-element.42.fields, ...), custom_call_target="tpu_custom_call" | custom-call | flops 1000000 | bytes 1048576 | tf_op jit(solution)/shard_map/pallas_call | solution.py:47
  41.4 1.9 %collective-permute-start.3 = (f32[640,128]{1,0:T(8,128)S(1)}, f32[640,128]{1,0:T(8,128)S(1)}, u32[]{:S(2)}, u32[]{:S(2)}) collective-permute-start(f32[640,128]{1,0:T(8,128)S(1)} %get-tuple-element.54), channel_id=1, source_target_pairs={{0,1},{1,0},{2,3},{3,2},{4,5},{5,4},{6,7},{7,6},{8,9},{9,8},{10,11... | collective-permute-start | bytes 983048 | tf_op jit(solution)/shard_map/ppermute | solution.py:657
  43.4 1.0 %shard_map.66.early = f32[168,128]{1,0:T(8,128)S(1)} custom-call(f32[20,88,128]{2,1,0:T(8,128)S(1)} %get-tuple-element.51.window, f32[3,88,128]{2,1,0:T(8,128)S(1)} %get-tuple-element.52.halos, f32[32,128]{1,0:T(8,128)S(1)} %get-tuple-element.42.fields), custom_call_target="tpu_custom_call" | custom-call | flops 1000000 | bytes 1048576 | tf_op jit(solution)/shard_map/pallas_call | solution.py:47
  44.3 0.0 collective-permute-done.5
  44.3 0.0 collective-permute-done.4
  44.4 0.5 collective-permute-done.3.more_ref
  45.0 0.2 shard_map.68
  45.2 1.9 %collective-permute-start.6 = (f16[336,128]{1,0:T(8,128)(2,1)S(1)}, f16[336,128]{1,0:T(8,128)(2,1)S(1)}, u32[]{:S(2)}, u32[]{:S(2)}) collective-permute-start(f16[336,128]{1,0:T(8,128)(2,1)S(1)} %convert_element_type.22), channel_id=1, source_target_pairs={{0,2},{2,0},{1,3},{3,1},{4,6},{6,4},{5,7},{7,5},{8,10},{10,8},{9,1... | collective-permute-start | bytes 258056 | tf_op jit(solution)/shard_map/ppermute | solution.py:663
  47.2 4.2 %shard_map.69 = f32[289,4,128]{2,1,0:T(4,128)} custom-call(f32[20,88,128]{2,1,0:T(8,128)S(1)} %get-tuple-element.51.window, f32[3,88,128]{2,1,0:T(8,128)S(1)} %get-tuple-element.52.halos, f32[32,128]{1,0:T(8,128)S(1)} %get-tuple-element.42.fields, f32[168,128]{1,0:T(8,128)S(1)} %shard_map.66.early), custom_call_target="tpu_custom_call" | custom-call | flops 1000000 | bytes 1048576 | tf_op jit(solution)/shard_map/pallas_call | solution.py:47
  51.4 6.0 %collective-permute-done.6 = f16[336,128]{1,0:T(8,128)(2,1)S(1)} collective-permute-done((f16[336,128]{1,0:T(8,128)(2,1)S(1)}, f16[336,128]{1,0:T(8,128)(2,1)S(1)}, u32[]{:S(2)}, u32[]{:S(2)}) %collective-permute-start.6) | collective-permute-done | bytes 86048 | tf_op jit(solution)/shard_map/ppermute | solution.py:663
  57.4 0.7 %fusion = f32[320,128]{1,0:T(8,128)} fusion(f32[320,128]{1,0:T(8,128)S(1)} %get-tuple-element.64, f32[336,128]{1,0:T(8,128)S(1)} %convert_element_type.23, f32[128]{0:T(128)S(1)} %fusion.2), kind=kLoop, calls=%fused_computation.1 | loop fusion | flops 81920 | bytes 492032 | tf_op jit(solution)/shard_map/add | solution.py:667
  (9 shorter events, 0.1 us)
Async XLA Ops:
  1.6 1.0 %copy-start = (bf16[289,4,128]{2,1,0:T(4,128)(2,1)S(1)}, bf16[289,4,128]{2,1,0:T(4,128)(2,1)}, u32[]{:S(2)}) copy-start(bf16[289,4,128]{2,1,0:T(4,128)(2,1)} %taper_ref.1) | copy-start | bytes 887812
  2.8 8.6 %collective-permute-start = (bf16[64,128]{1,0:T(8,128)(2,1)S(1)}, bf16[64,128]{1,0:T(8,128)(2,1)S(1)}, u32[]{:S(2)}, u32[]{:S(2)}) collective-permute-start(bf16[64,128]{1,0:T(8,128)(2,1)S(1)} %get-tuple-element.34), channel_id=1, source_target_pairs={{32,64},{64,32},{96,128},{128,96},{160,192},{192,160},{224,256},{2... | collective-permute-start | bytes 49160 | tf_op jit(solution)/shard_map/ppermute | solution.py:634
  8.3 5.6 %collective-permute-start.1 = (bf16[64,128]{1,0:T(8,128)(2,1)S(1)}, bf16[64,128]{1,0:T(8,128)(2,1)S(1)}, u32[]{:S(2)}, u32[]{:S(2)}) collective-permute-start(bf16[64,128]{1,0:T(8,128)(2,1)S(1)} %get-tuple-element.35), channel_id=1, source_target_pairs={{0,32},{32,0},{64,96},{96,64},{128,160},{160,128},{192,224},{224,1... | collective-permute-start | bytes 49160 | tf_op jit(solution)/shard_map/ppermute | solution.py:635
  25.2 14.8 %collective-permute-start.2 = (bf16[736,128]{1,0:T(8,128)(2,1)S(1)}, bf16[736,128]{1,0:T(8,128)(2,1)S(1)}, u32[]{:S(2)}, u32[]{:S(2)}) collective-permute-start(bf16[736,128]{1,0:T(8,128)(2,1)S(1)} %shard_map.62), channel_id=1, source_target_pairs={{0,4},{1,5},{4,8},{5,9},{8,12},{9,13},{12,16},{13,17},{16,20},{17,... | collective-permute-start | bytes 565256 | tf_op jit(solution)/shard_map/ppermute | solution.py:648
  28.1 16.2 %collective-permute-start.5 = (f16[336,128]{1,0:T(8,128)(2,1)S(1)}, f16[336,128]{1,0:T(8,128)(2,1)S(1)}, u32[]{:S(2)}, u32[]{:S(2)}) collective-permute-start(f16[336,128]{1,0:T(8,128)(2,1)S(1)} %convert_element_type.19), channel_id=1, source_target_pairs={{4,1},{5,0},{8,5},{9,4},{12,9},{13,8},{16,13},{17,12},{20,17},{21,... | collective-permute-start | bytes 258056 | tf_op jit(solution)/shard_map/ppermute | solution.py:652
  32.7 11.6 %collective-permute-start.4 = (f16[336,128]{1,0:T(8,128)(2,1)S(1)}, f16[336,128]{1,0:T(8,128)(2,1)S(1)}, u32[]{:S(2)}, u32[]{:S(2)}) collective-permute-start(f16[336,128]{1,0:T(8,128)(2,1)S(1)} %convert_element_type.18), channel_id=1, source_target_pairs={{4,0},{5,1},{8,4},{9,5},{12,8},{13,9},{16,12},{17,13},{20,16},{21,... | collective-permute-start | bytes 258056 | tf_op jit(solution)/shard_map/ppermute | solution.py:651
  41.4 3.5 %collective-permute-start.3 = (f32[640,128]{1,0:T(8,128)S(1)}, f32[640,128]{1,0:T(8,128)S(1)}, u32[]{:S(2)}, u32[]{:S(2)}) collective-permute-start(f32[640,128]{1,0:T(8,128)S(1)} %get-tuple-element.54), channel_id=1, source_target_pairs={{0,1},{1,0},{2,3},{3,2},{4,5},{5,4},{6,7},{7,6},{8,9},{9,8},{10,11... | collective-permute-start | bytes 983048 | tf_op jit(solution)/shard_map/ppermute | solution.py:657
  45.2 12.2 %collective-permute-start.6 = (f16[336,128]{1,0:T(8,128)(2,1)S(1)}, f16[336,128]{1,0:T(8,128)(2,1)S(1)}, u32[]{:S(2)}, u32[]{:S(2)}) collective-permute-start(f16[336,128]{1,0:T(8,128)(2,1)S(1)} %convert_element_type.22), channel_id=1, source_target_pairs={{0,2},{2,0},{1,3},{3,1},{4,6},{6,4},{5,7},{7,5},{8,10},{10,8},{9,1... | collective-permute-start | bytes 258056 | tf_op jit(solution)/shard_map/ppermute | solution.py:663

commit v6 on v4

--- a/solution.py
+++ b/solution.py
@@ -652,13 +652,11 @@
     keep, send, window, halos = first_sum(
         wide, lat_halo, fields, edges, band, rim, pushed
     )
-    back, send = lax.optimization_barrier((back, send))
+    early = early_taps(window, halos, fields)
+    back, send, early = lax.optimization_barrier((back, send, early))
     back = back.astype(F32)
     send = near_parts(send, back, fields)
-    send, window = lax.optimization_barrier((send, window))
     more = lax.ppermute(send, "mem", [(0, 1), (1, 0), (2, 3), (3, 2)])
-    early = early_taps(window, halos, fields)
-    more, early = lax.optimization_barrier((more, early))
     mine, send = far_parts(keep, more, back, fields)
     half = lax.ppermute(send.astype(jnp.float16), "mem", [(0, 2), (2, 0), (1, 3), (3, 1)])
     mine, early = lax.optimization_barrier((mine, early))

time: 58.5 us -> 58.4 us (level)
    ppermute x1, waiting for transfers between devices: 3 us -> 2.02 us  [body(): lax.ppermute(pushed_out.astype(jnp.float16), ('lat', 'mem'), [(b, a) for...]
    ppermute x1, waiting for transfers between devices: 0.27 us -> 1.23 us  [body(): more = lax.ppermute(send, 'mem', [(0, 1), (1, 0), (2, 3), (3, 2)])]
where the time goes in v6:
time: 58.4 us; the launch traced here: 58 us
  starting transfers between devices  19.5 us (33%)
  blocking collectives  14.7 us (25%)
  Pallas kernels  11.2 us (19%)
  waiting for transfers between devices  9.24 us (16%)
  other arithmetic  1.7 us (3%)
  local copies, waits for them, and re-layouts  0.96 us (2%)
  between operations  0.8 us (1%)
    all_gather x1, blocking collectives, body(): gathered = lax.all_gather(message, 'mem', axis=0, tiled=True)  14.7 us
    pallas_call x11, Pallas kernels, call(): pl.pallas_call(kernel, out_shape=out_shape, in_specs=[pl.BlockSpec(memory...  11.2 us
    ppermute x1, starting transfers between devices, body(): lat_halo = lax.ppermute(message, ('lat', 'mem'), down + up)  5.21 us
    ppermute x1, waiting for transfers between devices, body(): lax.ppermute(send.astype(jnp.float16), 'mem', [(0, 2), (2, 0), (1, 3), (3...  4.7 us
    ppermute x1, starting transfers between devices, body(): first = lax.ppermute(first, 'lon', swaps[0])  4.27 us
    ppermute x1, starting transfers between devices, body(): more = lax.ppermute(send, 'mem', [(0, 1), (1, 0), (2, 3), (3, 2)])  3.6 us
    ppermute x1, starting transfers between devices, body(): lax.ppermute(send.astype(jnp.float16), 'mem', [(0, 2), (2, 0), (1, 3), (3...  2.49 us
    ppermute x1, waiting for transfers between devices, body(): lax.ppermute(pushed_out.astype(jnp.float16), ('lat', 'mem'), [(b, a) for...  2.02 us
  transfers between devices with their start and end apart: 6, of which 4 were waited for; matrix products, arithmetic and copies ran while one was open for 0% of the time, Pallas kernels for 18%

profile of v6, /device:TPU:201, one launch (start us, length us, event | category | flops | bytes accessed | tf_op | source)
XLA Modules:
  0.0 58.0 jit_solution(9188630595594352386)
XLA Ops:
  0.6 0.9 %pad_maximum_fusion.own_ref = bf16[352,128]{1,0:T(8,128)(2,1)S(1)} fusion(bf16[16,128]{1,0:T(8,128)(2,1)} %param.6, bf16[16,128]{1,0:T(8,128)(2,1)} %param.5, bf16[320,128]{1,0:T(8,128)(2,1)} %bitcast.5), kind=kLoop, calls=%fused_computation.2 | loop fusion | flops 270336 | bytes 180224 | tf_op jit(solution)/shard_map/concatenate | solution.py:626
  1.6 0.0 copy-start
  1.6 1.0 %copy-done = bf16[289,4,128]{2,1,0:T(4,128)(2,1)S(1)} copy-done((bf16[289,4,128]{2,1,0:T(4,128)(2,1)S(1)}, bf16[289,4,128]{2,1,0:T(4,128)(2,1)}, u32[]{:S(2)}) %copy-start) | copy-done | bytes 295960
  2.5 0.3 shard_map.59
  2.8 4.3 %collective-permute-start = (bf16[64,128]{1,0:T(8,128)(2,1)S(1)}, bf16[64,128]{1,0:T(8,128)(2,1)S(1)}, u32[]{:S(2)}, u32[]{:S(2)}) collective-permute-start(bf16[64,128]{1,0:T(8,128)(2,1)S(1)} %get-tuple-element.31), channel_id=1, source_target_pairs={{32,64},{64,32},{96,128},{128,96},{160,192},{192,160},{224,256},{2... | collective-permute-start | bytes 49160 | tf_op jit(solution)/shard_map/ppermute | solution.py:632
  7.1 2.0 %collective-permute-start.1 = (bf16[64,128]{1,0:T(8,128)(2,1)S(1)}, bf16[64,128]{1,0:T(8,128)(2,1)S(1)}, u32[]{:S(2)}, u32[]{:S(2)}) collective-permute-start(bf16[64,128]{1,0:T(8,128)(2,1)S(1)} %get-tuple-element.32), channel_id=1, source_target_pairs={{0,32},{32,0},{64,96},{96,64},{128,160},{160,128},{192,224},{224,1... | collective-permute-start | bytes 49160 | tf_op jit(solution)/shard_map/ppermute | solution.py:633
  9.1 1.2 %shard_map.60 = (bf16[2560,512]{1,0:T(8,128)(2,1)S(1)}, bf16[384,512]{1,0:T(8,128)(2,1)S(1)}) custom-call(f32[1184,128]{1,0:T(8,128)S(1)} %get-tuple-element.33.wide), custom_call_target="tpu_custom_call" | custom-call | bytes 1048576 | tf_op jit(solution)/shard_map/pallas_call | solution.py:47
  10.3 0.0 collective-permute-done.first_ref
  10.3 1.3 %collective-permute-done.1.second_ref = bf16[64,128]{1,0:T(8,128)(2,1)S(1)} collective-permute-done((bf16[64,128]{1,0:T(8,128)(2,1)S(1)}, bf16[64,128]{1,0:T(8,128)(2,1)S(1)}, u32[]{:S(2)}, u32[]{:S(2)}) %collective-permute-start.1) | collective-permute-done | bytes 16416 | tf_op jit(solution)/shard_map/ppermute | solution.py:633
  11.6 14.7 %all_gather.3.x_ref = bf16[1472,128]{1,0:T(8,128)(2,1)S(1)} all-gather(bf16[368,128]{1,0:T(8,128)(2,1)S(1)} %get-tuple-element.38), channel_id=1, replica_groups=mesh['lon'=16,'lat'=8,'mem'=4] {'mem'}, dimensions={0}, use_global_device_ids=true | all-gather | bytes 471040 | tf_op jit(solution)/shard_map/all_gather | solution.py:640
  26.3 0.1 shard_map.62
  26.3 5.2 %collective-permute-start.2 = (bf16[736,128]{1,0:T(8,128)(2,1)S(1)}, bf16[736,128]{1,0:T(8,128)(2,1)S(1)}, u32[]{:S(2)}, u32[]{:S(2)}) collective-permute-start(bf16[736,128]{1,0:T(8,128)(2,1)S(1)} %shard_map.62), channel_id=1, source_target_pairs={{0,4},{1,5},{4,8},{5,9},{8,12},{9,13},{12,16},{13,17},{16,20},{17,... | collective-permute-start | bytes 565256 | tf_op jit(solution)/shard_map/ppermute | solution.py:646
  31.6 0.9 %shard_map.63 = (f32[656,128]{1,0:T(8,128)S(1)}, bf16[160,640]{1,0:T(8,128)(2,1)S(1)}, bf16[2560,128]{1,0:T(8,128)(2,1)S(1)}, f32[1472,128]{1,0:T(8,128)S(1)}) custom-call(bf16[1472,128]{1,0:T(8,128)(2,1)S(1)} %all_gather.3.x_ref, f32[32,128]{1,0:T(8,128)S(1)} %get-tuple-element.39.fields, f32[128,128]{1,0:T(8,128)S(1)} %get-tuple-element.40.edges, ...), custom_call_target="tpu_custom_call" | custom-call | flops 1000000 | bytes 1048576 | tf_op jit(solution)/shard_map/pallas_call | solution.py:47
  32.5 1.9 %collective-permute-start.3 = (f16[656,128]{1,0:T(8,128)(2,1)S(1)}, f16[656,128]{1,0:T(8,128)(2,1)S(1)}, u32[]{:S(2)}, u32[]{:S(2)}) collective-permute-start(f16[656,128]{1,0:T(8,128)(2,1)S(1)} %convert_element_type.12), channel_id=1, source_target_pairs={{4,0},{5,1},{8,4},{9,5},{12,8},{13,9},{16,12},{17,13},{20,16},{21,... | collective-permute-start | bytes 503816 | tf_op jit(solution)/shard_map/ppermute | solution.py:648
  34.5 1.7 %shard_map.64.push_ref = f32[1280,128]{1,0:T(8,128)S(1)} custom-call(bf16[160,640]{1,0:T(8,128)(2,1)S(1)} %get-tuple-element.46.scaled, bf16[2560,128]{1,0:T(8,128)(2,1)S(1)} %get-tuple-element.47.corner, bf16[2560,512]{1,0:T(8,128)(2,1)S(1)} %get-tuple-element.42.band_ref), custom_call_target="tpu_custom_call" | custom-call | flops 1000000 | bytes 1048576 | tf_op jit(solution)/shard_map/pallas_call | solution.py:47
  36.2 0.0 collective-permute-done.2.lat_ref
  36.2 1.4 %shard_map.65 = (f32[640,128]{1,0:T(8,128)S(1)}, f32[640,128]{1,0:T(8,128)S(1)}, f32[20,88,128]{2,1,0:T(8,128)S(1)}, f32[3,88,128]{2,1,0:T(8,128)S(1)}) custom-call(f32[1472,128]{1,0:T(8,128)S(1)} %get-tuple-element.43.wide, bf16[736,128]{1,0:T(8,128)(2,1)S(1)} %collective-permute-done.2.lat_ref, f32[32,128]{1,0:T(8,128)S(1)} %get-tuple-element.39.fields, ...), custom_call_target="tpu_custom_call" | custom-call | flops 1000000 | bytes 1048576 | tf_op jit(solution)/shard_map/pallas_call | solution.py:47
  37.7 1.0 %shard_map.66.early = f32[168,128]{1,0:T(8,128)S(1)} custom-call(f32[20,88,128]{2,1,0:T(8,128)S(1)} %get-tuple-element.48.window, f32[3,88,128]{2,1,0:T(8,128)S(1)} %get-tuple-element.49.halos, f32[32,128]{1,0:T(8,128)S(1)} %get-tuple-element.39.fields), custom_call_target="tpu_custom_call" | custom-call | flops 20000000000 | bytes 1048576 | tf_op jit(solution)/shard_map/pallas_call | solution.py:47
  38.6 2.0 %collective-permute-done.3 = f16[656,128]{1,0:T(8,128)(2,1)S(1)} collective-permute-done((f16[656,128]{1,0:T(8,128)(2,1)S(1)}, f16[656,128]{1,0:T(8,128)(2,1)S(1)}, u32[]{:S(2)}, u32[]{:S(2)}) %collective-permute-start.3) | collective-permute-done | bytes 167968 | tf_op jit(solution)/shard_map/ppermute | solution.py:648
  40.7 3.6 %collective-permute-start.4 = (f32[640,128]{1,0:T(8,128)S(1)}, f32[640,128]{1,0:T(8,128)S(1)}, u32[]{:S(2)}, u32[]{:S(2)}) collective-permute-start(f32[640,128]{1,0:T(8,128)S(1)} %shard_map.67), channel_id=1, source_target_pairs={{0,1},{1,0},{2,3},{3,2},{4,5},{5,4},{6,7},{7,6},{8,9},{9,8},{10,11... | collective-permute-start | bytes 983048 | tf_op jit(solution)/shard_map/ppermute | solution.py:659
  44.3 1.2 %collective-permute-done.4.more_ref = f32[640,128]{1,0:T(8,128)S(1)} collective-permute-done((f32[640,128]{1,0:T(8,128)S(1)}, f32[640,128]{1,0:T(8,128)S(1)}, u32[]{:S(2)}, u32[]{:S(2)}) %collective-permute-start.4) | collective-permute-done | bytes 327712 | tf_op jit(solution)/shard_map/ppermute | solution.py:659
  45.6 0.3 shard_map.68
  45.8 2.5 %collective-permute-start.5 = (f16[336,128]{1,0:T(8,128)(2,1)S(1)}, f16[336,128]{1,0:T(8,128)(2,1)S(1)}, u32[]{:S(2)}, u32[]{:S(2)}) collective-permute-start(f16[336,128]{1,0:T(8,128)(2,1)S(1)} %convert_element_type.14), channel_id=1, source_target_pairs={{0,2},{2,0},{1,3},{3,1},{4,6},{6,4},{5,7},{7,5},{8,10},{10,8},{9,1... | collective-permute-start | bytes 258056 | tf_op jit(solution)/shard_map/ppermute | solution.py:661
  48.3 4.2 %shard_map.69 = f32[289,4,128]{2,1,0:T(4,128)} custom-call(f32[20,88,128]{2,1,0:T(8,128)S(1)} %get-tuple-element.48.window, f32[3,88,128]{2,1,0:T(8,128)S(1)} %get-tuple-element.49.halos, f32[32,128]{1,0:T(8,128)S(1)} %get-tuple-element.39.fields, f32[168,128]{1,0:T(8,128)S(1)} %shard_map.66.early), custom_call_target="tpu_custom_call" | custom-call | flops 1000000 | bytes 1048576 | tf_op jit(solution)/shard_map/pallas_call | solution.py:47
  52.6 4.7 %collective-permute-done.5 = f16[336,128]{1,0:T(8,128)(2,1)S(1)} collective-permute-done((f16[336,128]{1,0:T(8,128)(2,1)S(1)}, f16[336,128]{1,0:T(8,128)(2,1)S(1)}, u32[]{:S(2)}, u32[]{:S(2)}) %collective-permute-start.5) | collective-permute-done | bytes 86048 | tf_op jit(solution)/shard_map/ppermute | solution.py:661
  57.3 0.7 %fusion = f32[320,128]{1,0:T(8,128)} fusion(f32[320,128]{1,0:T(8,128)S(1)} %get-tuple-element.58, f32[336,128]{1,0:T(8,128)S(1)} %convert_element_type.15, f32[128]{0:T(128)S(1)} %fusion.2), kind=kLoop, calls=%fused_computation.1 | loop fusion | flops 81920 | bytes 492032 | tf_op jit(solution)/shard_map/add | solution.py:665
  (7 shorter events, 0.2 us)
Async XLA Ops:
  1.6 1.0 %copy-start = (bf16[289,4,128]{2,1,0:T(4,128)(2,1)S(1)}, bf16[289,4,128]{2,1,0:T(4,128)(2,1)}, u32[]{:S(2)}) copy-start(bf16[289,4,128]{2,1,0:T(4,128)(2,1)} %taper_ref.1) | copy-start | bytes 887812
  2.8 7.5 %collective-permute-start = (bf16[64,128]{1,0:T(8,128)(2,1)S(1)}, bf16[64,128]{1,0:T(8,128)(2,1)S(1)}, u32[]{:S(2)}, u32[]{:S(2)}) collective-permute-start(bf16[64,128]{1,0:T(8,128)(2,1)S(1)} %get-tuple-element.31), channel_id=1, source_target_pairs={{32,64},{64,32},{96,128},{128,96},{160,192},{192,160},{224,256},{2... | collective-permute-start | bytes 49160 | tf_op jit(solution)/shard_map/ppermute | solution.py:632
  7.1 4.5 %collective-permute-start.1 = (bf16[64,128]{1,0:T(8,128)(2,1)S(1)}, bf16[64,128]{1,0:T(8,128)(2,1)S(1)}, u32[]{:S(2)}, u32[]{:S(2)}) collective-permute-start(bf16[64,128]{1,0:T(8,128)(2,1)S(1)} %get-tuple-element.32), channel_id=1, source_target_pairs={{0,32},{32,0},{64,96},{96,64},{128,160},{160,128},{192,224},{224,1... | collective-permute-start | bytes 49160 | tf_op jit(solution)/shard_map/ppermute | solution.py:633
  26.3 9.8 %collective-permute-start.2 = (bf16[736,128]{1,0:T(8,128)(2,1)S(1)}, bf16[736,128]{1,0:T(8,128)(2,1)S(1)}, u32[]{:S(2)}, u32[]{:S(2)}) collective-permute-start(bf16[736,128]{1,0:T(8,128)(2,1)S(1)} %shard_map.62), channel_id=1, source_target_pairs={{0,4},{1,5},{4,8},{5,9},{8,12},{9,13},{12,16},{13,17},{16,20},{17,... | collective-permute-start | bytes 565256 | tf_op jit(solution)/shard_map/ppermute | solution.py:646
  32.5 8.1 %collective-permute-start.3 = (f16[656,128]{1,0:T(8,128)(2,1)S(1)}, f16[656,128]{1,0:T(8,128)(2,1)S(1)}, u32[]{:S(2)}, u32[]{:S(2)}) collective-permute-start(f16[656,128]{1,0:T(8,128)(2,1)S(1)} %convert_element_type.12), channel_id=1, source_target_pairs={{4,0},{5,1},{8,4},{9,5},{12,8},{13,9},{16,12},{17,13},{20,16},{21,... | collective-permute-start | bytes 503816 | tf_op jit(solution)/shard_map/ppermute | solution.py:648
  40.7 4.8 %collective-permute-start.4 = (f32[640,128]{1,0:T(8,128)S(1)}, f32[640,128]{1,0:T(8,128)S(1)}, u32[]{:S(2)}, u32[]{:S(2)}) collective-permute-start(f32[640,128]{1,0:T(8,128)S(1)} %shard_map.67), channel_id=1, source_target_pairs={{0,1},{1,0},{2,3},{3,2},{4,5},{5,4},{6,7},{7,6},{8,9},{9,8},{10,11... | collective-permute-start | bytes 983048 | tf_op jit(solution)/shard_map/ppermute | solution.py:659
  45.8 11.4 %collective-permute-start.5 = (f16[336,128]{1,0:T(8,128)(2,1)S(1)}, f16[336,128]{1,0:T(8,128)(2,1)S(1)}, u32[]{:S(2)}, u32[]{:S(2)}) collective-permute-start(f16[336,128]{1,0:T(8,128)(2,1)S(1)} %convert_element_type.14), channel_id=1, source_target_pairs={{0,2},{2,0},{1,3},{3,1},{4,6},{6,4},{5,7},{7,5},{8,10},{10,8},{9,1... | collective-permute-start | bytes 258056 | tf_op jit(solution)/shard_map/ppermute | solution.py:661

commit v7 on v6

--- a/solution.py
+++ b/solution.py
@@ -583,7 +583,7 @@
             flat[pl.ds(a * SPAN * ROWS + i, SPAN, stride=ROWS), :] = taps[0:SPAN]
 
 
-EARLY = 2
+EARLY = 4
 
 
 def early_kernel(window, halos, fields, flat, *scratch):

time: 58.4 us -> 58.6 us (level)
  no operation moved by 1% of the time
where the time goes in v7:
time: 58.6 us; the launch traced here: 58.3 us
  starting transfers between devices  19.8 us (34%)
  blocking collectives  14.7 us (25%)
  Pallas kernels  11.1 us (19%)
  waiting for transfers between devices  9.24 us (16%)
  other arithmetic  1.7 us (3%)
  local copies, waits for them, and re-layouts  0.96 us (2%)
  between operations  0.79 us (1%)
    all_gather x1, blocking collectives, body(): gathered = lax.all_gather(message, 'mem', axis=0, tiled=True)  14.7 us
    pallas_call x11, Pallas kernels, call(): pl.pallas_call(kernel, out_shape=out_shape, in_specs=[pl.BlockSpec(memory...  11.1 us
    ppermute x1, starting transfers between devices, body(): lat_halo = lax.ppermute(message, ('lat', 'mem'), down + up)  5.21 us
    ppermute x1, waiting for transfers between devices, body(): lax.ppermute(send.astype(jnp.float16), 'mem', [(0, 2), (2, 0), (1, 3), (3...  5.03 us
    ppermute x1, starting transfers between devices, body(): first = lax.ppermute(first, 'lon', swaps[0])  4.27 us
    ppermute x1, starting transfers between devices, body(): more = lax.ppermute(send, 'mem', [(0, 1), (1, 0), (2, 3), (3, 2)])  3.6 us
    ppermute x1, starting transfers between devices, body(): lax.ppermute(send.astype(jnp.float16), 'mem', [(0, 2), (2, 0), (1, 3), (3...  2.82 us
    ppermute x1, starting transfers between devices, body(): second = lax.ppermute(second, 'lon', swaps[1])  1.97 us
  transfers between devices with their start and end apart: 6, of which 4 were waited for; matrix products, arithmetic and copies ran while one was open for 0% of the time, Pallas kernels for 18%

profile of v7, /device:TPU:201, one launch (start us, length us, event | category | flops | bytes accessed | tf_op | source)
XLA Modules:
  0.0 58.3 jit_solution(6105494645933286042)
XLA Ops:
  0.6 0.9 %pad_maximum_fusion.own_ref = bf16[352,128]{1,0:T(8,128)(2,1)S(1)} fusion(bf16[16,128]{1,0:T(8,128)(2,1)} %param.6, bf16[16,128]{1,0:T(8,128)(2,1)} %param.5, bf16[320,128]{1,0:T(8,128)(2,1)} %bitcast.5), kind=kLoop, calls=%fused_computation.2 | loop fusion | flops 270336 | bytes 180224 | tf_op jit(solution)/shard_map/concatenate | solution.py:626
  1.6 0.0 copy-start
  1.6 1.0 %copy-done = bf16[289,4,128]{2,1,0:T(4,128)(2,1)S(1)} copy-done((bf16[289,4,128]{2,1,0:T(4,128)(2,1)S(1)}, bf16[289,4,128]{2,1,0:T(4,128)(2,1)}, u32[]{:S(2)}) %copy-start) | copy-done | bytes 295960
  2.5 0.3 shard_map.59
  2.8 4.3 %collective-permute-start = (bf16[64,128]{1,0:T(8,128)(2,1)S(1)}, bf16[64,128]{1,0:T(8,128)(2,1)S(1)}, u32[]{:S(2)}, u32[]{:S(2)}) collective-permute-start(bf16[64,128]{1,0:T(8,128)(2,1)S(1)} %get-tuple-element.31), channel_id=1, source_target_pairs={{32,64},{64,32},{96,128},{128,96},{160,192},{192,160},{224,256},{2... | collective-permute-start | bytes 49160 | tf_op jit(solution)/shard_map/ppermute | solution.py:632
  7.1 2.0 %collective-permute-start.1 = (bf16[64,128]{1,0:T(8,128)(2,1)S(1)}, bf16[64,128]{1,0:T(8,128)(2,1)S(1)}, u32[]{:S(2)}, u32[]{:S(2)}) collective-permute-start(bf16[64,128]{1,0:T(8,128)(2,1)S(1)} %get-tuple-element.32), channel_id=1, source_target_pairs={{0,32},{32,0},{64,96},{96,64},{128,160},{160,128},{192,224},{224,1... | collective-permute-start | bytes 49160 | tf_op jit(solution)/shard_map/ppermute | solution.py:633
  9.1 1.2 %shard_map.60 = (bf16[2560,512]{1,0:T(8,128)(2,1)S(1)}, bf16[384,512]{1,0:T(8,128)(2,1)S(1)}) custom-call(f32[1184,128]{1,0:T(8,128)S(1)} %get-tuple-element.33.wide), custom_call_target="tpu_custom_call" | custom-call | bytes 1048576 | tf_op jit(solution)/shard_map/pallas_call | solution.py:47
  10.3 0.0 collective-permute-done.first_ref
  10.3 1.3 %collective-permute-done.1.second_ref = bf16[64,128]{1,0:T(8,128)(2,1)S(1)} collective-permute-done((bf16[64,128]{1,0:T(8,128)(2,1)S(1)}, bf16[64,128]{1,0:T(8,128)(2,1)S(1)}, u32[]{:S(2)}, u32[]{:S(2)}) %collective-permute-start.1) | collective-permute-done | bytes 16416 | tf_op jit(solution)/shard_map/ppermute | solution.py:633
  11.6 14.7 %all_gather.3.x_ref = bf16[1472,128]{1,0:T(8,128)(2,1)S(1)} all-gather(bf16[368,128]{1,0:T(8,128)(2,1)S(1)} %get-tuple-element.38), channel_id=1, replica_groups=mesh['lon'=16,'lat'=8,'mem'=4] {'mem'}, dimensions={0}, use_global_device_ids=true | all-gather | bytes 471040 | tf_op jit(solution)/shard_map/all_gather | solution.py:640
  26.3 0.1 shard_map.62
  26.3 5.2 %collective-permute-start.2 = (bf16[736,128]{1,0:T(8,128)(2,1)S(1)}, bf16[736,128]{1,0:T(8,128)(2,1)S(1)}, u32[]{:S(2)}, u32[]{:S(2)}) collective-permute-start(bf16[736,128]{1,0:T(8,128)(2,1)S(1)} %shard_map.62), channel_id=1, source_target_pairs={{0,4},{1,5},{4,8},{5,9},{8,12},{9,13},{12,16},{13,17},{16,20},{17,... | collective-permute-start | bytes 565256 | tf_op jit(solution)/shard_map/ppermute | solution.py:646
  31.6 0.9 %shard_map.63 = (f32[656,128]{1,0:T(8,128)S(1)}, bf16[160,640]{1,0:T(8,128)(2,1)S(1)}, bf16[2560,128]{1,0:T(8,128)(2,1)S(1)}, f32[1472,128]{1,0:T(8,128)S(1)}) custom-call(bf16[1472,128]{1,0:T(8,128)(2,1)S(1)} %all_gather.3.x_ref, f32[32,128]{1,0:T(8,128)S(1)} %get-tuple-element.39.fields, f32[128,128]{1,0:T(8,128)S(1)} %get-tuple-element.40.edges, ...), custom_call_target="tpu_custom_call" | custom-call | flops 1000000 | bytes 1048576 | tf_op jit(solution)/shard_map/pallas_call | solution.py:47
  32.5 1.9 %collective-permute-start.3 = (f16[656,128]{1,0:T(8,128)(2,1)S(1)}, f16[656,128]{1,0:T(8,128)(2,1)S(1)}, u32[]{:S(2)}, u32[]{:S(2)}) collective-permute-start(f16[656,128]{1,0:T(8,128)(2,1)S(1)} %convert_element_type.12), channel_id=1, source_target_pairs={{4,0},{5,1},{8,4},{9,5},{12,8},{13,9},{16,12},{17,13},{20,16},{21,... | collective-permute-start | bytes 503816 | tf_op jit(solution)/shard_map/ppermute | solution.py:648
  34.5 1.7 %shard_map.64.push_ref = f32[1280,128]{1,0:T(8,128)S(1)} custom-call(bf16[160,640]{1,0:T(8,128)(2,1)S(1)} %get-tuple-element.46.scaled, bf16[2560,128]{1,0:T(8,128)(2,1)S(1)} %get-tuple-element.47.corner, bf16[2560,512]{1,0:T(8,128)(2,1)S(1)} %get-tuple-element.42.band_ref), custom_call_target="tpu_custom_call" | custom-call | flops 1000000 | bytes 1048576 | tf_op jit(solution)/shard_map/pallas_call | solution.py:47
  36.2 0.0 collective-permute-done.2.lat_ref
  36.2 1.4 %shard_map.65 = (f32[640,128]{1,0:T(8,128)S(1)}, f32[640,128]{1,0:T(8,128)S(1)}, f32[20,88,128]{2,1,0:T(8,128)S(1)}, f32[3,88,128]{2,1,0:T(8,128)S(1)}) custom-call(f32[1472,128]{1,0:T(8,128)S(1)} %get-tuple-element.43.wide, bf16[736,128]{1,0:T(8,128)(2,1)S(1)} %collective-permute-done.2.lat_ref, f32[32,128]{1,0:T(8,128)S(1)} %get-tuple-element.39.fields, ...), custom_call_target="tpu_custom_call" | custom-call | flops 1000000 | bytes 1048576 | tf_op jit(solution)/shard_map/pallas_call | solution.py:47
  37.6 1.3 %shard_map.66.early = f32[304,128]{1,0:T(8,128)S(1)} custom-call(f32[20,88,128]{2,1,0:T(8,128)S(1)} %get-tuple-element.48.window, f32[3,88,128]{2,1,0:T(8,128)S(1)} %get-tuple-element.49.halos, f32[32,128]{1,0:T(8,128)S(1)} %get-tuple-element.39.fields), custom_call_target="tpu_custom_call" | custom-call | flops 20000000000 | bytes 1048576 | tf_op jit(solution)/shard_map/pallas_call | solution.py:47
  38.9 1.7 %collective-permute-done.3 = f16[656,128]{1,0:T(8,128)(2,1)S(1)} collective-permute-done((f16[656,128]{1,0:T(8,128)(2,1)S(1)}, f16[656,128]{1,0:T(8,128)(2,1)S(1)}, u32[]{:S(2)}, u32[]{:S(2)}) %collective-permute-start.3) | collective-permute-done | bytes 167968 | tf_op jit(solution)/shard_map/ppermute | solution.py:648
  40.7 3.6 %collective-permute-start.4 = (f32[640,128]{1,0:T(8,128)S(1)}, f32[640,128]{1,0:T(8,128)S(1)}, u32[]{:S(2)}, u32[]{:S(2)}) collective-permute-start(f32[640,128]{1,0:T(8,128)S(1)} %shard_map.67), channel_id=1, source_target_pairs={{0,1},{1,0},{2,3},{3,2},{4,5},{5,4},{6,7},{7,6},{8,9},{9,8},{10,11... | collective-permute-start | bytes 983048 | tf_op jit(solution)/shard_map/ppermute | solution.py:659
  44.3 1.2 %collective-permute-done.4.more_ref = f32[640,128]{1,0:T(8,128)S(1)} collective-permute-done((f32[640,128]{1,0:T(8,128)S(1)}, f32[640,128]{1,0:T(8,128)S(1)}, u32[]{:S(2)}, u32[]{:S(2)}) %collective-permute-start.4) | collective-permute-done | bytes 327712 | tf_op jit(solution)/shard_map/ppermute | solution.py:659
  45.6 0.2 shard_map.68
  45.8 2.8 %collective-permute-start.5 = (f16[336,128]{1,0:T(8,128)(2,1)S(1)}, f16[336,128]{1,0:T(8,128)(2,1)S(1)}, u32[]{:S(2)}, u32[]{:S(2)}) collective-permute-start(f16[336,128]{1,0:T(8,128)(2,1)S(1)} %convert_element_type.14), channel_id=1, source_target_pairs={{0,2},{2,0},{1,3},{3,1},{4,6},{6,4},{5,7},{7,5},{8,10},{10,8},{9,1... | collective-permute-start | bytes 258056 | tf_op jit(solution)/shard_map/ppermute | solution.py:661
  48.7 3.9 %shard_map.69 = f32[289,4,128]{2,1,0:T(4,128)} custom-call(f32[20,88,128]{2,1,0:T(8,128)S(1)} %get-tuple-element.48.window, f32[3,88,128]{2,1,0:T(8,128)S(1)} %get-tuple-element.49.halos, f32[32,128]{1,0:T(8,128)S(1)} %get-tuple-element.39.fields, f32[304,128]{1,0:T(8,128)S(1)} %shard_map.66.early), custom_call_target="tpu_custom_call" | custom-call | flops 1000000 | bytes 1048576 | tf_op jit(solution)/shard_map/pallas_call | solution.py:47
  52.5 5.0 %collective-permute-done.5 = f16[336,128]{1,0:T(8,128)(2,1)S(1)} collective-permute-done((f16[336,128]{1,0:T(8,128)(2,1)S(1)}, f16[336,128]{1,0:T(8,128)(2,1)S(1)}, u32[]{:S(2)}, u32[]{:S(2)}) %collective-permute-start.5) | collective-permute-done | bytes 86048 | tf_op jit(solution)/shard_map/ppermute | solution.py:661
  57.6 0.7 %fusion = f32[320,128]{1,0:T(8,128)} fusion(f32[320,128]{1,0:T(8,128)S(1)} %get-tuple-element.58, f32[336,128]{1,0:T(8,128)S(1)} %convert_element_type.15, f32[128]{0:T(128)S(1)} %fusion.2), kind=kLoop, calls=%fused_computation.1 | loop fusion | flops 81920 | bytes 492032 | tf_op jit(solution)/shard_map/add | solution.py:665
  (7 shorter events, 0.2 us)
Async XLA Ops:
  1.6 1.0 %copy-start = (bf16[289,4,128]{2,1,0:T(4,128)(2,1)S(1)}, bf16[289,4,128]{2,1,0:T(4,128)(2,1)}, u32[]{:S(2)}) copy-start(bf16[289,4,128]{2,1,0:T(4,128)(2,1)} %taper_ref.1) | copy-start | bytes 887812
  2.8 7.5 %collective-permute-start = (bf16[64,128]{1,0:T(8,128)(2,1)S(1)}, bf16[64,128]{1,0:T(8,128)(2,1)S(1)}, u32[]{:S(2)}, u32[]{:S(2)}) collective-permute-start(bf16[64,128]{1,0:T(8,128)(2,1)S(1)} %get-tuple-element.31), channel_id=1, source_target_pairs={{32,64},{64,32},{96,128},{128,96},{160,192},{192,160},{224,256},{2... | collective-permute-start | bytes 49160 | tf_op jit(solution)/shard_map/ppermute | solution.py:632
  7.1 4.5 %collective-permute-start.1 = (bf16[64,128]{1,0:T(8,128)(2,1)S(1)}, bf16[64,128]{1,0:T(8,128)(2,1)S(1)}, u32[]{:S(2)}, u32[]{:S(2)}) collective-permute-start(bf16[64,128]{1,0:T(8,128)(2,1)S(1)} %get-tuple-element.32), channel_id=1, source_target_pairs={{0,32},{32,0},{64,96},{96,64},{128,160},{160,128},{192,224},{224,1... | collective-permute-start | bytes 49160 | tf_op jit(solution)/shard_map/ppermute | solution.py:633
  26.3 9.8 %collective-permute-start.2 = (bf16[736,128]{1,0:T(8,128)(2,1)S(1)}, bf16[736,128]{1,0:T(8,128)(2,1)S(1)}, u32[]{:S(2)}, u32[]{:S(2)}) collective-permute-start(bf16[736,128]{1,0:T(8,128)(2,1)S(1)} %shard_map.62), channel_id=1, source_target_pairs={{0,4},{1,5},{4,8},{5,9},{8,12},{9,13},{12,16},{13,17},{16,20},{17,... | collective-permute-start | bytes 565256 | tf_op jit(solution)/shard_map/ppermute | solution.py:646
  32.5 8.1 %collective-permute-start.3 = (f16[656,128]{1,0:T(8,128)(2,1)S(1)}, f16[656,128]{1,0:T(8,128)(2,1)S(1)}, u32[]{:S(2)}, u32[]{:S(2)}) collective-permute-start(f16[656,128]{1,0:T(8,128)(2,1)S(1)} %convert_element_type.12), channel_id=1, source_target_pairs={{4,0},{5,1},{8,4},{9,5},{12,8},{13,9},{16,12},{17,13},{20,16},{21,... | collective-permute-start | bytes 503816 | tf_op jit(solution)/shard_map/ppermute | solution.py:648
  40.7 4.8 %collective-permute-start.4 = (f32[640,128]{1,0:T(8,128)S(1)}, f32[640,128]{1,0:T(8,128)S(1)}, u32[]{:S(2)}, u32[]{:S(2)}) collective-permute-start(f32[640,128]{1,0:T(8,128)S(1)} %shard_map.67), channel_id=1, source_target_pairs={{0,1},{1,0},{2,3},{3,2},{4,5},{5,4},{6,7},{7,6},{8,9},{9,8},{10,11... | collective-permute-start | bytes 983048 | tf_op jit(solution)/shard_map/ppermute | solution.py:659
  45.8 11.7 %collective-permute-start.5 = (f16[336,128]{1,0:T(8,128)(2,1)S(1)}, f16[336,128]{1,0:T(8,128)(2,1)S(1)}, u32[]{:S(2)}, u32[]{:S(2)}) collective-permute-start(f16[336,128]{1,0:T(8,128)(2,1)S(1)} %convert_element_type.14), channel_id=1, source_target_pairs={{0,2},{2,0},{1,3},{3,1},{4,6},{6,4},{5,7},{7,5},{8,10},{10,8},{9,1... | collective-permute-start | bytes 258056 | tf_op jit(solution)/shard_map/ppermute | solution.py:661
